TPU v7x, 256 devices: a whole 4x4x8 slice. The times are simulated.
256 devices in a mesh: imp: 32 (over z, y), camp: 8 (over x, core).
Axes of the slice: x: 4, y: 4, z: 8, core: 2. Of those that a mesh axis runs over, the one named last changes fastest.
Arguments:
- imp_emb: bfloat16 [131072, 256], P(('imp', 'camp')), may hold values from -512 to 512
- imp_cost: bfloat16 [131072], P(('imp', 'camp')), may hold values from 0.099609375 to 1
- camp_emb: bfloat16 [32768, 256], P(('camp', 'imp')), may hold values from -6 to 6
- prices: bfloat16 [32768], P(('camp', 'imp')), may hold values from -5 to 5
- spend_limits: float32 [32768], P(('camp', 'imp')), may hold values from 5 to 64
- block_lists: int32 [1024, 8, 8], P('imp', 'camp'), may hold values from 0 to 31, as said below
- block_counts: int32 [1024, 8], P('imp', 'camp'), may hold values from 1 to 8, as said below
Outputs:
- new_prices: float32 [32768], P(('camp', 'imp'))
- row_logz: float32 [131072], P('imp')
Inputs may be any that keep to these rules, and one draw needn't show every extreme that they name: `block_lists`: entries of a list of one tile and owner are distinct block numbers of that owner; slots past the count hold block numbers too, which are ignored. `block_counts`: tile 0 uses all 8 slots of every owner.
All inputs are finite; a program needn't handle non-finite values.
Results may differ from a plain program's by a relative error of at most 0.0003.
Values may be sent and summed in bfloat16 or wider, within the bound.
No kernel may reach another device: no remote copies, remote signals or barrier semaphores. Data moves between devices by JAX's collectives and lax.ppermute only.
A program may use at most 64 MiB of HBM per device.

v0:
```python
import jax
import jax.numpy as jnp
from jax import lax
from jax.sharding import PartitionSpec as P

D = 256
BLOCK = 128
SLOTS = 8
GROUP = 4


def local(imp_emb, imp_cost, camp_emb, prices, spend_limits, block_lists, block_counts):
    scale = 3.0 / jnp.sqrt(jnp.float32(D))
    emb_rows, cost_rows = (
        lax.all_gather(imp_emb, "camp", axis=0, tiled=True),
        lax.all_gather(imp_cost, "camp", axis=0, tiled=True),
    )
    camp_all, price_all = (
        lax.all_gather(camp_emb, "imp", axis=0, tiled=True),
        lax.all_gather(prices, "imp", axis=0, tiled=True),
    )
    own_count = camp_all.shape[0] // BLOCK
    camp_table = camp_all.reshape(own_count, BLOCK, D)
    price_table = price_all.astype(jnp.float32).reshape(own_count, BLOCK)
    lists = block_lists[:, 0, :]
    counts = block_counts[:, 0]
    tiles = lists.shape[0]
    turns = tiles // GROUP
    emb_groups = emb_rows.reshape(turns, GROUP, BLOCK, D)
    cost_groups = cost_rows.astype(jnp.float32).reshape(turns, GROUP, BLOCK)
    list_groups = lists.reshape(turns, GROUP, SLOTS)
    count_groups = counts.reshape(turns, GROUP)

    def scores_of(emb, ids, cnt):
        chosen = camp_table[ids]
        chosen_price = price_table[ids]
        raw = jnp.einsum("gbd,gscd->gbsc", emb, chosen, preferred_element_type=jnp.float32)
        logits = raw * scale - chosen_price[:, None, :, :]
        live = (jnp.arange(SLOTS, dtype=jnp.int32)[None, :] < cnt[:, None])[:, None, :, None]
        return (logits, live)

    def local_max(items):
        emb, ids, cnt = items
        logits, live = scores_of(emb, ids, cnt)
        return jnp.max(jnp.where(live, logits, -jnp.inf), axis=(2, 3))

    def local_total(items):
        emb, ids, cnt, top = items
        logits, live = scores_of(emb, ids, cnt)
        expo = jnp.exp(jnp.where(live, logits - top[:, :, None, None], -jnp.inf))
        return jnp.sum(expo, axis=(2, 3))

    tops_here = lax.map(local_max, (emb_groups, list_groups, count_groups))
    top = lax.pmax(tops_here, "camp")
    totals_here = lax.map(local_total, (emb_groups, list_groups, count_groups, top))
    total = lax.psum(totals_here, "camp")
    row_logz = (top + jnp.log(total)).reshape(tiles * BLOCK)
    block_index = jnp.arange(own_count, dtype=jnp.int32)

    def accumulate(spend, items):
        emb, ids, cnt, cost, top_now, total_now = items
        logits, live = scores_of(emb, ids, cnt)
        expo = jnp.exp(jnp.where(live, logits - top_now[:, :, None, None], -jnp.inf))
        weight = expo / total_now[:, :, None, None]
        contrib = jnp.sum(weight * cost[:, :, None, None], axis=1)
        slot_live = jnp.arange(SLOTS, dtype=jnp.int32)[None, :] < cnt[:, None]
        onehot = ((ids[:, :, None] == block_index[None, None, :]) & slot_live[:, :, None]).astype(
            jnp.float32
        )
        added = jnp.einsum("gso,gsc->oc", onehot, contrib, precision=lax.Precision.HIGHEST)
        return (spend + added, None)

    spend_zero = jnp.zeros((own_count, BLOCK), jnp.float32)
    spend, unused = lax.scan(
        accumulate, spend_zero, (emb_groups, list_groups, count_groups, cost_groups, top, total)
    )
    spend = spend.reshape(own_count * BLOCK)
    width = prices.shape[0]
    whole = lax.psum(spend, "imp")
    mine = lax.dynamic_slice_in_dim(whole, lax.axis_index("imp") * width, width)
    new_prices = prices.astype(jnp.float32) + 2.0 * (mine - spend_limits) / (mine + spend_limits)
    return (new_prices, row_logz)


def solution(mesh):
    return jax.shard_map(
        local,
        mesh=mesh,
        in_specs=(
            P(("imp", "camp"), None),
            P(("imp", "camp")),
            P(("camp", "imp"), None),
            P(("camp", "imp")),
            P(("camp", "imp")),
            P("imp", "camp", None),
            P("imp", "camp"),
        ),
        out_specs=(P(("camp", "imp")), P("imp")),
        check_vma=False,
    )
```

profile of v0, /device:TPU:8, one launch (start us, length us, event | category | flops | bytes accessed | tf_op | source)
XLA Modules:
  0.0 434.0 jit_solution(10466042822037340445)
XLA Ops:
  8.7 41.5 %all-gather = bf16[32,1,128]{2,1,0:T(2,128)(2,1)S(1)} all-gather(bf16[1,1,128]{2,1,0:T(2,128)(2,1)} %bitcast.142), channel_id=1, replica_groups=mesh['imp'=32,'camp'=8] {'imp'}, dimensions={0}, use_global_device_ids=true | all-gather | bytes 8448 | tf_op jit(solution)/shard_map/all_gather | solution.py:20
  53.5 11.9 %all-gather.1 = bf16[8,1,512]{2,1,0:T(2,128)(2,1)S(1)} all-gather(bf16[1,1,512]{2,1,0:T(2,128)(2,1)S(1)} %reshape.289), channel_id=1, replica_groups=mesh['imp'=32,'camp'=8] {'camp'}, dimensions={0}, use_global_device_ids=true | all-gather | bytes 9216 | tf_op jit(solution)/shard_map/all_gather | solution.py:16
  65.5 54.7 %all-gather.7.cloned.1.call-done = bf16[4096,256]{1,0:T(8,128)(2,1)} async-done(((bf16[128,256]{1,0:T(8,128)(2,1)}), bf16[4096,256]{1,0:T(8,128)(2,1)}) %all-gather.7.cloned.1.call-update) | async-done | bytes 2097168 | tf_op jit(solution)/shard_map/all_gather | solution.py:19
  120.2 39.6 %while.31 = (s32[]{:T(128)}, f32[8,4,128]{2,1,0:T(4,128)S(1)}, s32[8,4]{1,0:T(8,128)S(1)}, bf16[8,4,128,256]{3,2,1,0:T(8,128)(2,1)}, s32[8,4,8]{2,1,0:T(4,128)S(...) while((s32[]{:T(128)}, f32[8,4,128]{2,1,0:T(4,128)S(1)}, s32[8,4]{1,0:T(8,128)S(1)}, ...), condition=%wide.region_2.3_spmd, body=%wide.region_0.2_spmd.sunk | while | flops 270533248 | bytes 6614609 | solution.py:53
  120.3 2.3 gather_fusion
  125.2 2.3 gather_fusion
  130.2 2.3 gather_fusion
  135.1 2.3 gather_fusion
  140.1 2.3 gather_fusion
  145.0 2.3 gather_fusion
  150.0 2.3 gather_fusion
  154.9 2.3 gather_fusion
  159.8 23.6 %pmax.7 = f32[8,4,128]{2,1,0:T(4,128)S(1)} all-reduce(f32[8,4,128]{2,1,0:T(4,128)S(1)} %get-tuple-element.138), channel_id=1, replica_groups=mesh['imp'=32,'camp'=8] {'camp'}, use_global_device_ids=true, to_apply=%region_3.4 | all-reduce | flops 4096 | bytes 32768 | tf_op jit(solution)/shard_map/pmax | solution.py:54
  183.3 40.0 %while.32 = (s32[]{:T(128)}, f32[8,4,128]{2,1,0:T(4,128)S(1)}, s32[8,4]{1,0:T(8,128)S(1)}, bf16[8,4,128,256]{3,2,1,0:T(8,128)(2,1)}, s32[8,4,8]{2,1,0:T(4,128)S(...) while((s32[]{:T(128)}, f32[8,4,128]{2,1,0:T(4,128)S(1)}, ...), condition=%wide.region_6.7_spmd, body=%wide.region_4.6_spmd.sunk | while | flops 271057536 | bytes 6620765 | solution.py:55
  183.4 2.3 gather_fusion.2
  188.4 2.3 gather_fusion.2
  191.4 1.9 exponential_reduce_fusion.2
  193.4 2.3 gather_fusion.2
  196.4 1.9 exponential_reduce_fusion.2
  198.4 2.3 gather_fusion.2
  201.4 1.9 exponential_reduce_fusion.2
  203.5 2.3 gather_fusion.2
  206.4 1.9 exponential_reduce_fusion.2
  208.5 2.3 gather_fusion.2
  211.4 1.9 exponential_reduce_fusion.2
  213.5 2.3 gather_fusion.2
  216.4 1.9 exponential_reduce_fusion.2
  218.5 2.3 gather_fusion.2
  221.4 1.9 exponential_reduce_fusion.2
  223.3 23.6 %psum.14 = f32[8,4,128]{2,1,0:T(4,128)S(1)} all-reduce(f32[8,4,128]{2,1,0:T(4,128)S(1)} %get-tuple-element.139), channel_id=1, replica_groups=mesh['imp'=32,'camp'=8] {'camp'}, use_global_device_ids=true, to_apply=%region_7.8 | all-reduce | flops 4096 | bytes 32768 | tf_op jit(solution)/shard_map/psum | solution.py:56
  246.9 42.9 %while.33 = (s32[]{:T(128)}, f32[32,128]{1,0:T(8,128)S(1)}, s32[8,4,8]{2,1,0:T(4,128)S(1)}, s32[8,4]{1,0:T(8,128)S(1)}, bf16[8,4,128,256]{3,2,1,0:T(8,128)(2,1)}...) while((s32[]{:T(128)}, f32[32,128]{1,0:T(8,128)S(1)}, ...), condition=%wide.region_10.11_spmd.clone, body=%wide.region_8.10_spmd.clone.sunk | while | flops 273685632 | bytes 6692899 | solution.py:74
  247.0 2.3 gather_fusion.4
  250.0 2.0 multiply_reduce_fusion.2
  252.4 2.3 gather_fusion.4
  255.3 2.0 multiply_reduce_fusion.2
  257.7 2.3 gather_fusion.4
  260.7 2.0 multiply_reduce_fusion.2
  263.1 2.3 gather_fusion.4
  266.1 2.0 multiply_reduce_fusion.2
  268.5 2.3 gather_fusion.4
  271.4 2.0 multiply_reduce_fusion.2
  273.8 2.3 gather_fusion.4
  276.8 2.0 multiply_reduce_fusion.2
  279.2 2.3 gather_fusion.4
  282.1 2.0 multiply_reduce_fusion.2
  284.5 2.3 gather_fusion.4
  287.5 2.0 multiply_reduce_fusion.2
  289.8 136.1 %psum.15 = f32[4096]{0:T(1024)S(1)} all-reduce(f32[4096]{0:T(1024)S(1)} %bitcast.141), channel_id=1, replica_groups=mesh['imp'=32,'camp'=8] {'imp'}, use_global_device_ids=true, to_apply=%region_11.12 | all-reduce | flops 4096 | bytes 32768 | tf_op jit(solution)/shard_map/psum | solution.py:79
  (230 shorter events, 43.7 us)
Async XLA Ops:
  7.2 58.3 %all-gather.5.cloned.1.call-start = ((), (), s32[]{:S(2)}) async-start(), calls=%async_computation | async-start | bytes 2359296 | tf_op jit(solution)/shard_map/all_gather | solution.py:15
  7.9 112.3 %all-gather.7.cloned.1.call-start = ((), (), s32[]{:S(2)}) async-start(), calls=%async_computation.1 | async-start | bytes 2162688 | tf_op jit(solution)/shard_map/all_gather | solution.py:19
  246.9 179.6 %copy-start = (bf16[128]{0:T(256)(128)(2,1)S(1)}, bf16[128]{0:T(256)(128)(2,1)}, u32[]{:S(2)}) copy-start(bf16[128]{0:T(256)(128)(2,1)} %param.16) | copy-start | bytes 772
  246.9 179.6 %copy-start.1 = (f32[128]{0:T(128)S(1)}, f32[128]{0:T(128)}, u32[]{:S(2)}) copy-start(f32[128]{0:T(128)} %param.17) | copy-start | bytes 1540
Sparse Core Ops, SparseCore 0:
  9.9 30.5 all-gather.4
  43.0 77.0 all-gather.6
where the time goes:
time: 439 us; the launch traced here: 434 us
  blocking collectives  237 us (54%)
  local copies, waits for them, and re-layouts  73 us (17%)
  waiting for transfers between devices  56.1 us (13%)
  matrix products  48 us (11%)
  between operations  14.1 us (3%)
  other arithmetic  4.68 us (1%)
    psum x1, blocking collectives, local(): whole = lax.psum(spend, 'imp')  136 us
    all_gather x1, waiting for transfers between devices, local(): lax.all_gather(camp_emb, 'imp', axis=0, tiled=True)  54.7 us
    gather x24, local copies, waits for them, and re-layouts, scores_of(): chosen = camp_table[ids]  54.5 us
    dot_general x24, matrix products, scores_of(): jnp.einsum('gbd,gscd->gbsc', emb, chosen, preferred_element_type=jnp.floa...  45.8 us
    all_gather x1, blocking collectives, local(): lax.all_gather(prices, 'imp', axis=0, tiled=True)  41.5 us
    pmax x1, blocking collectives, local(): top = lax.pmax(tops_here, 'camp')  23.6 us
    psum x1, blocking collectives, local(): total = lax.psum(totals_here, 'camp')  23.6 us
    gather x24, local copies, waits for them, and re-layouts, scores_of(): chosen_price = price_table[ids]  13.8 us
  transfers between devices with their start and end apart: 2, of which 1 were waited for; matrix products, arithmetic and copies ran while one was open for 1% of the time, Pallas kernels for 0%

commit v1 on v0

v1 whole, which is shorter than its diff:
```python
import functools
import math

import jax
import jax.numpy as jnp
from jax import lax
from jax.experimental import pallas as pl
from jax.experimental.pallas import tpu as pltpu
from jax.sharding import PartitionSpec as P

D = 256
BLOCK = 128
SLOTS = 8
NZ, NY, NX, NC = 8, 4, 4, 2
OWN = NZ * NY
TILES = 32
DEAD = OWN
PAD = 16
CBLK = BLOCK + PAD
LOG2E = math.log2(math.e)
LN2 = math.log(2.0)
SCALE2 = 3.0 / math.sqrt(D) * LOG2E
VMEM_LIMIT = 56 * 1024 * 1024


def shift_z(v, k):
    perm = [(z * NY + y, (z + k) % NZ * NY + y) for z in range(NZ) for y in range(NY)]
    return lax.ppermute(v, "imp", perm)


def shift_y(v, k):
    perm = [(z * NY + y, z * NY + (y + k) % NY) for z in range(NZ) for y in range(NY)]
    return lax.ppermute(v, "imp", perm)


def shift_x(v, k):
    perm = [(x * NC + c, (x + k) % NX * NC + c) for x in range(NX) for c in range(NC)]
    return lax.ppermute(v, "camp", perm)


def other_core(v):
    perm = [(x * NC + c, x * NC + 1 - c) for x in range(NX) for c in range(NC)]
    return lax.ppermute(v, "camp", perm)


PAIR_DZ = (0, 4)
REST_DZ = (7, 3, 1, 5, 6, 2)
DY = (0, 3, 1, 2)
DX = (0, 3, 1, 2)


def scores(tab, pb, rows_t, b):
    raw = lax.dot_general(tab[b], rows_t, (((1,), (1,)), ((), ())), preferred_element_type=jnp.float32)
    return raw * SCALE2 - pb[b]


def by_count(count, body):
    for hi in (2, 4, 6, 8):
        pl.when((count > hi - 2) & (count <= hi))(functools.partial(body, hi))


def fold(v):
    return v.reshape(v.shape[0] // 8, 8, v.shape[1])


def stats_kernel(ids, counts, where, *refs):
    rows_in, pairs, rests = refs[:8], refs[8:12], refs[12:16]
    stat, rows, tab, pb, sbuf = refs[16:]
    z, y, x, core = where[0], where[1], where[2], where[3]
    eye = lax.broadcasted_iota(jnp.int32, (BLOCK, BLOCK), 0) == lax.broadcasted_iota(jnp.int32, (BLOCK, BLOCK), 1)
    ones = jnp.ones((BLOCK, BLOCK), jnp.bfloat16)
    for bufs, offsets in ((pairs, PAIR_DZ), (rests, REST_DZ)):
        for buf, dy in zip(bufs, DY):
            for i, dz in enumerate(offsets):
                b = lax.rem(z + dz, NZ) * NY + lax.rem(y + dy, NY)
                tab[b] = buf[i * CBLK : i * CBLK + BLOCK, :]
                row = buf[i * CBLK + BLOCK : (i + 1) * CBLK, :][0:1, 0:BLOCK].astype(jnp.float32)
                diag = jnp.where(eye, jnp.broadcast_to(row, (BLOCK, BLOCK)), 0.0).astype(jnp.bfloat16)
                pb[b] = jnp.dot(diag, ones, preferred_element_type=jnp.float32) * LOG2E
    tab[DEAD] = jnp.zeros((BLOCK, D), jnp.bfloat16)
    pb[DEAD] = jnp.full((BLOCK, BLOCK), jnp.inf, jnp.float32)
    for k in range(8):
        xs = lax.rem(x + DX[k % 4], NX)
        cs = core if k < 4 else 1 - core
        for j in range(4):
            rows[(xs * NC + cs) * 4 + j] = rows_in[k][j * BLOCK : (j + 1) * BLOCK, :]

    def tile(t, carry):
        def body(n):
            rows_t = rows[t]
            top = None
            for s in range(n):
                logit = scores(tab, pb, rows_t, ids[t, s])
                sbuf[s] = logit
                part = jnp.max(fold(logit), axis=0)
                top = part if top is None else jnp.maximum(top, part)
            top = jnp.max(top, axis=0, keepdims=True)
            total = jnp.zeros((8, BLOCK), jnp.float32)
            for s in range(n):
                total = total + jnp.sum(fold(jnp.exp2(sbuf[s] - top)), axis=0)
            stat[pl.ds(t, 1), :] = top
            stat[pl.ds(TILES + t, 1), :] = jnp.sum(total, axis=0, keepdims=True)

        by_count(counts[t], body)
        return carry

    lax.fori_loop(0, TILES, tile, 0)


def spend_kernel(ids, counts, s0, s1, s2, s3, cost, rows, tab, pb, spend, logz, acc, topw):
    stats = (s0, s1, s2, s3)
    top = functools.reduce(jnp.maximum, [s[0:TILES, :] for s in stats])
    total = sum(s[TILES:, :] * jnp.exp2(s[0:TILES, :] - top) for s in stats)
    logz[...] = (top + jnp.log2(total)) * LN2
    topw[0:TILES, :] = top
    topw[TILES:, :] = cost[...] / total
    for b in range(OWN):
        acc[b] = jnp.zeros((BLOCK, BLOCK), jnp.float32)

    def tile(t, carry):
        def body(n):
            rows_t = rows[t]
            top_t = topw[pl.ds(t, 1), :]
            w_t = topw[pl.ds(TILES + t, 1), :]
            out = []
            for s in range(n):
                e = jnp.exp2(scores(tab, pb, rows_t, ids[t, s]) - top_t) * w_t
                out.append(acc[ids[t, s]] + e)
            for s in range(n):
                acc[ids[t, s]] = out[s]

        by_count(counts[t], body)
        return carry

    lax.fori_loop(0, TILES, tile, 0)
    for b in range(OWN):
        spend[b : b + 1, :] = jnp.sum(acc[b].T, axis=0, keepdims=True)


VM = pl.BlockSpec(memory_space=pltpu.VMEM)
SM = pl.BlockSpec(memory_space=pltpu.SMEM)


def local(imp_emb, imp_cost, camp_emb, prices, spend_limits, block_lists, block_counts):
    imp, camp = lax.axis_index("imp"), lax.axis_index("camp")
    where = jnp.stack([imp // NY, imp % NY, camp // NC, camp % NC]).astype(jnp.int32)
    counts = block_counts[:, 0]
    ids = jnp.where(jnp.arange(SLOTS, dtype=jnp.int32)[None, :] < counts[:, None], block_lists[:, 0, :], DEAD)

    blk = jnp.concatenate([camp_emb, jnp.pad(prices.reshape(1, BLOCK), ((0, PAD - 1), (0, D - BLOCK)))], 0)
    pair = jnp.concatenate([blk, shift_z(blk, 4)], 0)
    own = jnp.concatenate([imp_emb, jnp.pad(imp_cost.reshape(2, D), ((0, PAD - 2), (0, 0)))], 0)
    rows_in = [own] + [shift_x(own, k) for k in (1, -1, 2)]
    rest = jnp.concatenate([shift_z(pair, 1), shift_z(pair, -1), shift_z(pair, 2)], 0)
    pairs = [pair] + [shift_y(pair, k) for k in (1, -1, 2)]
    rests = [rest] + [shift_y(rest, k) for k in (1, -1, 2)]
    rows_in = rows_in + [other_core(v) for v in rows_in]

    stat, rows, tab, pb = pl.pallas_call(
        stats_kernel,
        in_specs=[SM] * 3 + [VM] * 16,
        out_specs=[VM] * 4,
        out_shape=[
            jax.ShapeDtypeStruct((2 * TILES, BLOCK), jnp.float32),
            jax.ShapeDtypeStruct((TILES, BLOCK, D), jnp.bfloat16),
            jax.ShapeDtypeStruct((OWN + 1, BLOCK, D), jnp.bfloat16),
            jax.ShapeDtypeStruct((OWN + 1, BLOCK, BLOCK), jnp.float32),
        ],
        scratch_shapes=[pltpu.VMEM((SLOTS, BLOCK, BLOCK), jnp.float32)],
        compiler_params=pltpu.CompilerParams(vmem_limit_bytes=VMEM_LIMIT),
        name="stats",
    )(ids, counts, where, *rows_in, *pairs, *rests)

    xs = [(camp // NC + d) % NX for d in DX]
    order = jnp.stack([x * NC + camp % NC for x in xs] + [x * NC + 1 - camp % NC for x in xs])
    cost_in = jnp.stack([v[512:514, :].reshape(4, BLOCK) for v in rows_in]).astype(jnp.float32)
    onehot = order[None, :] == jnp.arange(8)[:, None]
    cost = jnp.sum(jnp.where(onehot[:, :, None, None], cost_in[None], 0.0), axis=1).reshape(TILES, BLOCK)

    far = other_core(stat)
    m0, m1 = stat[:TILES], far[:TILES]
    m = jnp.maximum(m0, m1)
    both = jnp.concatenate([m, stat[TILES:] * jnp.exp2(m0 - m) + far[TILES:] * jnp.exp2(m1 - m)], 0)
    all_stats = [both] + [shift_x(both, k) for k in (1, -1, 2)]

    spend, logz = pl.pallas_call(
        spend_kernel,
        in_specs=[SM] * 2 + [VM] * 8,
        out_specs=[VM] * 2,
        out_shape=[jax.ShapeDtypeStruct((TILES, BLOCK), jnp.float32)] * 2,
        scratch_shapes=[
            pltpu.VMEM((OWN + 1, BLOCK, BLOCK), jnp.float32),
            pltpu.VMEM((2 * TILES, BLOCK), jnp.float32),
        ],
        compiler_params=pltpu.CompilerParams(vmem_limit_bytes=VMEM_LIMIT),
        name="spend",
    )(ids, counts, *all_stats, cost, rows, tab, pb)

    mine = jnp.sum(lax.all_to_all(spend, "imp", 0, 0), axis=0)
    new_prices = prices.astype(jnp.float32) + 2.0 * (mine - spend_limits) / (mine + spend_limits)
    return (new_prices, logz.reshape(TILES * BLOCK))


def solution(mesh):
    return jax.shard_map(
        local,
        mesh=mesh,
        in_specs=(
            P(("imp", "camp"), None),
            P(("imp", "camp")),
            P(("camp", "imp"), None),
            P(("camp", "imp")),
            P(("camp", "imp")),
            P("imp", "camp", None),
            P("imp", "camp"),
        ),
        out_specs=(P(("camp", "imp")), P("imp")),
        check_vma=False,
    )
```

time: 439 us -> 125 us (0.28)
  blocking collectives: 237 us -> 18.2 us
  local copies, waits for them, and re-layouts: 73 us -> 10 us
  matrix products: 48 us -> 0 us
  starting transfers between devices: 0.08 us -> 31.7 us
  Pallas kernels: 0 us -> 28.8 us
  waiting for transfers between devices: 56.1 us -> 27.7 us
  between operations: 14.1 us -> 0.92 us
    psum x2 -> x0, blocking collectives: 160 us -> none  [the longest x1 136 us: local(): whole = lax.psum(spend, 'imp')]
    gather x48 -> x0, local copies, waits for them, and re-layouts: 68.3 us -> none  [the longest x24 54.5 us: scores_of(): chosen = camp_table[ids]]
    all_gather x2 -> x0, waiting for transfers between devices: 54.7 us -> none  [the longest x1 54.7 us: local(): lax.all_gather(camp_emb, 'imp', axis=0, tiled=True)]
    all_gather x2 -> x0, blocking collectives: 53.4 us -> none  [the longest x1 41.5 us: local(): lax.all_gather(prices, 'imp', axis=0, tiled=True)]
    dot_general x32 -> x0, matrix products: 48 us -> none  [the longest x24 45.8 us: scores_of(): jnp.einsum('gbd,gscd->gbsc', emb, chosen, preferred_element_type=jnp.floa...]
    ppermute x0 -> x21, starting transfers between devices: none -> 31.7 us  [the longest x4 12.1 us: shift_z(): return lax.ppermute(v, 'imp', perm)]
    pallas_call x0 -> x2, Pallas kernels: none -> 28.8 us  [the longest x1 15.7 us: local(): pl.pallas_call(stats_kernel, in_specs=[SM] * 3 + [VM] * 16, out_specs=[VM...]
    ppermute x0 -> x21, waiting for transfers between devices: none -> 27.7 us  [the longest x6 16.3 us: shift_y(): return lax.ppermute(v, 'imp', perm)]
  transfers between devices with their start and end apart: 2 -> 21, of which waited for: 1 -> 8; matrix products, arithmetic and copies ran while one was open for 1% -> 9% of each run, Pallas kernels for 0% -> 0%
where the time goes in v1:
time: 125 us; the launch traced here: 124 us
  starting transfers between devices  31.7 us (25%)
  Pallas kernels  28.8 us (23%)
  waiting for transfers between devices  27.7 us (22%)
  blocking collectives  18.2 us (15%)
  local copies, waits for them, and re-layouts  10 us (8%)
  other arithmetic  6.62 us (5%)
    all_to_all x1, blocking collectives, local(): mine = jnp.sum(lax.all_to_all(spend, 'imp', 0, 0), axis=0)  18.2 us
    ppermute x6, waiting for transfers between devices, shift_y(): return lax.ppermute(v, 'imp', perm)  16.3 us
    pallas_call x1, Pallas kernels, local(): pl.pallas_call(stats_kernel, in_specs=[SM] * 3 + [VM] * 16, out_specs=[VM...  15.7 us
    pallas_call x1, Pallas kernels, local(): pl.pallas_call(spend_kernel, in_specs=[SM] * 2 + [VM] * 8, out_specs=[VM]...  13.1 us
    ppermute x4, starting transfers between devices, shift_z(): return lax.ppermute(v, 'imp', perm)  12.1 us
    ppermute x6, starting transfers between devices, shift_x(): return lax.ppermute(v, 'camp', perm)  10.3 us
    ppermute x6, starting transfers between devices, shift_y(): return lax.ppermute(v, 'imp', perm)  8.7 us
    ppermute x4, waiting for transfers between devices, shift_z(): return lax.ppermute(v, 'imp', perm)  7.61 us
  transfers between devices with their start and end apart: 21, of which 8 were waited for; matrix products, arithmetic and copies ran while one was open for 9% of the time, Pallas kernels for 0%

profile of v1, /device:TPU:8, one launch (start us, length us, event | category | flops | bytes accessed | tf_op | source)
XLA Modules:
  0.0 124.0 jit_solution(15611041122343030424)
XLA Ops:
  0.6 0.7 pad.9
  1.3 0.8 pad_maximum_fusion.1
  2.1 7.2 %collective-permute-start.7 = (bf16[144,256]{1,0:T(8,128)(2,1)S(1)}, bf16[144,256]{1,0:T(8,128)(2,1)S(1)}, u32[]{:S(2)}, u32[]{:S(2)}) collective-permute-start(bf16[144,256]{1,0:T(8,128)(2,1)S(1)} %pad_maximum_fusion.1), channel_id=1, source_target_pairs={{0,128},{8,136},{16,144},{24,152},{32,160},{40,168},{48,176},{56,1... | collective-permute-start | bytes 221192 | tf_op jit(solution)/shard_map/ppermute | solution.py:28
  9.3 0.7 reshape.102
  10.0 2.1 %collective-permute-done.7 = bf16[144,256]{1,0:T(8,128)(2,1)S(1)} collective-permute-done((bf16[144,256]{1,0:T(8,128)(2,1)S(1)}, bf16[144,256]{1,0:T(8,128)(2,1)S(1)}, u32[]{:S(2)}, u32[]{:S(2)}) %collective-permute-start.7) | collective-permute-done | bytes 73760 | tf_op jit(solution)/shard_map/ppermute | solution.py:28
  12.1 0.8 pad_maximum_fusion.refs_8_
  12.9 1.7 %collective-permute-start.8 = (bf16[288,256]{1,0:T(8,128)(2,1)S(1)}, bf16[288,256]{1,0:T(8,128)(2,1)S(1)}, u32[]{:S(2)}, u32[]{:S(2)}) collective-permute-start(bf16[288,256]{1,0:T(8,128)(2,1)S(1)} %pad_maximum_fusion.refs_8_), channel_id=1, source_target_pairs={{0,8},{8,16},{16,24},{24,0},{32,40},{40,48},{48,56},{56,32},{64,72... | collective-permute-start | bytes 442376 | tf_op jit(solution)/shard_map/ppermute | solution.py:33
  14.6 1.0 fusion.1.refs_0_
  15.6 1.6 %collective-permute-start = (bf16[528,256]{1,0:T(8,128)(2,1)S(1)}, bf16[528,256]{1,0:T(8,128)(2,1)S(1)}, u32[]{:S(2)}, u32[]{:S(2)}) collective-permute-start(bf16[528,256]{1,0:T(8,128)(2,1)S(1)} %fusion.1.refs_0_), channel_id=1, source_target_pairs={{0,2},{1,3},{2,4},{3,5},{4,6},{5,7},{6,0},{7,1},{8,10},{9,11},{10,... | collective-permute-start | bytes 811016 | tf_op jit(solution)/shard_map/ppermute | solution.py:38
  17.1 0.4 collective-permute-start.9
  17.6 1.7 %collective-permute-start.11 = (bf16[288,256]{1,0:T(8,128)(2,1)S(1)}, bf16[288,256]{1,0:T(8,128)(2,1)S(1)}, u32[]{:S(2)}, u32[]{:S(2)}) collective-permute-start(bf16[288,256]{1,0:T(8,128)(2,1)S(1)} %pad_maximum_fusion.refs_8_), channel_id=1, source_target_pairs={{0,32},{8,40},{16,48},{24,56},{32,64},{40,72},{48,80},{56,88},{64,... | collective-permute-start | bytes 442376 | tf_op jit(solution)/shard_map/ppermute | solution.py:28
  19.3 2.7 %collective-permute-start.12 = (bf16[288,256]{1,0:T(8,128)(2,1)S(1)}, bf16[288,256]{1,0:T(8,128)(2,1)S(1)}, u32[]{:S(2)}, u32[]{:S(2)}) collective-permute-start(bf16[288,256]{1,0:T(8,128)(2,1)S(1)} %pad_maximum_fusion.refs_8_), channel_id=1, source_target_pairs={{0,224},{8,232},{16,240},{24,248},{32,0},{40,8},{48,16},{56,24},{6... | collective-permute-start | bytes 442376 | tf_op jit(solution)/shard_map/ppermute | solution.py:28
  22.0 0.6 collective-permute-start.13
  22.6 1.7 %collective-permute-start.1 = (bf16[528,256]{1,0:T(8,128)(2,1)S(1)}, bf16[528,256]{1,0:T(8,128)(2,1)S(1)}, u32[]{:S(2)}, u32[]{:S(2)}) collective-permute-start(bf16[528,256]{1,0:T(8,128)(2,1)S(1)} %fusion.1.refs_0_), channel_id=1, source_target_pairs={{0,6},{1,7},{2,0},{3,1},{4,2},{5,3},{6,4},{7,5},{8,14},{9,15},{10,... | collective-permute-start | bytes 811016 | tf_op jit(solution)/shard_map/ppermute | solution.py:38
  24.4 2.5 %collective-permute-done.11 = bf16[288,256]{1,0:T(8,128)(2,1)S(1)} collective-permute-done((bf16[288,256]{1,0:T(8,128)(2,1)S(1)}, bf16[288,256]{1,0:T(8,128)(2,1)S(1)}, u32[]{:S(2)}, u32[]{:S(2)}) %collective-permute-start.11) | collective-permute-done | bytes 147488 | tf_op jit(solution)/shard_map/ppermute | solution.py:28
  26.9 2.7 %collective-permute-start.2 = (bf16[528,256]{1,0:T(8,128)(2,1)S(1)}, bf16[528,256]{1,0:T(8,128)(2,1)S(1)}, u32[]{:S(2)}, u32[]{:S(2)}) collective-permute-start(bf16[528,256]{1,0:T(8,128)(2,1)S(1)} %fusion.1.refs_0_), channel_id=1, source_target_pairs={{0,4},{1,5},{2,6},{3,7},{4,0},{5,1},{6,2},{7,3},{8,12},{9,13},{10,... | collective-permute-start | bytes 811016 | tf_op jit(solution)/shard_map/ppermute | solution.py:38
  29.8 3.0 %collective-permute-done.13 = bf16[288,256]{1,0:T(8,128)(2,1)S(1)} collective-permute-done((bf16[288,256]{1,0:T(8,128)(2,1)S(1)}, bf16[288,256]{1,0:T(8,128)(2,1)S(1)}, u32[]{:S(2)}, u32[]{:S(2)}) %collective-permute-start.13) | collective-permute-done | bytes 147488 | tf_op jit(solution)/shard_map/ppermute | solution.py:28
  32.8 2.3 %collective-permute-start.10 = (bf16[288,256]{1,0:T(8,128)(2,1)S(1)}, bf16[288,256]{1,0:T(8,128)(2,1)}, u32[]{:S(2)}, u32[]{:S(2)}) collective-permute-start(bf16[288,256]{1,0:T(8,128)(2,1)S(1)} %pad_maximum_fusion.refs_8_), channel_id=1, source_target_pairs={{0,16},{8,24},{16,0},{24,8},{32,48},{40,56},{48,32},{56,40},{64,80... | collective-permute-start | bytes 442376 | tf_op jit(solution)/shard_map/ppermute | solution.py:33
  35.1 4.4 %collective-permute-done.10.refs_11_ = bf16[288,256]{1,0:T(8,128)(2,1)} collective-permute-done((bf16[288,256]{1,0:T(8,128)(2,1)S(1)}, bf16[288,256]{1,0:T(8,128)(2,1)}, u32[]{:S(2)}, u32[]{:S(2)}) %collective-permute-start.10) | collective-permute-done | bytes 147488 | tf_op jit(solution)/shard_map/ppermute | solution.py:33
  39.5 2.7 %collective-permute-start.14 = (bf16[864,256]{1,0:T(8,128)(2,1)S(1)}, bf16[864,256]{1,0:T(8,128)(2,1)S(1)}, u32[]{:S(2)}, u32[]{:S(2)}) collective-permute-start(bf16[864,256]{1,0:T(8,128)(2,1)S(1)} %constant_dynamic-update-slice_fusion.refs_12_), channel_id=1, source_target_pairs={{0,8},{8,16},{16,24},{24,0},{32,40},{40,48},{48,56},{56,32},{64,72... | collective-permute-start | bytes 1327112 | tf_op jit(solution)/shard_map/ppermute | solution.py:33
  42.3 1.6 %collective-permute-start.16 = (bf16[864,256]{1,0:T(8,128)(2,1)S(1)}, bf16[864,256]{1,0:T(8,128)(2,1)S(1)}, u32[]{:S(2)}, u32[]{:S(2)}) collective-permute-start(bf16[864,256]{1,0:T(8,128)(2,1)S(1)} %constant_dynamic-update-slice_fusion.refs_12_), channel_id=1, source_target_pairs={{0,16},{8,24},{16,0},{24,8},{32,48},{40,56},{48,32},{56,40},{64,80... | collective-permute-start | bytes 1327112 | tf_op jit(solution)/shard_map/ppermute | solution.py:33
  43.9 0.5 collective-permute-start.6
  44.4 0.6 pad_add_fusion.where
  45.0 0.8 copy.24
  45.7 0.7 stack.74
  46.4 1.3 %bitcast_select_fusion.ids = s32[32,8]{1,0:T(8,128)} fusion(s32[32,1,8]{2,0,1:T(8,128)S(1)} %copy.24, s32[32]{0:T(128)} %bitcast.24), kind=kLoop, calls=%fused_computation.9 | loop fusion | flops 512 | bytes 2176 | tf_op jit(solution)/shard_map/jit(_where)/select_n | solution.py:148
  47.7 4.9 %collective-permute-done.14.refs_13_ = bf16[864,256]{1,0:T(8,128)(2,1)S(1)} collective-permute-done((bf16[864,256]{1,0:T(8,128)(2,1)S(1)}, bf16[864,256]{1,0:T(8,128)(2,1)S(1)}, u32[]{:S(2)}, u32[]{:S(2)}) %collective-permute-start.14) | collective-permute-done | bytes 442400 | tf_op jit(solution)/shard_map/ppermute | solution.py:33
  52.6 7.0 %collective-permute-done.15.refs_14_ = bf16[864,256]{1,0:T(8,128)(2,1)S(1)} collective-permute-done((bf16[864,256]{1,0:T(8,128)(2,1)S(1)}, bf16[864,256]{1,0:T(8,128)(2,1)S(1)}, u32[]{:S(2)}, u32[]{:S(2)}) %collective-permute-start.15) | collective-permute-done | bytes 442400 | tf_op jit(solution)/shard_map/ppermute | solution.py:33
  59.7 0.7 copy-done.4
  60.4 0.8 copy-done.5
  61.2 15.7 %stats.1 = (f32[64,128]{1,0:T(8,128)}, bf16[32,128,256]{2,1,0:T(8,128)(2,1)}, bf16[33,128,256]{2,1,0:T(8,128)(2,1)}, f32[33,128,128]{2,1,0:T(8,128)}) custom-call(s32[32,8]{1,0:T(8,128)} %bitcast_select_fusion.ids, s32[32]{0:T(128)} %bitcast.25, s32[4]{0:T(128)} %pad_add_fusion.where, bf16[528,256]{1,0:T(8,128)(2,1)} %copy-done, bf16[528,256]{1,0:T(8,128)(2,1)} %copy-done.6, ...), custom_call_target="tpu_custom_call" | custom-call | tf_op jit(solution)/shard_map/stats/pallas_call | solution.py:159
  77.0 0.7 slice.47
  77.7 0.7 slice.48
  78.4 0.7 slice.49
  79.1 0.7 slice.50
  79.8 0.7 slice.51
  80.5 0.7 slice.52
  81.2 0.7 slice.53
  82.0 0.8 fusion.2
  82.9 3.1 %collective-permute-start.19 = (f32[64,128]{1,0:T(8,128)S(1)}, f32[64,128]{1,0:T(8,128)S(1)}, u32[]{:S(2)}, u32[]{:S(2)}) collective-permute-start(f32[64,128]{1,0:T(8,128)S(1)} %pad_maximum_fusion.2.s0), channel_id=1, source_target_pairs={{0,6},{1,7},{2,0},{3,1},{4,2},{5,3},{6,4},{7,5},{8,14},{9,15},{10,... | collective-permute-start | bytes 98312 | tf_op jit(solution)/shard_map/ppermute | solution.py:38
  86.1 0.9 collective-permute-start.20
  87.0 0.7 select_reduce_fusion
  87.7 0.2 collective-permute-done.18.s1
  87.9 3.5 %collective-permute-done.20.s3 = f32[64,128]{1,0:T(8,128)S(1)} collective-permute-done((f32[64,128]{1,0:T(8,128)S(1)}, f32[64,128]{1,0:T(8,128)S(1)}, u32[]{:S(2)}, u32[]{:S(2)}) %collective-permute-start.20) | collective-permute-done | bytes 32800 | tf_op jit(solution)/shard_map/ppermute | solution.py:38
  91.5 0.6 copy-done.15
  92.1 13.1 %spend.1 = (f32[32,128]{1,0:T(8,128)}, f32[32,128]{1,0:T(8,128)}) custom-call(s32[32,8]{1,0:T(8,128)} %bitcast_select_fusion.ids, s32[32]{0:T(128)} %bitcast.26, f32[64,128]{1,0:T(8,128)} %copy-done.12, f32[64,128]{1,0:T(8,128)} %copy-done.13, f32[64,128]{1,0:T(8,128)} %copy-done.14, f32[64,128]{1,0:T(8,128)} %copy-done.15, f32[32,128]{1,0:T(8,128)} %bitcast.22, ...), custom_call_target="tpu_custom_call" | custom-call | tf_op jit(solution)/shard_map/spend/pallas_call | solution.py:186
  105.2 18.2 %all_to_all.9 = f32[32,1,128]{2,1,0:T(1,128)S(1)} all-to-all(f32[32,1,128]{2,1,0:T(1,128)} %bitcast.23), channel_id=1, replica_groups=mesh['imp'=32,'camp'=8] {'imp'}, dimensions={0} | all-to-all | bytes 32768 | tf_op jit(solution)/shard_map/all_to_all | solution.py:199
  123.5 0.5 divide_add_fusion
  (72 shorter events, 0.7 us)
Async XLA Ops:
  2.1 9.9 %collective-permute-start.7 = (bf16[144,256]{1,0:T(8,128)(2,1)S(1)}, bf16[144,256]{1,0:T(8,128)(2,1)S(1)}, u32[]{:S(2)}, u32[]{:S(2)}) collective-permute-start(bf16[144,256]{1,0:T(8,128)(2,1)S(1)} %pad_maximum_fusion.1), channel_id=1, source_target_pairs={{0,128},{8,136},{16,144},{24,152},{32,160},{40,168},{48,176},{56,1... | collective-permute-start | bytes 221192 | tf_op jit(solution)/shard_map/ppermute | solution.py:28
  12.9 46.7 %copy-start.2 = (bf16[288,256]{1,0:T(8,128)(2,1)}, bf16[288,256]{1,0:T(8,128)(2,1)S(1)}, u32[]{:S(2)}) copy-start(bf16[288,256]{1,0:T(8,128)(2,1)S(1)} %pad_maximum_fusion.refs_8_) | copy-start | bytes 442372
  12.9 9.0 %collective-permute-start.8 = (bf16[288,256]{1,0:T(8,128)(2,1)S(1)}, bf16[288,256]{1,0:T(8,128)(2,1)S(1)}, u32[]{:S(2)}, u32[]{:S(2)}) collective-permute-start(bf16[288,256]{1,0:T(8,128)(2,1)S(1)} %pad_maximum_fusion.refs_8_), channel_id=1, source_target_pairs={{0,8},{8,16},{16,24},{24,0},{32,40},{40,48},{48,56},{56,32},{64,72... | collective-permute-start | bytes 442376 | tf_op jit(solution)/shard_map/ppermute | solution.py:33
  15.6 44.1 %copy-start = (bf16[528,256]{1,0:T(8,128)(2,1)}, bf16[528,256]{1,0:T(8,128)(2,1)S(1)}, u32[]{:S(2)}) copy-start(bf16[528,256]{1,0:T(8,128)(2,1)S(1)} %fusion.1.refs_0_) | copy-start | bytes 811012
  15.6 19.5 %collective-permute-start = (bf16[528,256]{1,0:T(8,128)(2,1)S(1)}, bf16[528,256]{1,0:T(8,128)(2,1)S(1)}, u32[]{:S(2)}, u32[]{:S(2)}) collective-permute-start(bf16[528,256]{1,0:T(8,128)(2,1)S(1)} %fusion.1.refs_0_), channel_id=1, source_target_pairs={{0,2},{1,3},{2,4},{3,5},{4,6},{5,7},{6,0},{7,1},{8,10},{9,11},{10,... | collective-permute-start | bytes 811016 | tf_op jit(solution)/shard_map/ppermute | solution.py:38
  17.1 5.5 %collective-permute-start.9 = (bf16[288,256]{1,0:T(8,128)(2,1)S(1)}, bf16[288,256]{1,0:T(8,128)(2,1)}, u32[]{:S(2)}, u32[]{:S(2)}) collective-permute-start(bf16[288,256]{1,0:T(8,128)(2,1)S(1)} %pad_maximum_fusion.refs_8_), channel_id=1, source_target_pairs={{0,24},{8,0},{16,8},{24,16},{32,56},{40,32},{48,40},{56,48},{64,88... | collective-permute-start | bytes 442376 | tf_op jit(solution)/shard_map/ppermute | solution.py:33
  17.6 9.3 %collective-permute-start.11 = (bf16[288,256]{1,0:T(8,128)(2,1)S(1)}, bf16[288,256]{1,0:T(8,128)(2,1)S(1)}, u32[]{:S(2)}, u32[]{:S(2)}) collective-permute-start(bf16[288,256]{1,0:T(8,128)(2,1)S(1)} %pad_maximum_fusion.refs_8_), channel_id=1, source_target_pairs={{0,32},{8,40},{16,48},{24,56},{32,64},{40,72},{48,80},{56,88},{64,... | collective-permute-start | bytes 442376 | tf_op jit(solution)/shard_map/ppermute | solution.py:28
  19.3 10.3 %collective-permute-start.12 = (bf16[288,256]{1,0:T(8,128)(2,1)S(1)}, bf16[288,256]{1,0:T(8,128)(2,1)S(1)}, u32[]{:S(2)}, u32[]{:S(2)}) collective-permute-start(bf16[288,256]{1,0:T(8,128)(2,1)S(1)} %pad_maximum_fusion.refs_8_), channel_id=1, source_target_pairs={{0,224},{8,232},{16,240},{24,248},{32,0},{40,8},{48,16},{56,24},{6... | collective-permute-start | bytes 442376 | tf_op jit(solution)/shard_map/ppermute | solution.py:28
  22.0 0.7 copy-start.11
  22.0 10.8 %collective-permute-start.13 = (bf16[288,256]{1,0:T(8,128)(2,1)S(1)}, bf16[288,256]{1,0:T(8,128)(2,1)S(1)}, u32[]{:S(2)}, u32[]{:S(2)}) collective-permute-start(bf16[288,256]{1,0:T(8,128)(2,1)S(1)} %pad_maximum_fusion.refs_8_), channel_id=1, source_target_pairs={{0,64},{8,72},{16,80},{24,88},{32,96},{40,104},{48,112},{56,120},{... | collective-permute-start | bytes 442376 | tf_op jit(solution)/shard_map/ppermute | solution.py:28
  22.6 19.6 %collective-permute-start.1 = (bf16[528,256]{1,0:T(8,128)(2,1)S(1)}, bf16[528,256]{1,0:T(8,128)(2,1)S(1)}, u32[]{:S(2)}, u32[]{:S(2)}) collective-permute-start(bf16[528,256]{1,0:T(8,128)(2,1)S(1)} %fusion.1.refs_0_), channel_id=1, source_target_pairs={{0,6},{1,7},{2,0},{3,1},{4,2},{5,3},{6,4},{7,5},{8,14},{9,15},{10,... | collective-permute-start | bytes 811016 | tf_op jit(solution)/shard_map/ppermute | solution.py:38
  26.9 15.4 %collective-permute-start.2 = (bf16[528,256]{1,0:T(8,128)(2,1)S(1)}, bf16[528,256]{1,0:T(8,128)(2,1)S(1)}, u32[]{:S(2)}, u32[]{:S(2)}) collective-permute-start(bf16[528,256]{1,0:T(8,128)(2,1)S(1)} %fusion.1.refs_0_), channel_id=1, source_target_pairs={{0,4},{1,5},{2,6},{3,7},{4,0},{5,1},{6,2},{7,3},{8,12},{9,13},{10,... | collective-permute-start | bytes 811016 | tf_op jit(solution)/shard_map/ppermute | solution.py:38
  29.7 14.2 %collective-permute-start.3 = (bf16[528,256]{1,0:T(8,128)(2,1)S(1)}, bf16[528,256]{1,0:T(8,128)(2,1)S(1)}, u32[]{:S(2)}, u32[]{:S(2)}) collective-permute-start(bf16[528,256]{1,0:T(8,128)(2,1)S(1)} %fusion.1.refs_0_), channel_id=1, source_target_pairs={{0,1},{1,0},{2,3},{3,2},{4,5},{5,4},{6,7},{7,6},{8,9},{9,8},{10,11... | collective-permute-start | bytes 811016 | tf_op jit(solution)/shard_map/ppermute | solution.py:43
  32.8 6.8 %collective-permute-start.10 = (bf16[288,256]{1,0:T(8,128)(2,1)S(1)}, bf16[288,256]{1,0:T(8,128)(2,1)}, u32[]{:S(2)}, u32[]{:S(2)}) collective-permute-start(bf16[288,256]{1,0:T(8,128)(2,1)S(1)} %pad_maximum_fusion.refs_8_), channel_id=1, source_target_pairs={{0,16},{8,24},{16,0},{24,8},{32,48},{40,56},{48,32},{56,40},{64,80... | collective-permute-start | bytes 442376 | tf_op jit(solution)/shard_map/ppermute | solution.py:33
  35.1 24.6 %copy-start.6 = (bf16[528,256]{1,0:T(8,128)(2,1)}, bf16[528,256]{1,0:T(8,128)(2,1)S(1)}, u32[]{:S(2)}) copy-start(bf16[528,256]{1,0:T(8,128)(2,1)S(1)} %collective-permute-done.refs_1_) | copy-start | bytes 811012
  35.1 8.8 %collective-permute-start.4 = (bf16[528,256]{1,0:T(8,128)(2,1)S(1)}, bf16[528,256]{1,0:T(8,128)(2,1)S(1)}, u32[]{:S(2)}, u32[]{:S(2)}) collective-permute-start(bf16[528,256]{1,0:T(8,128)(2,1)S(1)} %collective-permute-done.refs_1_), channel_id=1, source_target_pairs={{0,1},{1,0},{2,3},{3,2},{4,5},{5,4},{6,7},{7,6},{8,9},{9,8},{10,11... | collective-permute-start | bytes 811016 | tf_op jit(solution)/shard_map/ppermute | solution.py:43
  35.1 24.5 %copy-start.1 = (bf16[864,256]{1,0:T(8,128)(2,1)}, bf16[864,256]{1,0:T(8,128)(2,1)S(1)}, u32[]{:S(2)}) copy-start(bf16[864,256]{1,0:T(8,128)(2,1)S(1)} %constant_dynamic-update-slice_fusion.refs_12_) | copy-start | bytes 1327108
  39.5 13.1 %collective-permute-start.14 = (bf16[864,256]{1,0:T(8,128)(2,1)S(1)}, bf16[864,256]{1,0:T(8,128)(2,1)S(1)}, u32[]{:S(2)}, u32[]{:S(2)}) collective-permute-start(bf16[864,256]{1,0:T(8,128)(2,1)S(1)} %constant_dynamic-update-slice_fusion.refs_12_), channel_id=1, source_target_pairs={{0,8},{8,16},{16,24},{24,0},{32,40},{40,48},{48,56},{56,32},{64,72... | collective-permute-start | bytes 1327112 | tf_op jit(solution)/shard_map/ppermute | solution.py:33
  42.3 17.4 %copy-start.7 = (bf16[528,256]{1,0:T(8,128)(2,1)}, bf16[528,256]{1,0:T(8,128)(2,1)S(1)}, u32[]{:S(2)}) copy-start(bf16[528,256]{1,0:T(8,128)(2,1)S(1)} %collective-permute-done.1.refs_2_) | copy-start | bytes 811012
  42.3 17.3 %collective-permute-start.15 = (bf16[864,256]{1,0:T(8,128)(2,1)S(1)}, bf16[864,256]{1,0:T(8,128)(2,1)S(1)}, u32[]{:S(2)}, u32[]{:S(2)}) collective-permute-start(bf16[864,256]{1,0:T(8,128)(2,1)S(1)} %constant_dynamic-update-slice_fusion.refs_12_), channel_id=1, source_target_pairs={{0,24},{8,0},{16,8},{24,16},{32,56},{40,32},{48,40},{56,48},{64,88... | collective-permute-start | bytes 1327112 | tf_op jit(solution)/shard_map/ppermute | solution.py:33
  42.3 17.4 %copy-start.8 = (bf16[528,256]{1,0:T(8,128)(2,1)}, bf16[528,256]{1,0:T(8,128)(2,1)S(1)}, u32[]{:S(2)}) copy-start(bf16[528,256]{1,0:T(8,128)(2,1)S(1)} %collective-permute-done.2.refs_3_) | copy-start | bytes 811012
  42.3 17.3 %collective-permute-start.16 = (bf16[864,256]{1,0:T(8,128)(2,1)S(1)}, bf16[864,256]{1,0:T(8,128)(2,1)S(1)}, u32[]{:S(2)}, u32[]{:S(2)}) collective-permute-start(bf16[864,256]{1,0:T(8,128)(2,1)S(1)} %constant_dynamic-update-slice_fusion.refs_12_), channel_id=1, source_target_pairs={{0,16},{8,24},{16,0},{24,8},{32,48},{40,56},{48,32},{56,40},{64,80... | collective-permute-start | bytes 1327112 | tf_op jit(solution)/shard_map/ppermute | solution.py:33
  43.9 15.8 %copy-start.9 = (bf16[528,256]{1,0:T(8,128)(2,1)}, bf16[528,256]{1,0:T(8,128)(2,1)S(1)}, u32[]{:S(2)}) copy-start(bf16[528,256]{1,0:T(8,128)(2,1)S(1)} %collective-permute-done.3.refs_4_) | copy-start | bytes 811012
  43.9 3.8 %collective-permute-start.5 = (bf16[528,256]{1,0:T(8,128)(2,1)S(1)}, bf16[528,256]{1,0:T(8,128)(2,1)}, u32[]{:S(2)}, u32[]{:S(2)}) collective-permute-start(bf16[528,256]{1,0:T(8,128)(2,1)S(1)} %collective-permute-done.1.refs_2_), channel_id=1, source_target_pairs={{0,1},{1,0},{2,3},{3,2},{4,5},{5,4},{6,7},{7,6},{8,9},{9,8},{10,11... | collective-permute-start | bytes 811016 | tf_op jit(solution)/shard_map/ppermute | solution.py:43
  43.9 15.8 %copy-start.10 = (bf16[528,256]{1,0:T(8,128)(2,1)}, bf16[528,256]{1,0:T(8,128)(2,1)S(1)}, u32[]{:S(2)}) copy-start(bf16[528,256]{1,0:T(8,128)(2,1)S(1)} %collective-permute-done.4.refs_5_) | copy-start | bytes 811012
  43.9 3.8 %collective-permute-start.6 = (bf16[528,256]{1,0:T(8,128)(2,1)S(1)}, bf16[528,256]{1,0:T(8,128)(2,1)}, u32[]{:S(2)}, u32[]{:S(2)}) collective-permute-start(bf16[528,256]{1,0:T(8,128)(2,1)S(1)} %collective-permute-done.2.refs_3_), channel_id=1, source_target_pairs={{0,1},{1,0},{2,3},{3,2},{4,5},{5,4},{6,7},{7,6},{8,9},{9,8},{10,11... | collective-permute-start | bytes 811016 | tf_op jit(solution)/shard_map/ppermute | solution.py:43
  47.7 29.2 %copy-start.18 = (s32[8]{0:T(128)S(1)}, s32[8]{0:T(128)}, u32[]{:S(2)}) copy-start(s32[8]{0:T(128)} %stack.74) | copy-start | bytes 100
  47.7 29.3 %copy-start.16 = (bf16[512]{0:T(512)(128)(2,1)S(1)}, bf16[512]{0:T(512)(128)(2,1)}, u32[]{:S(2)}) copy-start(bf16[512]{0:T(512)(128)(2,1)} %param.8) | copy-start | bytes 3076
  52.6 7.1 %copy-start.3 = (bf16[864,256]{1,0:T(8,128)(2,1)}, bf16[864,256]{1,0:T(8,128)(2,1)S(1)}, u32[]{:S(2)}) copy-start(bf16[864,256]{1,0:T(8,128)(2,1)S(1)} %collective-permute-done.14.refs_13_) | copy-start | bytes 1327108
  59.6 0.8 copy-start.4
  60.4 0.8 copy-start.5
  76.9 5.0 %collective-permute-start.17 = (f32[64,128]{1,0:T(8,128)}, f32[64,128]{1,0:T(8,128)S(1)}, u32[]{:S(2)}, u32[]{:S(2)}) collective-permute-start(f32[64,128]{1,0:T(8,128)} %get-tuple-element.8), channel_id=1, source_target_pairs={{0,1},{1,0},{2,3},{3,2},{4,5},{5,4},{6,7},{7,6},{8,9},{9,8},{10,11... | collective-permute-start | bytes 98312 | tf_op jit(solution)/shard_map/ppermute | solution.py:43
  82.7 8.7 %copy-start.12 = (f32[64,128]{1,0:T(8,128)}, f32[64,128]{1,0:T(8,128)S(1)}, u32[]{:S(2)}) copy-start(f32[64,128]{1,0:T(8,128)S(1)} %pad_maximum_fusion.2.s0) | copy-start | bytes 98308
  82.7 5.2 %collective-permute-start.18 = (f32[64,128]{1,0:T(8,128)S(1)}, f32[64,128]{1,0:T(8,128)S(1)}, u32[]{:S(2)}, u32[]{:S(2)}) collective-permute-start(f32[64,128]{1,0:T(8,128)S(1)} %pad_maximum_fusion.2.s0), channel_id=1, source_target_pairs={{0,2},{1,3},{2,4},{3,5},{4,6},{5,7},{6,0},{7,1},{8,10},{9,11},{10,... | collective-permute-start | bytes 98312 | tf_op jit(solution)/shard_map/ppermute | solution.py:38
  82.9 5.0 %collective-permute-start.19 = (f32[64,128]{1,0:T(8,128)S(1)}, f32[64,128]{1,0:T(8,128)S(1)}, u32[]{:S(2)}, u32[]{:S(2)}) collective-permute-start(f32[64,128]{1,0:T(8,128)S(1)} %pad_maximum_fusion.2.s0), channel_id=1, source_target_pairs={{0,6},{1,7},{2,0},{3,1},{4,2},{5,3},{6,4},{7,5},{8,14},{9,15},{10,... | collective-permute-start | bytes 98312 | tf_op jit(solution)/shard_map/ppermute | solution.py:38
  86.1 5.4 %collective-permute-start.20 = (f32[64,128]{1,0:T(8,128)S(1)}, f32[64,128]{1,0:T(8,128)S(1)}, u32[]{:S(2)}, u32[]{:S(2)}) collective-permute-start(f32[64,128]{1,0:T(8,128)S(1)} %pad_maximum_fusion.2.s0), channel_id=1, source_target_pairs={{0,4},{1,5},{2,6},{3,7},{4,0},{5,1},{6,2},{7,3},{8,12},{9,13},{10,... | collective-permute-start | bytes 98312 | tf_op jit(solution)/shard_map/ppermute | solution.py:38
  87.9 3.5 %copy-start.13 = (f32[64,128]{1,0:T(8,128)}, f32[64,128]{1,0:T(8,128)S(1)}, u32[]{:S(2)}) copy-start(f32[64,128]{1,0:T(8,128)S(1)} %collective-permute-done.18.s1) | copy-start | bytes 98308
  87.9 3.5 %copy-start.14 = (f32[64,128]{1,0:T(8,128)}, f32[64,128]{1,0:T(8,128)S(1)}, u32[]{:S(2)}) copy-start(f32[64,128]{1,0:T(8,128)S(1)} %collective-permute-done.19.s2) | copy-start | bytes 98308
  91.5 0.6 copy-start.15
  92.1 31.4 %copy-start.17 = (bf16[128]{0:T(256)(128)(2,1)S(1)}, bf16[128]{0:T(256)(128)(2,1)}, u32[]{:S(2)}) copy-start(bf16[128]{0:T(256)(128)(2,1)} %param.10) | copy-start | bytes 772
  92.1 31.4 %copy-start.19 = (f32[128]{0:T(128)S(1)}, f32[128]{0:T(128)}, u32[]{:S(2)}) copy-start(f32[128]{0:T(128)} %param.11) | copy-start | bytes 1540

commit v2 on v1

v2 whole, which is shorter than its diff:
```python
import functools
import math

import jax
import jax.numpy as jnp
from jax import lax
from jax.experimental import pallas as pl
from jax.experimental.pallas import tpu as pltpu
from jax.sharding import PartitionSpec as P

D = 256
BLOCK = 128
SLOTS = 8
NZ, NY, NX, NC = 8, 4, 4, 2
OWN = NZ * NY
TILES = 32
DEAD = OWN
PAD = 16
CBLK = BLOCK + PAD
LOG2E = math.log2(math.e)
LN2 = math.log(2.0)
SCALE2 = 3.0 / math.sqrt(D) * LOG2E
VMEM_LIMIT = 24 * 1024 * 1024
UNROLL = 4
GROUPS = TILES * SLOTS // 2 + UNROLL
LAST = GROUPS
TRASH = TILES * SLOTS
LOWEST = -3e38


def shift_z(v, k):
    perm = [(z * NY + y, (z + k) % NZ * NY + y) for z in range(NZ) for y in range(NY)]
    return lax.ppermute(v, "imp", perm)


def shift_y(v, k):
    perm = [(z * NY + y, z * NY + (y + k) % NY) for z in range(NZ) for y in range(NY)]
    return lax.ppermute(v, "imp", perm)


def shift_x(v, k):
    perm = [(x * NC + c, (x + k) % NX * NC + c) for x in range(NX) for c in range(NC)]
    return lax.ppermute(v, "camp", perm)


def other_core(v):
    perm = [(x * NC + c, x * NC + 1 - c) for x in range(NX) for c in range(NC)]
    return lax.ppermute(v, "camp", perm)


PAIR_DZ = (0, 4)
REST_DZ = (7, 3, 1, 5, 6, 2)
DY = (0, 3, 1, 2)
DX = (0, 3, 1, 2)


def fold(v):
    return v.reshape(v.shape[0] // 8, 8, v.shape[1])


def prep_kernel(lists, counts, where, *refs):
    rows_in = refs[:8]
    rows, cost, groups = refs[8:]
    x, core = where[2], where[3]
    for k in range(8):
        xs = lax.rem(x + DX[k % 4], NX)
        cs = core if k < 4 else 1 - core
        first = (xs * NC + cs) * 4
        extra = rows_in[k][4 * BLOCK :, :].astype(jnp.float32)
        for j in range(4):
            rows[first + j] = rows_in[k][j * BLOCK : (j + 1) * BLOCK, :]
            cost[pl.ds(first + j, 1), :] = extra[j // 2 : j // 2 + 1, j % 2 * BLOCK : (j % 2 + 1) * BLOCK]

    def tile(t, at):
        count = counts[t]

        def group(j, at):
            groups[0, at] = t
            groups[1, at] = t * SLOTS + 2 * j
            groups[2, at] = lists[t, 2 * j]
            groups[3, at] = jnp.where(2 * j + 1 < count, lists[t, 2 * j + 1], DEAD)
            return at + 1

        return lax.fori_loop(0, (count + 1) // 2, group, at)

    end = lax.fori_loop(0, TILES, tile, 0)
    for j in range(UNROLL):
        groups[0, end + j] = 0
        groups[1, end + j] = TRASH
        groups[2, end + j] = DEAD
        groups[3, end + j] = DEAD
    groups[0, LAST] = (end + UNROLL - 1) // UNROLL


def stats_kernel(groups, where, *refs):
    rows, pairs, rests = refs[0], refs[1:5], refs[5:9]
    stat, expo, tops, tab, pb, totals = refs[9:]
    z, y = where[0], where[1]
    eye = lax.broadcasted_iota(jnp.int32, (BLOCK, BLOCK), 0) == lax.broadcasted_iota(jnp.int32, (BLOCK, BLOCK), 1)
    ones = jnp.ones((BLOCK, BLOCK), jnp.bfloat16)
    for bufs, offsets in ((pairs, PAIR_DZ), (rests, REST_DZ)):
        for buf, dy in zip(bufs, DY):
            for i, dz in enumerate(offsets):
                b = lax.rem(z + dz, NZ) * NY + lax.rem(y + dy, NY)
                tab[b] = buf[i * CBLK : i * CBLK + BLOCK, :]
                row = buf[i * CBLK + BLOCK : (i + 1) * CBLK, :][0:1, 0:BLOCK].astype(jnp.float32)
                diag = jnp.where(eye, jnp.broadcast_to(row, (BLOCK, BLOCK)), 0.0).astype(jnp.bfloat16)
                pb[b] = jnp.dot(diag, ones, preferred_element_type=jnp.float32) * LOG2E
    tab[DEAD] = jnp.zeros((BLOCK, D), jnp.bfloat16)
    pb[DEAD] = jnp.full((BLOCK, BLOCK), -LOWEST, jnp.float32)
    for p in range(TILES * SLOTS):
        tops[p] = jnp.full((8, BLOCK), LOWEST, jnp.float32)
        totals[p] = jnp.zeros((8, BLOCK), jnp.float32)

    def step(i, carry):
        for u in range(UNROLL):
            g = i * UNROLL + u
            rows_t = rows[groups[0, g]]
            for k in range(2):
                b = groups[2 + k, g]
                raw = lax.dot_general(tab[b], rows_t, (((1,), (1,)), ((), ())), preferred_element_type=jnp.float32)
                logit = fold(raw * SCALE2 - pb[b])
                top = jnp.max(logit, axis=0)
                e = jnp.exp2(logit - top[None])
                expo[2 * g + k] = e.reshape(BLOCK, BLOCK)
                tops[groups[1, g] + k] = top
                totals[groups[1, g] + k] = jnp.sum(e, axis=0)
        return carry

    lax.fori_loop(0, groups[0, LAST], step, 0)

    for t in range(TILES):
        top_s = [tops[t * SLOTS + s] for s in range(SLOTS)]
        top8 = functools.reduce(jnp.maximum, top_s)
        top = jnp.max(top8, axis=0, keepdims=True)
        total8 = sum(totals[t * SLOTS + s] * jnp.exp2(top_s[s] - top) for s in range(SLOTS))
        total = jnp.sum(total8, axis=0, keepdims=True)
        for c in range(NX * NC):
            stat[c, t : t + 1, :] = top
            stat[c, TILES + t : TILES + t + 1, :] = total


def spend_kernel(groups, stats, cost, expo, tops, spend, logz, acc, topw):
    owners = NX * NC
    top = functools.reduce(jnp.maximum, [stats[c, 0:TILES, :] for c in range(owners)])
    total = sum(stats[c, TILES:, :] * jnp.exp2(stats[c, 0:TILES, :] - top) for c in range(owners))
    logz[...] = (top + jnp.log2(total)) * LN2
    topw[0:TILES, :] = top
    topw[TILES:, :] = cost[...] / total
    for b in range(OWN):
        acc[b] = jnp.zeros((BLOCK, BLOCK), jnp.float32)

    def step(i, carry):
        for u in range(UNROLL):
            g = i * UNROLL + u
            t = groups[0, g]
            top_t = topw[pl.ds(t, 1), :]
            w_t = topw[pl.ds(TILES + t, 1), :]
            for k in range(2):
                factor = jnp.exp2(tops[groups[1, g] + k] - top_t) * w_t
                b = groups[2 + k, g]
                part = fold(expo[2 * g + k]) * factor[None]
                acc[b] = acc[b] + part.reshape(BLOCK, BLOCK)
        return carry

    lax.fori_loop(0, groups[0, LAST], step, 0)
    for b in range(OWN):
        spend[b : b + 1, :] = jnp.sum(acc[b].T, axis=0, keepdims=True)


VM = pl.BlockSpec(memory_space=pltpu.VMEM)
SM = pl.BlockSpec(memory_space=pltpu.SMEM)
OUT = pltpu.VMEM


def local(imp_emb, imp_cost, camp_emb, prices, spend_limits, block_lists, block_counts):
    imp, camp = lax.axis_index("imp"), lax.axis_index("camp")
    where = jnp.stack([imp // NY, imp % NY, camp // NC, camp % NC]).astype(jnp.int32)

    blk = jnp.concatenate([camp_emb, jnp.pad(prices.reshape(1, BLOCK), ((0, PAD - 1), (0, D - BLOCK)))], 0)
    pair = jnp.concatenate([blk, shift_z(blk, 4)], 0)
    own = jnp.concatenate([imp_emb, jnp.pad(imp_cost.reshape(2, D), ((0, PAD - 2), (0, 0)))], 0)
    rows_in = [own] + [shift_x(own, k) for k in (1, -1, 2)]
    rest = jnp.concatenate([shift_z(pair, 1), shift_z(pair, -1), shift_z(pair, 2)], 0)
    pairs = [pair] + [shift_y(pair, k) for k in (1, -1, 2)]
    rests = [rest] + [shift_y(rest, k) for k in (1, -1, 2)]
    rows_in = rows_in + [other_core(v) for v in rows_in]

    params = pltpu.CompilerParams(vmem_limit_bytes=VMEM_LIMIT)
    rows, cost, groups = pl.pallas_call(
        prep_kernel,
        in_specs=[SM] * 3 + [VM] * 8,
        out_specs=[VM, VM, SM],
        out_shape=[
            OUT((TILES, BLOCK, D), jnp.bfloat16),
            OUT((TILES, BLOCK), jnp.float32),
            jax.ShapeDtypeStruct((4, GROUPS + 1), jnp.int32),
        ],
        compiler_params=params,
        name="prep",
    )(block_lists[:, 0, :], block_counts[:, 0], where, *rows_in)

    stat, expo, tops = pl.pallas_call(
        stats_kernel,
        in_specs=[SM] * 2 + [VM] * 9,
        out_specs=[VM] * 3,
        out_shape=[
            OUT((NX * NC, 2 * TILES, BLOCK), jnp.float32),
            OUT((2 * GROUPS, BLOCK, BLOCK), jnp.float32),
            OUT((TRASH + 2, 8, BLOCK), jnp.float32),
        ],
        scratch_shapes=[
            pltpu.VMEM((OWN + 1, BLOCK, D), jnp.bfloat16),
            pltpu.VMEM((OWN + 1, BLOCK, BLOCK), jnp.float32),
            pltpu.VMEM((TRASH + 2, 8, BLOCK), jnp.float32),
        ],
        compiler_params=params,
        name="stats",
    )(groups, where, rows, *pairs, *rests)

    stats = lax.all_to_all(stat, "camp", 0, 0)

    spend, logz = pl.pallas_call(
        spend_kernel,
        in_specs=[SM] + [VM] * 4,
        out_specs=[VM] * 2,
        out_shape=[
            OUT((OWN, BLOCK), jnp.float32),
            jax.ShapeDtypeStruct((TILES, BLOCK), jnp.float32),
        ],
        scratch_shapes=[
            pltpu.VMEM((OWN + 1, BLOCK, BLOCK), jnp.float32),
            pltpu.VMEM((2 * TILES, BLOCK), jnp.float32),
        ],
        compiler_params=params,
        name="spend",
    )(groups, stats, cost, expo, tops)

    mine = jnp.sum(lax.all_to_all(spend, "imp", 0, 0), axis=0)
    new_prices = prices.astype(jnp.float32) + 2.0 * (mine - spend_limits) / (mine + spend_limits)
    return (new_prices, logz.reshape(TILES * BLOCK))


def solution(mesh):
    return jax.shard_map(
        local,
        mesh=mesh,
        in_specs=(
            P(("imp", "camp"), None),
            P(("imp", "camp")),
            P(("camp", "imp"), None),
            P(("camp", "imp")),
            P(("camp", "imp")),
            P("imp", "camp", None),
            P("imp", "camp"),
        ),
        out_specs=(P(("camp", "imp")), P("imp")),
        check_vma=False,
    )
```

time: 125 us -> 105 us (0.84)
  Pallas kernels: 28.8 us -> 13 us
  blocking collectives: 18.2 us -> 28.1 us
  starting transfers between devices: 31.7 us -> 26.2 us
  other arithmetic: 6.62 us -> 3.31 us
  waiting for transfers between devices: 27.7 us -> 24.4 us
  local copies, waits for them, and re-layouts: 10 us -> 8.59 us
    pallas_call x2 -> x3, Pallas kernels: 28.8 us -> 13 us  [the longest x1 7.38 us: local(): pl.pallas_call(stats_kernel, in_specs=[SM] * 2 + [VM] * 9, out_specs=[VM]...]
    all_to_all x0 -> x1, blocking collectives: none -> 11.5 us  [local(): stats = lax.all_to_all(stat, 'camp', 0, 0)]
    ppermute x6 -> x3, starting transfers between devices: 10.3 us -> 4.95 us  [shift_x(): return lax.ppermute(v, 'camp', perm)]
    slice x7 -> x0, local copies, waits for them, and re-layouts: 4.77 us -> none  [local(): v[512:514, :].reshape(4, BLOCK)]
    unnamed x43 -> x25, local copies, waits for them, and re-layouts: 3.05 us -> 7.22 us
    ppermute x6 -> x3, waiting for transfers between devices: 3.78 us -> 0.01 us  [shift_x(): return lax.ppermute(v, 'camp', perm)]
    all_to_all x1, blocking collectives: 18.2 us -> 16.5 us  [local(): mine = jnp.sum(lax.all_to_all(spend, 'imp', 0, 0), axis=0)]
    select_n x1 -> x0, other arithmetic: 1.32 us -> none  [local(): jnp.where(jnp.arange(SLOTS, dtype=jnp.int32)[None, :] < counts[:, None],...]
  transfers between devices with their start and end apart: 21 -> 17, of which waited for: 8 -> 6; matrix products, arithmetic and copies ran while one was open for 9% -> 3% of each run, Pallas kernels for 0% -> 3%
where the time goes in v2:
time: 105 us; the launch traced here: 104 us
  blocking collectives  28.1 us (27%)
  starting transfers between devices  26.2 us (25%)
  waiting for transfers between devices  24.4 us (23%)
  Pallas kernels  13 us (12%)
  local copies, waits for them, and re-layouts  8.59 us (8%)
  other arithmetic  3.31 us (3%)
    all_to_all x1, blocking collectives, local(): mine = jnp.sum(lax.all_to_all(spend, 'imp', 0, 0), axis=0)  16.5 us
    ppermute x6, waiting for transfers between devices, shift_y(): return lax.ppermute(v, 'imp', perm)  15.9 us
    ppermute x4, starting transfers between devices, shift_z(): return lax.ppermute(v, 'imp', perm)  12 us
    all_to_all x1, blocking collectives, local(): stats = lax.all_to_all(stat, 'camp', 0, 0)  11.5 us
    ppermute x6, starting transfers between devices, shift_y(): return lax.ppermute(v, 'imp', perm)  8.73 us
    ppermute x4, waiting for transfers between devices, shift_z(): return lax.ppermute(v, 'imp', perm)  7.47 us
    pallas_call x1, Pallas kernels, local(): pl.pallas_call(stats_kernel, in_specs=[SM] * 2 + [VM] * 9, out_specs=[VM]...  7.38 us
    unnamed x25, local copies, waits for them, and re-layouts  7.22 us
  transfers between devices with their start and end apart: 17, of which 6 were waited for; matrix products, arithmetic and copies ran while one was open for 3% of the time, Pallas kernels for 3%

profile of v2, /device:TPU:8, one launch (start us, length us, event | category | flops | bytes accessed | tf_op | source)
XLA Modules:
  0.0 104.3 jit_solution(10812666433041607296)
XLA Ops:
  0.6 0.7 pad.9
  1.3 0.8 pad_maximum_fusion.1
  2.1 7.2 %collective-permute-start.7 = (bf16[144,256]{1,0:T(8,128)(2,1)S(1)}, bf16[144,256]{1,0:T(8,128)(2,1)S(1)}, u32[]{:S(2)}, u32[]{:S(2)}) collective-permute-start(bf16[144,256]{1,0:T(8,128)(2,1)S(1)} %pad_maximum_fusion.1), channel_id=1, source_target_pairs={{0,128},{8,136},{16,144},{24,152},{32,160},{40,168},{48,176},{56,1... | collective-permute-start | bytes 221192 | tf_op jit(solution)/shard_map/ppermute | solution.py:33
  9.3 0.7 reshape.15
  10.0 1.0 fusion.1.refs_0_
  11.0 3.1 %collective-permute-start.2 = (bf16[528,256]{1,0:T(8,128)(2,1)S(1)}, bf16[528,256]{1,0:T(8,128)(2,1)S(1)}, u32[]{:S(2)}, u32[]{:S(2)}) collective-permute-start(bf16[528,256]{1,0:T(8,128)(2,1)S(1)} %fusion.1.refs_0_), channel_id=1, source_target_pairs={{0,4},{1,5},{2,6},{3,7},{4,0},{5,1},{6,2},{7,3},{8,12},{9,13},{10,... | collective-permute-start | bytes 811016 | tf_op jit(solution)/shard_map/ppermute | solution.py:43
  14.1 0.0 collective-permute-done.7
  14.1 0.8 pad_maximum_fusion.refs_1_
  15.0 1.6 %collective-permute-start.13 = (bf16[288,256]{1,0:T(8,128)(2,1)S(1)}, bf16[288,256]{1,0:T(8,128)(2,1)S(1)}, u32[]{:S(2)}, u32[]{:S(2)}) collective-permute-start(bf16[288,256]{1,0:T(8,128)(2,1)S(1)} %pad_maximum_fusion.refs_1_), channel_id=1, source_target_pairs={{0,64},{8,72},{16,80},{24,88},{32,96},{40,104},{48,112},{56,120},{... | collective-permute-start | bytes 442376 | tf_op jit(solution)/shard_map/ppermute | solution.py:33
  16.5 1.0 collective-permute-start.11
  17.5 2.2 %collective-permute-start.12 = (bf16[288,256]{1,0:T(8,128)(2,1)S(1)}, bf16[288,256]{1,0:T(8,128)(2,1)S(1)}, u32[]{:S(2)}, u32[]{:S(2)}) collective-permute-start(bf16[288,256]{1,0:T(8,128)(2,1)S(1)} %pad_maximum_fusion.refs_1_), channel_id=1, source_target_pairs={{0,224},{8,232},{16,240},{24,248},{32,0},{40,8},{48,16},{56,24},{6... | collective-permute-start | bytes 442376 | tf_op jit(solution)/shard_map/ppermute | solution.py:33
  19.7 7.3 %collective-permute-done.13 = bf16[288,256]{1,0:T(8,128)(2,1)S(1)} collective-permute-done((bf16[288,256]{1,0:T(8,128)(2,1)S(1)}, bf16[288,256]{1,0:T(8,128)(2,1)S(1)}, u32[]{:S(2)}, u32[]{:S(2)}) %collective-permute-start.13) | collective-permute-done | bytes 147488 | tf_op jit(solution)/shard_map/ppermute | solution.py:33
  27.0 0.8 collective-permute-start.1
  27.9 0.2 collective-permute-done.11
  28.0 1.0 collective-permute-start
  29.1 0.0 collective-permute-start.6
  29.1 0.0 collective-permute-done.12
  29.1 2.4 %collective-permute-start.10 = (bf16[288,256]{1,0:T(8,128)(2,1)S(1)}, bf16[288,256]{1,0:T(8,128)(2,1)S(1)}, u32[]{:S(2)}, u32[]{:S(2)}) collective-permute-start(bf16[288,256]{1,0:T(8,128)(2,1)S(1)} %pad_maximum_fusion.refs_1_), channel_id=1, source_target_pairs={{0,16},{8,24},{16,0},{24,8},{32,48},{40,56},{48,32},{56,40},{64,80... | collective-permute-start | bytes 442376 | tf_op jit(solution)/shard_map/ppermute | solution.py:38
  31.5 5.4 %collective-permute-done.10.refs_4_ = bf16[288,256]{1,0:T(8,128)(2,1)S(1)} collective-permute-done((bf16[288,256]{1,0:T(8,128)(2,1)S(1)}, bf16[288,256]{1,0:T(8,128)(2,1)S(1)}, u32[]{:S(2)}, u32[]{:S(2)}) %collective-permute-start.10) | collective-permute-done | bytes 147488 | tf_op jit(solution)/shard_map/ppermute | solution.py:38
  36.9 0.7 copy-done.6
  37.6 2.3 %collective-permute-start.16 = (bf16[864,256]{1,0:T(8,128)(2,1)S(1)}, bf16[864,256]{1,0:T(8,128)(2,1)S(1)}, u32[]{:S(2)}, u32[]{:S(2)}) collective-permute-start(bf16[864,256]{1,0:T(8,128)(2,1)S(1)} %constant_dynamic-update-slice_fusion.refs_5_), channel_id=1, source_target_pairs={{0,16},{8,24},{16,0},{24,8},{32,48},{40,56},{48,32},{56,40},{64,80... | collective-permute-start | bytes 1327112 | tf_op jit(solution)/shard_map/ppermute | solution.py:38
  39.9 0.0 collective-permute-done.3.refs_4_
  39.9 1.3 %collective-permute-start.15 = (bf16[864,256]{1,0:T(8,128)(2,1)S(1)}, bf16[864,256]{1,0:T(8,128)(2,1)S(1)}, u32[]{:S(2)}, u32[]{:S(2)}) collective-permute-start(bf16[864,256]{1,0:T(8,128)(2,1)S(1)} %constant_dynamic-update-slice_fusion.refs_5_), channel_id=1, source_target_pairs={{0,24},{8,0},{16,8},{24,16},{32,56},{40,32},{48,40},{56,48},{64,88... | collective-permute-start | bytes 1327112 | tf_op jit(solution)/shard_map/ppermute | solution.py:38
  41.3 0.0 collective-permute-done.1.refs_2_
  41.3 0.7 collective-permute-start.14
  41.9 0.0 collective-permute-done.refs_1_
  41.9 0.5 collective-permute-start.4
  42.5 1.0 collective-permute-done.5.refs_6_
  43.5 0.7 copy-done.2
  44.2 1.3 %collective-permute-start.9 = (bf16[288,256]{1,0:T(8,128)(2,1)S(1)}, bf16[288,256]{1,0:T(8,128)(2,1)}, u32[]{:S(2)}, u32[]{:S(2)}) collective-permute-start(bf16[288,256]{1,0:T(8,128)(2,1)S(1)} %pad_maximum_fusion.refs_1_), channel_id=1, source_target_pairs={{0,24},{8,0},{16,8},{24,16},{32,56},{40,32},{48,40},{56,48},{64,88... | collective-permute-start | bytes 442376 | tf_op jit(solution)/shard_map/ppermute | solution.py:38
  45.6 0.7 copy-done.4
  46.3 0.7 collective-permute-start.8
  46.9 0.8 copy.10
  47.7 0.1 pad_add_fusion.where
  47.8 1.0 copy-done.3
  48.7 1.0 copy-done.5
  49.7 0.7 copy-done.8
  50.3 3.0 %prep.1 = (bf16[32,128,256]{2,1,0:T(8,128)(2,1)S(1)}, f32[32,128]{1,0:T(8,128)S(1)}, s32[4,133]{1,0:T(4,128)S(1)}) custom-call(s32[32,8]{1,0:T(8,128)S(1)} %bitcast.11, s32[32]{0:T(128)S(1)} %bitcast.13, s32[4]{0:T(128)S(1)} %pad_add_fusion.where, bf16[528,256]{1,0:T(8,128)(2,1)S(1)} %fusion.1.refs_0_, bf16[528,256]{1,0:T(8,128)(2,1)S(1)} %collective-permute-done.refs_1_, ...), custom_call_target="tpu_custom_call" | custom-call | tf_op jit(solution)/shard_map/prep/pallas_call | solution.py:190
  53.3 10.3 %collective-permute-done.9.refs_3_ = bf16[288,256]{1,0:T(8,128)(2,1)} collective-permute-done((bf16[288,256]{1,0:T(8,128)(2,1)S(1)}, bf16[288,256]{1,0:T(8,128)(2,1)}, u32[]{:S(2)}, u32[]{:S(2)}) %collective-permute-start.9) | collective-permute-done | bytes 147488 | tf_op jit(solution)/shard_map/ppermute | solution.py:38
  63.7 0.2 collective-permute-done.8.refs_2_
  63.8 0.8 copy-done
  64.6 1.0 copy-done.1
  65.6 7.4 %stats.1 = (f32[8,64,128]{2,1,0:T(8,128)S(1)}, f32[264,128,128]{2,1,0:T(8,128)S(1)}, f32[258,8,128]{2,1,0:T(8,128)S(1)}) custom-call(s32[4,133]{1,0:T(4,128)S(1)} %get-tuple-element.10.groups, s32[4]{0:T(128)S(1)} %pad_add_fusion.where, bf16[32,128,256]{2,1,0:T(8,128)(2,1)S(1)} %get-tuple-element.11.refs_0_, bf16[288,256]{1,0:T(8,128)(2,1)S(1)} %pad_maximum_fusion.refs_1_, ...), custom_call_target="tpu_custom_call" | custom-call | tf_op jit(solution)/shard_map/stats/pallas_call | solution.py:203
  73.0 11.5 %all_to_all.14.stats = f32[8,64,128]{2,1,0:T(8,128)S(1)} all-to-all(f32[8,64,128]{2,1,0:T(8,128)S(1)} %get-tuple-element.12), channel_id=1, replica_groups=mesh['imp'=32,'camp'=8] {'camp'}, dimensions={0} | all-to-all | bytes 524288 | tf_op jit(solution)/shard_map/all_to_all | solution.py:221
  84.6 2.7 %spend.1 = (f32[32,128]{1,0:T(8,128)S(1)}, f32[32,128]{1,0:T(8,128)}) custom-call(s32[4,133]{1,0:T(4,128)S(1)} %get-tuple-element.10.groups, f32[8,64,128]{2,1,0:T(8,128)S(1)} %all_to_all.14.stats, f32[32,128]{1,0:T(8,128)S(1)} %get-tuple-element.13.cost, f32[264,128,128]{2,1,0:T(8,128)S(1)} %get-tuple-element.14.expo, f32[258,8,128]{2,1,0:T(8,128)S(1)} %get-tuple-element.15.tops), custom_call_target="tpu_custom_call" | custom-call | tf_op jit(solution)/shard_map/spend/pallas_call | solution.py:223
  87.2 16.5 %all_to_all.15 = f32[32,1,128]{2,1,0:T(1,128)S(1)} all-to-all(f32[32,1,128]{2,1,0:T(1,128)S(1)} %bitcast.12), channel_id=1, replica_groups=mesh['imp'=32,'camp'=8] {'imp'}, dimensions={0} | all-to-all | bytes 32768 | tf_op jit(solution)/shard_map/all_to_all | solution.py:239
  103.7 0.1 reduce_sum.9
  103.8 0.5 divide_add_fusion
  (25 shorter events, 0.1 us)
Async XLA Ops:
  2.1 12.0 %collective-permute-start.7 = (bf16[144,256]{1,0:T(8,128)(2,1)S(1)}, bf16[144,256]{1,0:T(8,128)(2,1)S(1)}, u32[]{:S(2)}, u32[]{:S(2)}) collective-permute-start(bf16[144,256]{1,0:T(8,128)(2,1)S(1)} %pad_maximum_fusion.1), channel_id=1, source_target_pairs={{0,128},{8,136},{16,144},{24,152},{32,160},{40,168},{48,176},{56,1... | collective-permute-start | bytes 221192 | tf_op jit(solution)/shard_map/ppermute | solution.py:33
  11.0 18.1 %collective-permute-start.2 = (bf16[528,256]{1,0:T(8,128)(2,1)S(1)}, bf16[528,256]{1,0:T(8,128)(2,1)S(1)}, u32[]{:S(2)}, u32[]{:S(2)}) collective-permute-start(bf16[528,256]{1,0:T(8,128)(2,1)S(1)} %fusion.1.refs_0_), channel_id=1, source_target_pairs={{0,4},{1,5},{2,6},{3,7},{4,0},{5,1},{6,2},{7,3},{8,12},{9,13},{10,... | collective-permute-start | bytes 811016 | tf_op jit(solution)/shard_map/ppermute | solution.py:43
  15.0 12.1 %collective-permute-start.13 = (bf16[288,256]{1,0:T(8,128)(2,1)S(1)}, bf16[288,256]{1,0:T(8,128)(2,1)S(1)}, u32[]{:S(2)}, u32[]{:S(2)}) collective-permute-start(bf16[288,256]{1,0:T(8,128)(2,1)S(1)} %pad_maximum_fusion.refs_1_), channel_id=1, source_target_pairs={{0,64},{8,72},{16,80},{24,88},{32,96},{40,104},{48,112},{56,120},{... | collective-permute-start | bytes 442376 | tf_op jit(solution)/shard_map/ppermute | solution.py:33
  16.5 11.5 %collective-permute-start.11 = (bf16[288,256]{1,0:T(8,128)(2,1)S(1)}, bf16[288,256]{1,0:T(8,128)(2,1)S(1)}, u32[]{:S(2)}, u32[]{:S(2)}) collective-permute-start(bf16[288,256]{1,0:T(8,128)(2,1)S(1)} %pad_maximum_fusion.refs_1_), channel_id=1, source_target_pairs={{0,32},{8,40},{16,48},{24,56},{32,64},{40,72},{48,80},{56,88},{64,... | collective-permute-start | bytes 442376 | tf_op jit(solution)/shard_map/ppermute | solution.py:33
  17.5 11.6 %collective-permute-start.12 = (bf16[288,256]{1,0:T(8,128)(2,1)S(1)}, bf16[288,256]{1,0:T(8,128)(2,1)S(1)}, u32[]{:S(2)}, u32[]{:S(2)}) collective-permute-start(bf16[288,256]{1,0:T(8,128)(2,1)S(1)} %pad_maximum_fusion.refs_1_), channel_id=1, source_target_pairs={{0,224},{8,232},{16,240},{24,248},{32,0},{40,8},{48,16},{56,24},{6... | collective-permute-start | bytes 442376 | tf_op jit(solution)/shard_map/ppermute | solution.py:33
  19.7 20.2 %collective-permute-start.3 = (bf16[528,256]{1,0:T(8,128)(2,1)S(1)}, bf16[528,256]{1,0:T(8,128)(2,1)S(1)}, u32[]{:S(2)}, u32[]{:S(2)}) collective-permute-start(bf16[528,256]{1,0:T(8,128)(2,1)S(1)} %fusion.1.refs_0_), channel_id=1, source_target_pairs={{0,1},{1,0},{2,3},{3,2},{4,5},{5,4},{6,7},{7,6},{8,9},{9,8},{10,11... | collective-permute-start | bytes 811016 | tf_op jit(solution)/shard_map/ppermute | solution.py:48
  27.0 14.2 %collective-permute-start.1 = (bf16[528,256]{1,0:T(8,128)(2,1)S(1)}, bf16[528,256]{1,0:T(8,128)(2,1)S(1)}, u32[]{:S(2)}, u32[]{:S(2)}) collective-permute-start(bf16[528,256]{1,0:T(8,128)(2,1)S(1)} %fusion.1.refs_0_), channel_id=1, source_target_pairs={{0,6},{1,7},{2,0},{3,1},{4,2},{5,3},{6,4},{7,5},{8,14},{9,15},{10,... | collective-permute-start | bytes 811016 | tf_op jit(solution)/shard_map/ppermute | solution.py:43
  28.0 13.9 %collective-permute-start = (bf16[528,256]{1,0:T(8,128)(2,1)S(1)}, bf16[528,256]{1,0:T(8,128)(2,1)S(1)}, u32[]{:S(2)}, u32[]{:S(2)}) collective-permute-start(bf16[528,256]{1,0:T(8,128)(2,1)S(1)} %fusion.1.refs_0_), channel_id=1, source_target_pairs={{0,2},{1,3},{2,4},{3,5},{4,6},{5,7},{6,0},{7,1},{8,10},{9,11},{10,... | collective-permute-start | bytes 811016 | tf_op jit(solution)/shard_map/ppermute | solution.py:43
  29.1 12.9 %collective-permute-start.6 = (bf16[528,256]{1,0:T(8,128)(2,1)S(1)}, bf16[528,256]{1,0:T(8,128)(2,1)S(1)}, u32[]{:S(2)}, u32[]{:S(2)}) collective-permute-start(bf16[528,256]{1,0:T(8,128)(2,1)S(1)} %collective-permute-done.2.refs_3_), channel_id=1, source_target_pairs={{0,1},{1,0},{2,3},{3,2},{4,5},{5,4},{6,7},{7,6},{8,9},{9,8},{10,11... | collective-permute-start | bytes 811016 | tf_op jit(solution)/shard_map/ppermute | solution.py:48
  29.1 7.9 %collective-permute-start.10 = (bf16[288,256]{1,0:T(8,128)(2,1)S(1)}, bf16[288,256]{1,0:T(8,128)(2,1)S(1)}, u32[]{:S(2)}, u32[]{:S(2)}) collective-permute-start(bf16[288,256]{1,0:T(8,128)(2,1)S(1)} %pad_maximum_fusion.refs_1_), channel_id=1, source_target_pairs={{0,16},{8,24},{16,0},{24,8},{32,48},{40,56},{48,32},{56,40},{64,80... | collective-permute-start | bytes 442376 | tf_op jit(solution)/shard_map/ppermute | solution.py:38
  36.9 0.7 copy-start.6
  37.6 26.2 %collective-permute-start.16 = (bf16[864,256]{1,0:T(8,128)(2,1)S(1)}, bf16[864,256]{1,0:T(8,128)(2,1)S(1)}, u32[]{:S(2)}, u32[]{:S(2)}) collective-permute-start(bf16[864,256]{1,0:T(8,128)(2,1)S(1)} %constant_dynamic-update-slice_fusion.refs_5_), channel_id=1, source_target_pairs={{0,16},{8,24},{16,0},{24,8},{32,48},{40,56},{48,32},{56,40},{64,80... | collective-permute-start | bytes 1327112 | tf_op jit(solution)/shard_map/ppermute | solution.py:38
  39.9 23.9 %collective-permute-start.15 = (bf16[864,256]{1,0:T(8,128)(2,1)S(1)}, bf16[864,256]{1,0:T(8,128)(2,1)S(1)}, u32[]{:S(2)}, u32[]{:S(2)}) collective-permute-start(bf16[864,256]{1,0:T(8,128)(2,1)S(1)} %constant_dynamic-update-slice_fusion.refs_5_), channel_id=1, source_target_pairs={{0,24},{8,0},{16,8},{24,16},{32,56},{40,32},{48,40},{56,48},{64,88... | collective-permute-start | bytes 1327112 | tf_op jit(solution)/shard_map/ppermute | solution.py:38
  41.3 22.6 %collective-permute-start.14 = (bf16[864,256]{1,0:T(8,128)(2,1)S(1)}, bf16[864,256]{1,0:T(8,128)(2,1)S(1)}, u32[]{:S(2)}, u32[]{:S(2)}) collective-permute-start(bf16[864,256]{1,0:T(8,128)(2,1)S(1)} %constant_dynamic-update-slice_fusion.refs_5_), channel_id=1, source_target_pairs={{0,8},{8,16},{16,24},{24,0},{32,40},{40,48},{48,56},{56,32},{64,72... | collective-permute-start | bytes 1327112 | tf_op jit(solution)/shard_map/ppermute | solution.py:38
  41.9 1.5 %collective-permute-start.5 = (bf16[528,256]{1,0:T(8,128)(2,1)S(1)}, bf16[528,256]{1,0:T(8,128)(2,1)S(1)}, u32[]{:S(2)}, u32[]{:S(2)}) collective-permute-start(bf16[528,256]{1,0:T(8,128)(2,1)S(1)} %collective-permute-done.1.refs_2_), channel_id=1, source_target_pairs={{0,1},{1,0},{2,3},{3,2},{4,5},{5,4},{6,7},{7,6},{8,9},{9,8},{10,11... | collective-permute-start | bytes 811016 | tf_op jit(solution)/shard_map/ppermute | solution.py:48
  41.9 3.6 %collective-permute-start.4 = (bf16[528,256]{1,0:T(8,128)(2,1)S(1)}, bf16[528,256]{1,0:T(8,128)(2,1)S(1)}, u32[]{:S(2)}, u32[]{:S(2)}) collective-permute-start(bf16[528,256]{1,0:T(8,128)(2,1)S(1)} %collective-permute-done.refs_1_), channel_id=1, source_target_pairs={{0,1},{1,0},{2,3},{3,2},{4,5},{5,4},{6,7},{7,6},{8,9},{9,8},{10,11... | collective-permute-start | bytes 811016 | tf_op jit(solution)/shard_map/ppermute | solution.py:48
  43.5 0.7 copy-start.2
  44.2 19.5 %collective-permute-start.9 = (bf16[288,256]{1,0:T(8,128)(2,1)S(1)}, bf16[288,256]{1,0:T(8,128)(2,1)}, u32[]{:S(2)}, u32[]{:S(2)}) collective-permute-start(bf16[288,256]{1,0:T(8,128)(2,1)S(1)} %pad_maximum_fusion.refs_1_), channel_id=1, source_target_pairs={{0,24},{8,0},{16,8},{24,16},{32,56},{40,32},{48,40},{56,48},{64,88... | collective-permute-start | bytes 442376 | tf_op jit(solution)/shard_map/ppermute | solution.py:38
  45.6 0.7 copy-start.4
  46.3 17.6 %collective-permute-start.8 = (bf16[288,256]{1,0:T(8,128)(2,1)S(1)}, bf16[288,256]{1,0:T(8,128)(2,1)}, u32[]{:S(2)}, u32[]{:S(2)}) collective-permute-start(bf16[288,256]{1,0:T(8,128)(2,1)S(1)} %pad_maximum_fusion.refs_1_), channel_id=1, source_target_pairs={{0,8},{8,16},{16,24},{24,0},{32,40},{40,48},{48,56},{56,32},{64,72... | collective-permute-start | bytes 442376 | tf_op jit(solution)/shard_map/ppermute | solution.py:38
  47.8 1.0 copy-start.3
  48.7 1.0 copy-start.5
  49.7 0.7 copy-start.8
  50.3 14.3 %copy-start.7 = (bf16[288,256]{1,0:T(8,128)(2,1)S(1)}, bf16[288,256]{1,0:T(8,128)(2,1)}, u32[]{:S(2)}) copy-start(bf16[288,256]{1,0:T(8,128)(2,1)} %copy-done.6) | copy-start | bytes 442372
  63.8 0.8 copy-start
  64.6 1.0 copy-start.1
  84.5 19.2 %copy-start.9 = (bf16[128]{0:T(256)(128)(2,1)S(1)}, bf16[128]{0:T(256)(128)(2,1)}, u32[]{:S(2)}) copy-start(bf16[128]{0:T(256)(128)(2,1)} %param.10) | copy-start | bytes 772
  84.6 19.2 %copy-start.10 = (f32[128]{0:T(128)S(1)}, f32[128]{0:T(128)}, u32[]{:S(2)}) copy-start(f32[128]{0:T(128)} %param.11) | copy-start | bytes 1540

commit v3 on v2

--- a/solution.py
+++ b/solution.py
@@ -20,7 +20,7 @@
 LOG2E = math.log2(math.e)
 LN2 = math.log(2.0)
 SCALE2 = 3.0 / math.sqrt(D) * LOG2E
-VMEM_LIMIT = 24 * 1024 * 1024
+VMEM_LIMIT = 16 * 1024 * 1024
 UNROLL = 4
 GROUPS = TILES * SLOTS // 2 + UNROLL
 LAST = GROUPS
@@ -48,9 +48,8 @@
     return lax.ppermute(v, "camp", perm)
 
 
-PAIR_DZ = (0, 4)
-REST_DZ = (7, 3, 1, 5, 6, 2)
-DY = (0, 3, 1, 2)
+NEAR, FAR = (7, 3, 1, 5), (0, 4, 6, 2)
+LAYOUT = ((0, NEAR), (0, FAR), (3, NEAR), (1, NEAR), (3, FAR), (1, FAR), (2, NEAR), (2, FAR))
 DX = (0, 3, 1, 2)
 
 
@@ -58,19 +57,7 @@
     return v.reshape(v.shape[0] // 8, 8, v.shape[1])
 
 
-def prep_kernel(lists, counts, where, *refs):
-    rows_in = refs[:8]
-    rows, cost, groups = refs[8:]
-    x, core = where[2], where[3]
-    for k in range(8):
-        xs = lax.rem(x + DX[k % 4], NX)
-        cs = core if k < 4 else 1 - core
-        first = (xs * NC + cs) * 4
-        extra = rows_in[k][4 * BLOCK :, :].astype(jnp.float32)
-        for j in range(4):
-            rows[first + j] = rows_in[k][j * BLOCK : (j + 1) * BLOCK, :]
-            cost[pl.ds(first + j, 1), :] = extra[j // 2 : j // 2 + 1, j % 2 * BLOCK : (j % 2 + 1) * BLOCK]
-
+def prep_kernel(lists, counts, groups):
     def tile(t, at):
         count = counts[t]
 
@@ -93,29 +80,43 @@
 
 
 def stats_kernel(groups, where, *refs):
-    rows, pairs, rests = refs[0], refs[1:5], refs[5:9]
-    stat, expo, tops, tab, pb, totals = refs[9:]
-    z, y = where[0], where[1]
+    rows_in, camps = refs[:8], refs[8:16]
+    stat, cost, expo, tops, rows, extra, tab, pb, totals, sems = refs[16:]
+    z, y, x, core = where[0], where[1], where[2], where[3]
+    copies = []
+    for k in range(8):
+        q = lax.rem(x + DX[k % 4], NX) * NC + (core if k < 4 else 1 - core)
+        whole = rows.at[pl.ds(pl.multiple_of(q * 512, 512), 512), :]
+        rest = extra.at[pl.ds(pl.multiple_of(q * PAD, PAD), PAD), :]
+        copies.append(pltpu.make_async_copy(rows_in[k].at[0:512, :], whole, sems.at[k]))
+        copies.append(pltpu.make_async_copy(rows_in[k].at[512:528, :], rest, sems.at[8 + k]))
+    for copy in copies:
+        copy.start()
     eye = lax.broadcasted_iota(jnp.int32, (BLOCK, BLOCK), 0) == lax.broadcasted_iota(jnp.int32, (BLOCK, BLOCK), 1)
     ones = jnp.ones((BLOCK, BLOCK), jnp.bfloat16)
-    for bufs, offsets in ((pairs, PAIR_DZ), (rests, REST_DZ)):
-        for buf, dy in zip(bufs, DY):
-            for i, dz in enumerate(offsets):
-                b = lax.rem(z + dz, NZ) * NY + lax.rem(y + dy, NY)
-                tab[b] = buf[i * CBLK : i * CBLK + BLOCK, :]
-                row = buf[i * CBLK + BLOCK : (i + 1) * CBLK, :][0:1, 0:BLOCK].astype(jnp.float32)
-                diag = jnp.where(eye, jnp.broadcast_to(row, (BLOCK, BLOCK)), 0.0).astype(jnp.bfloat16)
-                pb[b] = jnp.dot(diag, ones, preferred_element_type=jnp.float32) * LOG2E
+    for buf, (dy, offsets) in zip(camps, LAYOUT):
+        for i, dz in enumerate(offsets):
+            b = lax.rem(z + dz, NZ) * NY + lax.rem(y + dy, NY)
+            tab[b] = buf[i * CBLK : i * CBLK + BLOCK, :]
+            row = buf[i * CBLK + BLOCK : (i + 1) * CBLK, :][0:1, 0:BLOCK].astype(jnp.float32)
+            diag = jnp.where(eye, jnp.broadcast_to(row, (BLOCK, BLOCK)), 0.0).astype(jnp.bfloat16)
+            pb[b] = jnp.dot(diag, ones, preferred_element_type=jnp.float32) * LOG2E
     tab[DEAD] = jnp.zeros((BLOCK, D), jnp.bfloat16)
     pb[DEAD] = jnp.full((BLOCK, BLOCK), -LOWEST, jnp.float32)
     for p in range(TILES * SLOTS):
         tops[p] = jnp.full((8, BLOCK), LOWEST, jnp.float32)
         totals[p] = jnp.zeros((8, BLOCK), jnp.float32)
+    for copy in copies:
+        copy.wait()
+    for q in range(NX * NC):
+        two = extra[q * PAD : (q + 1) * PAD, :].astype(jnp.float32)
+        for j in range(4):
+            cost[4 * q + j : 4 * q + j + 1, :] = two[j // 2 : j // 2 + 1, j % 2 * BLOCK : (j % 2 + 1) * BLOCK]
 
     def step(i, carry):
         for u in range(UNROLL):
             g = i * UNROLL + u
-            rows_t = rows[groups[0, g]]
+            rows_t = rows[pl.ds(pl.multiple_of(groups[0, g] * BLOCK, BLOCK), BLOCK), :]
             for k in range(2):
                 b = groups[2 + k, g]
                 raw = lax.dot_general(tab[b], rows_t, (((1,), (1,)), ((), ())), preferred_element_type=jnp.float32)
@@ -177,46 +178,53 @@
     imp, camp = lax.axis_index("imp"), lax.axis_index("camp")
     where = jnp.stack([imp // NY, imp % NY, camp // NC, camp % NC]).astype(jnp.int32)
 
+    params = pltpu.CompilerParams(vmem_limit_bytes=VMEM_LIMIT)
+    groups = pl.pallas_call(
+        prep_kernel,
+        in_specs=[SM] * 2,
+        out_specs=SM,
+        out_shape=jax.ShapeDtypeStruct((4, GROUPS + 1), jnp.int32),
+        name="prep",
+    )(block_lists[:, 0, :], block_counts[:, 0])
+
     blk = jnp.concatenate([camp_emb, jnp.pad(prices.reshape(1, BLOCK), ((0, PAD - 1), (0, D - BLOCK)))], 0)
-    pair = jnp.concatenate([blk, shift_z(blk, 4)], 0)
     own = jnp.concatenate([imp_emb, jnp.pad(imp_cost.reshape(2, D), ((0, PAD - 2), (0, 0)))], 0)
-    rows_in = [own] + [shift_x(own, k) for k in (1, -1, 2)]
-    rest = jnp.concatenate([shift_z(pair, 1), shift_z(pair, -1), shift_z(pair, 2)], 0)
-    pairs = [pair] + [shift_y(pair, k) for k in (1, -1, 2)]
-    rests = [rest] + [shift_y(rest, k) for k in (1, -1, 2)]
-    rows_in = rows_in + [other_core(v) for v in rows_in]
-
-    params = pltpu.CompilerParams(vmem_limit_bytes=VMEM_LIMIT)
-    rows, cost, groups = pl.pallas_call(
-        prep_kernel,
-        in_specs=[SM] * 3 + [VM] * 8,
-        out_specs=[VM, VM, SM],
-        out_shape=[
-            OUT((TILES, BLOCK, D), jnp.bfloat16),
-            OUT((TILES, BLOCK), jnp.float32),
-            jax.ShapeDtypeStruct((4, GROUPS + 1), jnp.int32),
-        ],
-        compiler_params=params,
-        name="prep",
-    )(block_lists[:, 0, :], block_counts[:, 0], where, *rows_in)
-
-    stat, expo, tops = pl.pallas_call(
+    blk4 = shift_z(blk, 4)
+    near = other_core(own)
+    blk4, own1 = lax.optimization_barrier((blk4, own))
+    pair = jnp.concatenate([blk, blk4], 0)
+    up, down, two = shift_z(pair, 1), shift_z(pair, -1), shift_z(pair, 2)
+    left, right = shift_x(own1, 1), shift_x(own1, -1)
+    across = shift_x(own1, 2)
+    a, b = jnp.concatenate([up, down], 0), jnp.concatenate([pair, two], 0)
+    a_up, b_down = shift_y(a, 1), shift_y(b, -1)
+    b_up, a_down = shift_y(b, 1), shift_y(a, -1)
+    a_up, b_down, left, right, across, groups = lax.optimization_barrier((a_up, b_down, left, right, across, groups))
+    a_two, b_two = shift_y(a_up, 1), shift_y(b_down, -1)
+    rows_in = [own, left, right, across, near, other_core(left), other_core(right), other_core(across)]
+    camps = [a, b, a_up, a_down, b_up, b_down, a_two, b_two]
+
+    stat, cost, expo, tops = pl.pallas_call(
         stats_kernel,
-        in_specs=[SM] * 2 + [VM] * 9,
-        out_specs=[VM] * 3,
+        in_specs=[SM] * 2 + [pl.BlockSpec(memory_space=pl.ANY)] * 8 + [VM] * 8,
+        out_specs=[VM] * 4,
         out_shape=[
             OUT((NX * NC, 2 * TILES, BLOCK), jnp.float32),
+            OUT((TILES, BLOCK), jnp.float32),
             OUT((2 * GROUPS, BLOCK, BLOCK), jnp.float32),
             OUT((TRASH + 2, 8, BLOCK), jnp.float32),
         ],
         scratch_shapes=[
+            pltpu.VMEM((TILES * BLOCK, D), jnp.bfloat16),
+            pltpu.VMEM((NX * NC * PAD, D), jnp.bfloat16),
             pltpu.VMEM((OWN + 1, BLOCK, D), jnp.bfloat16),
             pltpu.VMEM((OWN + 1, BLOCK, BLOCK), jnp.float32),
             pltpu.VMEM((TRASH + 2, 8, BLOCK), jnp.float32),
+            pltpu.SemaphoreType.DMA((16,)),
         ],
         compiler_params=params,
         name="stats",
-    )(groups, where, rows, *pairs, *rests)
+    )(groups, where, *rows_in, *(pltpu.with_memory_space_constraint(v, pltpu.VMEM) for v in camps))
 
     stats = lax.all_to_all(stat, "camp", 0, 0)
 

time: 105 us -> 89.7 us (0.85)
  waiting for transfers between devices: 24.4 us -> 11.5 us
  local copies, waits for them, and re-layouts: 8.59 us -> 3.48 us
  Pallas kernels: 13 us -> 14.2 us
  starting transfers between devices: 26.2 us -> 27.3 us
    ppermute x6, waiting for transfers between devices: 15.9 us -> 6.27 us  [shift_y(): return lax.ppermute(v, 'imp', perm)]
    unnamed x25 -> x8, local copies, waits for them, and re-layouts: 7.22 us -> 2.06 us
    ppermute x4, waiting for transfers between devices: 7.47 us -> 2.59 us  [shift_z(): return lax.ppermute(v, 'imp', perm)]
    ppermute x3, waiting for transfers between devices: 0.01 us -> 1.12 us  [shift_x(): return lax.ppermute(v, 'camp', perm)]
    pallas_call x2, Pallas kernels: 10.4 us -> 11.5 us  [the longest x1 8.55 us: local(): pl.pallas_call(stats_kernel, in_specs=[SM] * 2 + [pl.BlockSpec(memory_spa...]
  transfers between devices with their start and end apart: 17 -> 17, of which waited for: 6 -> 9; matrix products, arithmetic and copies ran while one was open for 3% -> 4% of each run, Pallas kernels for 3% -> 3%
where the time goes in v3:
time: 89.7 us; the launch traced here: 88.8 us
  blocking collectives  27.5 us (31%)
  starting transfers between devices  27.3 us (30%)
  Pallas kernels  14.2 us (16%)
  waiting for transfers between devices  11.5 us (13%)
  other arithmetic  4.17 us (5%)
  local copies, waits for them, and re-layouts  3.48 us (4%)
    all_to_all x1, blocking collectives, local(): mine = jnp.sum(lax.all_to_all(spend, 'imp', 0, 0), axis=0)  16.3 us
    ppermute x4, starting transfers between devices, shift_z(): return lax.ppermute(v, 'imp', perm)  12.2 us
    all_to_all x1, blocking collectives, local(): stats = lax.all_to_all(stat, 'camp', 0, 0)  11.2 us
    ppermute x6, starting transfers between devices, shift_y(): return lax.ppermute(v, 'imp', perm)  8.89 us
    pallas_call x1, Pallas kernels, local(): pl.pallas_call(stats_kernel, in_specs=[SM] * 2 + [pl.BlockSpec(memory_spa...  8.55 us
    ppermute x6, waiting for transfers between devices, shift_y(): return lax.ppermute(v, 'imp', perm)  6.27 us
    ppermute x3, starting transfers between devices, shift_x(): return lax.ppermute(v, 'camp', perm)  5.65 us
    pallas_call x1, Pallas kernels, local(): pl.pallas_call(prep_kernel, in_specs=[SM] * 2, out_specs=SM, out_shape=ja...  2.92 us
  transfers between devices with their start and end apart: 17, of which 9 were waited for; matrix products, arithmetic and copies ran while one was open for 4% of the time, Pallas kernels for 3%

profile of v3, /device:TPU:8, one launch (start us, length us, event | category | flops | bytes accessed | tf_op | source)
XLA Modules:
  0.0 88.8 jit_solution(5914001576793432600)
XLA Ops:
  0.6 0.7 pad.8
  1.4 0.8 pad_maximum_fusion.2
  2.2 7.2 %collective-permute-start = (bf16[144,256]{1,0:T(8,128)(2,1)S(1)}, bf16[144,256]{1,0:T(8,128)(2,1)S(1)}, u32[]{:S(2)}, u32[]{:S(2)}) collective-permute-start(bf16[144,256]{1,0:T(8,128)(2,1)S(1)} %pad_maximum_fusion.2), channel_id=1, source_target_pairs={{0,128},{8,136},{16,144},{24,152},{32,160},{40,168},{48,176},{56,1... | collective-permute-start | bytes 221192 | tf_op jit(solution)/shard_map/ppermute | solution.py:33
  9.4 0.7 reshape.16
  10.1 1.0 %fusion.1.refs_0_ = bf16[528,256]{1,0:T(8,128)(2,1)S(1)} fusion(bf16[2,256]{1,0:T(2,128)(2,1)S(1)} %reshape.16, bf16[512,256]{1,0:T(8,128)(2,1)} %param.7), kind=kLoop, calls=%fused_computation.3 | loop fusion | flops 811008 | bytes 533504 | tf_op jit(solution)/shard_map/concatenate | solution.py:191
  11.1 1.1 %collective-permute-done = bf16[144,256]{1,0:T(8,128)(2,1)S(1)} collective-permute-done((bf16[144,256]{1,0:T(8,128)(2,1)S(1)}, bf16[144,256]{1,0:T(8,128)(2,1)S(1)}, u32[]{:S(2)}, u32[]{:S(2)}) %collective-permute-start) | collective-permute-done | bytes 73760 | tf_op jit(solution)/shard_map/ppermute | solution.py:33
  12.2 0.8 pad_maximum_fusion.1
  13.0 1.8 %collective-permute-start.1 = (bf16[288,256]{1,0:T(8,128)(2,1)S(1)}, bf16[288,256]{1,0:T(8,128)(2,1)S(1)}, u32[]{:S(2)}, u32[]{:S(2)}) collective-permute-start(bf16[288,256]{1,0:T(8,128)(2,1)S(1)} %pad_maximum_fusion.1), channel_id=1, source_target_pairs={{0,32},{8,40},{16,48},{24,56},{32,64},{40,72},{48,80},{56,88},{64,... | collective-permute-start | bytes 442376 | tf_op jit(solution)/shard_map/ppermute | solution.py:33
  14.8 2.7 %collective-permute-start.2 = (bf16[288,256]{1,0:T(8,128)(2,1)S(1)}, bf16[288,256]{1,0:T(8,128)(2,1)S(1)}, u32[]{:S(2)}, u32[]{:S(2)}) collective-permute-start(bf16[288,256]{1,0:T(8,128)(2,1)S(1)} %pad_maximum_fusion.1), channel_id=1, source_target_pairs={{0,224},{8,232},{16,240},{24,248},{32,0},{40,8},{48,16},{56,24},{6... | collective-permute-start | bytes 442376 | tf_op jit(solution)/shard_map/ppermute | solution.py:33
  17.6 0.5 collective-permute-start.4
  18.0 3.0 %collective-permute-start.8 = (bf16[528,256]{1,0:T(8,128)(2,1)S(1)}, bf16[528,256]{1,0:T(8,128)(2,1)S(1)}, u32[]{:S(2)}, u32[]{:S(2)}) collective-permute-start(bf16[528,256]{1,0:T(8,128)(2,1)S(1)} %fusion.1.refs_0_), channel_id=1, source_target_pairs={{0,4},{1,5},{2,6},{3,7},{4,0},{5,1},{6,2},{7,3},{8,12},{9,13},{10,... | collective-permute-start | bytes 811016 | tf_op jit(solution)/shard_map/ppermute | solution.py:43
  21.1 1.1 %collective-permute-start.7 = (bf16[528,256]{1,0:T(8,128)(2,1)S(1)}, bf16[528,256]{1,0:T(8,128)(2,1)S(1)}, u32[]{:S(2)}, u32[]{:S(2)}) collective-permute-start(bf16[528,256]{1,0:T(8,128)(2,1)S(1)} %fusion.1.refs_0_), channel_id=1, source_target_pairs={{0,6},{1,7},{2,0},{3,1},{4,2},{5,3},{6,4},{7,5},{8,14},{9,15},{10,... | collective-permute-start | bytes 811016 | tf_op jit(solution)/shard_map/ppermute | solution.py:43
  22.2 0.7 collective-permute-done.1
  22.9 1.5 %collective-permute-start.6 = (bf16[528,256]{1,0:T(8,128)(2,1)S(1)}, bf16[528,256]{1,0:T(8,128)(2,1)S(1)}, u32[]{:S(2)}, u32[]{:S(2)}) collective-permute-start(bf16[528,256]{1,0:T(8,128)(2,1)S(1)} %fusion.1.refs_0_), channel_id=1, source_target_pairs={{0,2},{1,3},{2,4},{3,5},{4,6},{5,7},{6,0},{7,1},{8,10},{9,11},{10,... | collective-permute-start | bytes 811016 | tf_op jit(solution)/shard_map/ppermute | solution.py:43
  24.4 0.0 collective-permute-done.2
  24.5 1.7 %collective-permute-start.3 = (bf16[576,256]{1,0:T(8,128)(2,1)S(1)}, bf16[576,256]{1,0:T(8,128)(2,1)S(1)}, u32[]{:S(2)}, u32[]{:S(2)}) collective-permute-start(bf16[576,256]{1,0:T(8,128)(2,1)S(1)} %constant_dynamic-update-slice_fusion.refs_8_), channel_id=1, source_target_pairs={{0,8},{8,16},{16,24},{24,0},{32,40},{40,48},{48,56},{56,32},{64,72... | collective-permute-start | bytes 884744 | tf_op jit(solution)/shard_map/ppermute | solution.py:38
  26.1 0.8 collective-permute-done.4
  26.9 0.9 pad_maximum_fusion.refs_9_
  27.7 0.9 %collective-permute-start.5 = (bf16[576,256]{1,0:T(8,128)(2,1)S(1)}, bf16[576,256]{1,0:T(8,128)(2,1)S(1)}, u32[]{:S(2)}, u32[]{:S(2)}) collective-permute-start(bf16[576,256]{1,0:T(8,128)(2,1)S(1)} %pad_maximum_fusion.refs_9_), channel_id=1, source_target_pairs={{0,24},{8,0},{16,8},{24,16},{32,56},{40,32},{48,40},{56,48},{64,88... | collective-permute-start | bytes 884744 | tf_op jit(solution)/shard_map/ppermute | solution.py:38
  28.7 0.0 collective-permute-done.8.refs_3_
  28.7 2.6 %collective-permute-start.13 = (bf16[576,256]{1,0:T(8,128)(2,1)S(1)}, bf16[576,256]{1,0:T(8,128)(2,1)S(1)}, u32[]{:S(2)}, u32[]{:S(2)}) collective-permute-start(bf16[576,256]{1,0:T(8,128)(2,1)S(1)} %constant_dynamic-update-slice_fusion.refs_8_), channel_id=1, source_target_pairs={{0,24},{8,0},{16,8},{24,16},{32,56},{40,32},{48,40},{56,48},{64,88... | collective-permute-start | bytes 884744 | tf_op jit(solution)/shard_map/ppermute | solution.py:38
  31.3 1.1 %collective-permute-done.7.refs_2_ = bf16[528,256]{1,0:T(8,128)(2,1)S(1)} collective-permute-done((bf16[528,256]{1,0:T(8,128)(2,1)S(1)}, bf16[528,256]{1,0:T(8,128)(2,1)S(1)}, u32[]{:S(2)}, u32[]{:S(2)}) %collective-permute-start.7) | collective-permute-done | bytes 270368 | tf_op jit(solution)/shard_map/ppermute | solution.py:43
  32.4 1.6 %collective-permute-start.14 = (bf16[576,256]{1,0:T(8,128)(2,1)S(1)}, bf16[576,256]{1,0:T(8,128)(2,1)S(1)}, u32[]{:S(2)}, u32[]{:S(2)}) collective-permute-start(bf16[576,256]{1,0:T(8,128)(2,1)S(1)} %pad_maximum_fusion.refs_9_), channel_id=1, source_target_pairs={{0,8},{8,16},{16,24},{24,0},{32,40},{40,48},{48,56},{56,32},{64,72... | collective-permute-start | bytes 884744 | tf_op jit(solution)/shard_map/ppermute | solution.py:38
  34.0 0.0 collective-permute-done.6.refs_1_
  34.0 0.0 collective-permute-start.9
  34.0 1.4 %copy.10 = s32[32,1,8]{2,0,1:T(8,128)} copy(s32[32,1,8]{0,2,1:T(8,128)} %param.12) | data formatting | bytes 2048 | tf_op args[5]
  35.4 2.9 %prep.1.groups = s32[4,133]{1,0:T(4,128)} custom-call(s32[32,8]{1,0:T(8,128)} %bitcast.12, s32[32]{0:T(128)} %bitcast.14), custom_call_target="tpu_custom_call" | custom-call | tf_op jit(solution)/shard_map/prep/pallas_call | solution.py:182
  38.3 0.0 collective-permute-done.3.refs_10_
  38.3 0.0 collective-permute-done.5.refs_13_
  38.3 1.3 %collective-permute-start.15 = (bf16[576,256]{1,0:T(8,128)(2,1)S(1)}, bf16[576,256]{1,0:T(8,128)(2,1)S(1)}, u32[]{:S(2)}, u32[]{:S(2)}) collective-permute-start(bf16[576,256]{1,0:T(8,128)(2,1)S(1)} %collective-permute-done.3.refs_10_), channel_id=1, source_target_pairs={{0,8},{8,16},{16,24},{24,0},{32,40},{40,48},{48,56},{56,32},{64,72... | collective-permute-start | bytes 884744 | tf_op jit(solution)/shard_map/ppermute | solution.py:38
  39.6 0.8 collective-permute-start.16
  40.4 0.0 collective-permute-done.9.refs_4_
  40.4 0.0 collective-permute-start.10
  40.4 1.9 %collective-permute-done.13.refs_11_ = bf16[576,256]{1,0:T(8,128)(2,1)S(1)} collective-permute-done((bf16[576,256]{1,0:T(8,128)(2,1)S(1)}, bf16[576,256]{1,0:T(8,128)(2,1)S(1)}, u32[]{:S(2)}, u32[]{:S(2)}) %collective-permute-start.13) | collective-permute-done | bytes 294944 | tf_op jit(solution)/shard_map/ppermute | solution.py:38
  42.3 0.0 collective-permute-start.11
  42.3 0.5 collective-permute-start.12
  42.8 0.1 pad_add_fusion.where
  42.9 1.1 %collective-permute-done.11.refs_6_ = bf16[528,256]{1,0:T(8,128)(2,1)} collective-permute-done((bf16[528,256]{1,0:T(8,128)(2,1)S(1)}, bf16[528,256]{1,0:T(8,128)(2,1)}, u32[]{:S(2)}, u32[]{:S(2)}) %collective-permute-start.11) | collective-permute-done | bytes 270368 | tf_op jit(solution)/shard_map/ppermute | solution.py:48
  44.0 0.4 collective-permute-done.12.refs_7_
  44.4 3.3 %collective-permute-done.15.refs_14_ = bf16[576,256]{1,0:T(8,128)(2,1)S(1)} collective-permute-done((bf16[576,256]{1,0:T(8,128)(2,1)S(1)}, bf16[576,256]{1,0:T(8,128)(2,1)S(1)}, u32[]{:S(2)}, u32[]{:S(2)}) %collective-permute-start.15) | collective-permute-done | bytes 294944 | tf_op jit(solution)/shard_map/ppermute | solution.py:38
  47.7 1.1 %collective-permute-done.16.refs_15_ = bf16[576,256]{1,0:T(8,128)(2,1)S(1)} collective-permute-done((bf16[576,256]{1,0:T(8,128)(2,1)S(1)}, bf16[576,256]{1,0:T(8,128)(2,1)S(1)}, u32[]{:S(2)}, u32[]{:S(2)}) %collective-permute-start.16) | collective-permute-done | bytes 294944 | tf_op jit(solution)/shard_map/ppermute | solution.py:38
  48.8 0.7 copy-done
  49.4 8.5 %stats.1 = (f32[8,64,128]{2,1,0:T(8,128)S(1)}, f32[32,128]{1,0:T(8,128)S(1)}, f32[264,128,128]{2,1,0:T(8,128)S(1)}, f32[258,8,128]{2,1,0:T(8,128)S(1)}) custom-call(s32[4,133]{1,0:T(4,128)S(1)} %copy-done, s32[4]{0:T(128)S(1)} %pad_add_fusion.where, bf16[528,256]{1,0:T(8,128)(2,1)S(1)} %fusion.1.refs_0_, ...), custom_call_target="tpu_custom_call" | custom-call | tf_op jit(solution)/shard_map/stats/pallas_call | solution.py:207
  58.0 11.2 %all_to_all.14.stats = f32[8,64,128]{2,1,0:T(8,128)S(1)} all-to-all(f32[8,64,128]{2,1,0:T(8,128)S(1)} %get-tuple-element.24), channel_id=1, replica_groups=mesh['imp'=32,'camp'=8] {'camp'}, dimensions={0} | all-to-all | bytes 524288 | tf_op jit(solution)/shard_map/all_to_all | solution.py:229
  69.2 2.7 %spend.1 = (f32[32,128]{1,0:T(8,128)S(1)}, f32[32,128]{1,0:T(8,128)}) custom-call(s32[4,133]{1,0:T(4,128)S(1)} %copy-done, f32[8,64,128]{2,1,0:T(8,128)S(1)} %all_to_all.14.stats, f32[32,128]{1,0:T(8,128)S(1)} %get-tuple-element.25.cost, f32[264,128,128]{2,1,0:T(8,128)S(1)} %get-tuple-element.26.expo, f32[258,8,128]{2,1,0:T(8,128)S(1)} %get-tuple-element.27.tops), custom_call_target="tpu_custom_call" | custom-call | tf_op jit(solution)/shard_map/spend/pallas_call | solution.py:231
  71.9 16.3 %all_to_all.15 = f32[32,1,128]{2,1,0:T(1,128)S(1)} all-to-all(f32[32,1,128]{2,1,0:T(1,128)S(1)} %bitcast.11), channel_id=1, replica_groups=mesh['imp'=32,'camp'=8] {'imp'}, dimensions={0} | all-to-all | bytes 32768 | tf_op jit(solution)/shard_map/all_to_all | solution.py:247
  88.3 0.1 reduce_sum.9
  88.3 0.5 divide_add_fusion
  (9 shorter events, 0.0 us)
Async XLA Ops:
  0.6 87.7 %copy-start.1 = (bf16[128]{0:T(256)(128)(2,1)S(1)}, bf16[128]{0:T(256)(128)(2,1)}, u32[]{:S(2)}) copy-start(bf16[128]{0:T(256)(128)(2,1)} %param.10) | copy-start | bytes 772
  0.6 87.7 %copy-start.2 = (f32[128]{0:T(128)S(1)}, f32[128]{0:T(128)}, u32[]{:S(2)}) copy-start(f32[128]{0:T(128)} %param.11) | copy-start | bytes 1540
  2.2 9.9 %collective-permute-start = (bf16[144,256]{1,0:T(8,128)(2,1)S(1)}, bf16[144,256]{1,0:T(8,128)(2,1)S(1)}, u32[]{:S(2)}, u32[]{:S(2)}) collective-permute-start(bf16[144,256]{1,0:T(8,128)(2,1)S(1)} %pad_maximum_fusion.2), channel_id=1, source_target_pairs={{0,128},{8,136},{16,144},{24,152},{32,160},{40,168},{48,176},{56,1... | collective-permute-start | bytes 221192 | tf_op jit(solution)/shard_map/ppermute | solution.py:33
  13.0 9.9 %collective-permute-start.1 = (bf16[288,256]{1,0:T(8,128)(2,1)S(1)}, bf16[288,256]{1,0:T(8,128)(2,1)S(1)}, u32[]{:S(2)}, u32[]{:S(2)}) collective-permute-start(bf16[288,256]{1,0:T(8,128)(2,1)S(1)} %pad_maximum_fusion.1), channel_id=1, source_target_pairs={{0,32},{8,40},{16,48},{24,56},{32,64},{40,72},{48,80},{56,88},{64,... | collective-permute-start | bytes 442376 | tf_op jit(solution)/shard_map/ppermute | solution.py:33
  14.8 9.6 %collective-permute-start.2 = (bf16[288,256]{1,0:T(8,128)(2,1)S(1)}, bf16[288,256]{1,0:T(8,128)(2,1)S(1)}, u32[]{:S(2)}, u32[]{:S(2)}) collective-permute-start(bf16[288,256]{1,0:T(8,128)(2,1)S(1)} %pad_maximum_fusion.1), channel_id=1, source_target_pairs={{0,224},{8,232},{16,240},{24,248},{32,0},{40,8},{48,16},{56,24},{6... | collective-permute-start | bytes 442376 | tf_op jit(solution)/shard_map/ppermute | solution.py:33
  17.6 9.3 %collective-permute-start.4 = (bf16[288,256]{1,0:T(8,128)(2,1)S(1)}, bf16[288,256]{1,0:T(8,128)(2,1)S(1)}, u32[]{:S(2)}, u32[]{:S(2)}) collective-permute-start(bf16[288,256]{1,0:T(8,128)(2,1)S(1)} %pad_maximum_fusion.1), channel_id=1, source_target_pairs={{0,64},{8,72},{16,80},{24,88},{32,96},{40,104},{48,112},{56,120},{... | collective-permute-start | bytes 442376 | tf_op jit(solution)/shard_map/ppermute | solution.py:33
  18.0 10.7 %collective-permute-start.8 = (bf16[528,256]{1,0:T(8,128)(2,1)S(1)}, bf16[528,256]{1,0:T(8,128)(2,1)S(1)}, u32[]{:S(2)}, u32[]{:S(2)}) collective-permute-start(bf16[528,256]{1,0:T(8,128)(2,1)S(1)} %fusion.1.refs_0_), channel_id=1, source_target_pairs={{0,4},{1,5},{2,6},{3,7},{4,0},{5,1},{6,2},{7,3},{8,12},{9,13},{10,... | collective-permute-start | bytes 811016 | tf_op jit(solution)/shard_map/ppermute | solution.py:43
  21.1 11.3 %collective-permute-start.7 = (bf16[528,256]{1,0:T(8,128)(2,1)S(1)}, bf16[528,256]{1,0:T(8,128)(2,1)S(1)}, u32[]{:S(2)}, u32[]{:S(2)}) collective-permute-start(bf16[528,256]{1,0:T(8,128)(2,1)S(1)} %fusion.1.refs_0_), channel_id=1, source_target_pairs={{0,6},{1,7},{2,0},{3,1},{4,2},{5,3},{6,4},{7,5},{8,14},{9,15},{10,... | collective-permute-start | bytes 811016 | tf_op jit(solution)/shard_map/ppermute | solution.py:43
  22.9 11.1 %collective-permute-start.6 = (bf16[528,256]{1,0:T(8,128)(2,1)S(1)}, bf16[528,256]{1,0:T(8,128)(2,1)S(1)}, u32[]{:S(2)}, u32[]{:S(2)}) collective-permute-start(bf16[528,256]{1,0:T(8,128)(2,1)S(1)} %fusion.1.refs_0_), channel_id=1, source_target_pairs={{0,2},{1,3},{2,4},{3,5},{4,6},{5,7},{6,0},{7,1},{8,10},{9,11},{10,... | collective-permute-start | bytes 811016 | tf_op jit(solution)/shard_map/ppermute | solution.py:43
  24.5 13.8 %collective-permute-start.3 = (bf16[576,256]{1,0:T(8,128)(2,1)S(1)}, bf16[576,256]{1,0:T(8,128)(2,1)S(1)}, u32[]{:S(2)}, u32[]{:S(2)}) collective-permute-start(bf16[576,256]{1,0:T(8,128)(2,1)S(1)} %constant_dynamic-update-slice_fusion.refs_8_), channel_id=1, source_target_pairs={{0,8},{8,16},{16,24},{24,0},{32,40},{40,48},{48,56},{56,32},{64,72... | collective-permute-start | bytes 884744 | tf_op jit(solution)/shard_map/ppermute | solution.py:38
  27.7 10.5 %collective-permute-start.5 = (bf16[576,256]{1,0:T(8,128)(2,1)S(1)}, bf16[576,256]{1,0:T(8,128)(2,1)S(1)}, u32[]{:S(2)}, u32[]{:S(2)}) collective-permute-start(bf16[576,256]{1,0:T(8,128)(2,1)S(1)} %pad_maximum_fusion.refs_9_), channel_id=1, source_target_pairs={{0,24},{8,0},{16,8},{24,16},{32,56},{40,32},{48,40},{56,48},{64,88... | collective-permute-start | bytes 884744 | tf_op jit(solution)/shard_map/ppermute | solution.py:38
  28.7 13.6 %collective-permute-start.13 = (bf16[576,256]{1,0:T(8,128)(2,1)S(1)}, bf16[576,256]{1,0:T(8,128)(2,1)S(1)}, u32[]{:S(2)}, u32[]{:S(2)}) collective-permute-start(bf16[576,256]{1,0:T(8,128)(2,1)S(1)} %constant_dynamic-update-slice_fusion.refs_8_), channel_id=1, source_target_pairs={{0,24},{8,0},{16,8},{24,16},{32,56},{40,32},{48,40},{56,48},{64,88... | collective-permute-start | bytes 884744 | tf_op jit(solution)/shard_map/ppermute | solution.py:38
  32.4 9.9 %collective-permute-start.14 = (bf16[576,256]{1,0:T(8,128)(2,1)S(1)}, bf16[576,256]{1,0:T(8,128)(2,1)S(1)}, u32[]{:S(2)}, u32[]{:S(2)}) collective-permute-start(bf16[576,256]{1,0:T(8,128)(2,1)S(1)} %pad_maximum_fusion.refs_9_), channel_id=1, source_target_pairs={{0,8},{8,16},{16,24},{24,0},{32,40},{40,48},{48,56},{56,32},{64,72... | collective-permute-start | bytes 884744 | tf_op jit(solution)/shard_map/ppermute | solution.py:38
  34.0 6.4 %collective-permute-start.9 = (bf16[528,256]{1,0:T(8,128)(2,1)S(1)}, bf16[528,256]{1,0:T(8,128)(2,1)}, u32[]{:S(2)}, u32[]{:S(2)}) collective-permute-start(bf16[528,256]{1,0:T(8,128)(2,1)S(1)} %fusion.1.refs_0_), channel_id=1, source_target_pairs={{0,1},{1,0},{2,3},{3,2},{4,5},{5,4},{6,7},{7,6},{8,9},{9,8},{10,11... | collective-permute-start | bytes 811016 | tf_op jit(solution)/shard_map/ppermute | solution.py:48
  38.3 9.4 %collective-permute-start.15 = (bf16[576,256]{1,0:T(8,128)(2,1)S(1)}, bf16[576,256]{1,0:T(8,128)(2,1)S(1)}, u32[]{:S(2)}, u32[]{:S(2)}) collective-permute-start(bf16[576,256]{1,0:T(8,128)(2,1)S(1)} %collective-permute-done.3.refs_10_), channel_id=1, source_target_pairs={{0,8},{8,16},{16,24},{24,0},{32,40},{40,48},{48,56},{56,32},{64,72... | collective-permute-start | bytes 884744 | tf_op jit(solution)/shard_map/ppermute | solution.py:38
  39.6 9.2 %collective-permute-start.16 = (bf16[576,256]{1,0:T(8,128)(2,1)S(1)}, bf16[576,256]{1,0:T(8,128)(2,1)S(1)}, u32[]{:S(2)}, u32[]{:S(2)}) collective-permute-start(bf16[576,256]{1,0:T(8,128)(2,1)S(1)} %collective-permute-done.5.refs_13_), channel_id=1, source_target_pairs={{0,24},{8,0},{16,8},{24,16},{32,56},{40,32},{48,40},{56,48},{64,88... | collective-permute-start | bytes 884744 | tf_op jit(solution)/shard_map/ppermute | solution.py:38
  40.4 2.5 %collective-permute-start.10 = (bf16[528,256]{1,0:T(8,128)(2,1)S(1)}, bf16[528,256]{1,0:T(8,128)(2,1)}, u32[]{:S(2)}, u32[]{:S(2)}) collective-permute-start(bf16[528,256]{1,0:T(8,128)(2,1)S(1)} %collective-permute-done.6.refs_1_), channel_id=1, source_target_pairs={{0,1},{1,0},{2,3},{3,2},{4,5},{5,4},{6,7},{7,6},{8,9},{9,8},{10,11... | collective-permute-start | bytes 811016 | tf_op jit(solution)/shard_map/ppermute | solution.py:48
  42.3 1.7 %collective-permute-start.11 = (bf16[528,256]{1,0:T(8,128)(2,1)S(1)}, bf16[528,256]{1,0:T(8,128)(2,1)}, u32[]{:S(2)}, u32[]{:S(2)}) collective-permute-start(bf16[528,256]{1,0:T(8,128)(2,1)S(1)} %collective-permute-done.7.refs_2_), channel_id=1, source_target_pairs={{0,1},{1,0},{2,3},{3,2},{4,5},{5,4},{6,7},{7,6},{8,9},{9,8},{10,11... | collective-permute-start | bytes 811016 | tf_op jit(solution)/shard_map/ppermute | solution.py:48
  42.3 2.1 %collective-permute-start.12 = (bf16[528,256]{1,0:T(8,128)(2,1)S(1)}, bf16[528,256]{1,0:T(8,128)(2,1)}, u32[]{:S(2)}, u32[]{:S(2)}) collective-permute-start(bf16[528,256]{1,0:T(8,128)(2,1)S(1)} %collective-permute-done.8.refs_3_), channel_id=1, source_target_pairs={{0,1},{1,0},{2,3},{3,2},{4,5},{5,4},{6,7},{7,6},{8,9},{9,8},{10,11... | collective-permute-start | bytes 811016 | tf_op jit(solution)/shard_map/ppermute | solution.py:48
  48.8 0.7 copy-start

commit v4 on v3

v4 whole, which is shorter than its diff:
```python
import functools
import math

import jax
import jax.numpy as jnp
from jax import lax
from jax.experimental import pallas as pl
from jax.experimental.pallas import tpu as pltpu
from jax.sharding import PartitionSpec as P

D = 256
BLOCK = 128
SLOTS = 8
NZ, NY, NX, NC = 8, 4, 4, 2
OWN = NZ * NY
TILES = 32
DEAD = OWN
PAD = 16
CBLK = BLOCK + PAD
LOG2E = math.log2(math.e)
LN2 = math.log(2.0)
SCALE2 = 3.0 / math.sqrt(D) * LOG2E
VMEM_LIMIT = 16 * 1024 * 1024
UNROLL = 4
GROUPS = TILES * SLOTS // 2 + UNROLL
LAST = GROUPS
FIRST, SECOND = 1024, 1024 * 64
TRASH = TILES * SLOTS
LOWEST = -3e38


def shift_z(v, k):
    perm = [(z * NY + y, (z + k) % NZ * NY + y) for z in range(NZ) for y in range(NY)]
    return lax.ppermute(v, "imp", perm)


def shift_y(v, k):
    perm = [(z * NY + y, z * NY + (y + k) % NY) for z in range(NZ) for y in range(NY)]
    return lax.ppermute(v, "imp", perm)


def shift_x(v, k):
    perm = [(x * NC + c, (x + k) % NX * NC + c) for x in range(NX) for c in range(NC)]
    return lax.ppermute(v, "camp", perm)


def other_core(v):
    perm = [(x * NC + c, x * NC + 1 - c) for x in range(NX) for c in range(NC)]
    return lax.ppermute(v, "camp", perm)


NEAR, FAR = (7, 3, 1, 5), (0, 4, 6, 2)
LAYOUT = ((0, NEAR), (0, FAR), (3, NEAR), (1, NEAR), (3, FAR), (1, FAR), (2, NEAR), (2, FAR))
DX = (0, 3, 1, 2)


def fold(v):
    return v.reshape(v.shape[0] // 8, 8, v.shape[1])


def prep_kernel(lists, counts, groups):
    def tile(t, at):
        count = counts[t]
        for j in range(SLOTS // 2):
            second = jnp.where(2 * j + 1 < count, lists[2 * j + 1, t], DEAD)
            groups[at] = t * SLOTS + 2 * j + lists[2 * j, t] * FIRST + second * SECOND
            at = at + (2 * j < count).astype(jnp.int32)
        return at

    end = lax.fori_loop(0, TILES, tile, 0)
    for j in range(UNROLL):
        groups[end + j] = TRASH + DEAD * FIRST + DEAD * SECOND
    groups[LAST] = (end + UNROLL - 1) // UNROLL


def unpack(group):
    slot = group & (FIRST - 1)
    return slot, (slot >> 3) & (TILES - 1), ((group >> 10) & 63, group >> 16)


def stats_kernel(groups, where, *refs):
    rows_in, camps, cost = refs[:8], refs[8:16], refs[16]
    stat, expo, tops, rows, tab, pb, totals, sems = refs[17:]
    z, y, x, core = where[0], where[1], where[2], where[3]
    copies = []
    for k in range(8):
        q = lax.rem(x + DX[k % 4], NX) * NC + (core if k < 4 else 1 - core)
        whole = rows.at[pl.ds(pl.multiple_of(q * 512, 512), 512), :]
        copies.append(pltpu.make_async_copy(rows_in[k], whole, sems.at[k]))
    for copy in copies:
        copy.start()
    eye = lax.broadcasted_iota(jnp.int32, (BLOCK, BLOCK), 0) == lax.broadcasted_iota(jnp.int32, (BLOCK, BLOCK), 1)
    ones = jnp.ones((BLOCK, BLOCK), jnp.bfloat16)
    for buf, (dy, offsets) in zip(camps, LAYOUT):
        for i, dz in enumerate(offsets):
            b = lax.rem(z + dz, NZ) * NY + lax.rem(y + dy, NY)
            tab[b] = buf[i * CBLK : i * CBLK + BLOCK, :]
            row = buf[i * CBLK + BLOCK : (i + 1) * CBLK, :][0:1, 0:BLOCK].astype(jnp.float32)
            diag = jnp.where(eye, jnp.broadcast_to(row, (BLOCK, BLOCK)), 0.0).astype(jnp.bfloat16)
            pb[b] = jnp.dot(diag, ones, preferred_element_type=jnp.float32) * LOG2E
    tab[DEAD] = jnp.zeros((BLOCK, D), jnp.bfloat16)
    pb[DEAD] = jnp.full((BLOCK, BLOCK), -LOWEST, jnp.float32)
    for p in range(TILES * SLOTS):
        tops[p] = jnp.full((8, BLOCK), LOWEST, jnp.float32)
        totals[p] = jnp.zeros((8, BLOCK), jnp.float32)
    for copy in copies:
        copy.wait()
    for q in range(NX * NC):
        stat[q, 2 * TILES :, :] = jnp.concatenate([cost[...], jnp.zeros((4, BLOCK), jnp.float32)], 0)

    def step(i, carry):
        for u in range(UNROLL):
            g = i * UNROLL + u
            slot, t, blocks = unpack(groups[g])
            rows_t = rows[pl.ds(pl.multiple_of(t * BLOCK, BLOCK), BLOCK), :]
            for k in range(2):
                b = blocks[k]
                raw = lax.dot_general(tab[b], rows_t, (((1,), (1,)), ((), ())), preferred_element_type=jnp.float32)
                logit = fold(raw * SCALE2 - pb[b])
                top = jnp.max(logit, axis=0)
                e = jnp.exp2(logit - top[None])
                expo[2 * g + k] = e.reshape(BLOCK, BLOCK)
                tops[slot + k] = top
                totals[slot + k] = jnp.sum(e, axis=0)
        return carry

    lax.fori_loop(0, groups[LAST], step, 0)

    for t in range(TILES):
        top_s = [tops[t * SLOTS + s] for s in range(SLOTS)]
        top8 = functools.reduce(jnp.maximum, top_s)
        top = jnp.max(top8, axis=0, keepdims=True)
        total8 = sum(totals[t * SLOTS + s] * jnp.exp2(top_s[s] - top) for s in range(SLOTS))
        total = jnp.sum(total8, axis=0, keepdims=True)
        for c in range(NX * NC):
            stat[c, t : t + 1, :] = top
            stat[c, TILES + t : TILES + t + 1, :] = total


def spend_kernel(groups, stats, expo, tops, spend, logz, acc, topw):
    owners = NX * NC
    top = functools.reduce(jnp.maximum, [stats[c, 0:TILES, :] for c in range(owners)])
    total = sum(stats[c, TILES : 2 * TILES, :] * jnp.exp2(stats[c, 0:TILES, :] - top) for c in range(owners))
    logz[...] = (top + jnp.log2(total)) * LN2
    topw[0:TILES, :] = top
    cost = jnp.concatenate([stats[c, 2 * TILES : 2 * TILES + 4, :] for c in range(owners)], 0)
    topw[TILES:, :] = cost / total
    for b in range(OWN):
        acc[b] = jnp.zeros((BLOCK, BLOCK), jnp.float32)

    def step(i, carry):
        for u in range(UNROLL):
            g = i * UNROLL + u
            slot, t, blocks = unpack(groups[g])
            top_t = topw[pl.ds(t, 1), :]
            w_t = topw[pl.ds(TILES + t, 1), :]
            for k in range(2):
                factor = jnp.exp2(tops[slot + k] - top_t) * w_t
                b = blocks[k]
                part = fold(expo[2 * g + k]) * factor[None]
                acc[b] = acc[b] + part.reshape(BLOCK, BLOCK)
        return carry

    lax.fori_loop(0, groups[LAST], step, 0)
    for b in range(OWN):
        spend[b : b + 1, :] = jnp.sum(acc[b].T, axis=0, keepdims=True)


VM = pl.BlockSpec(memory_space=pltpu.VMEM)
SM = pl.BlockSpec(memory_space=pltpu.SMEM)
OUT = pltpu.VMEM
GOUT = pltpu.SMEM


def local(imp_emb, imp_cost, camp_emb, prices, spend_limits, block_lists, block_counts):
    imp, camp = lax.axis_index("imp"), lax.axis_index("camp")
    where = jnp.stack([imp // NY, imp % NY, camp // NC, camp % NC]).astype(jnp.int32)

    params = pltpu.CompilerParams(vmem_limit_bytes=VMEM_LIMIT)
    groups = pl.pallas_call(
        prep_kernel,
        in_specs=[SM] * 2,
        out_specs=SM,
        out_shape=GOUT((GROUPS + 1,), jnp.int32),
        name="prep",
    )(block_lists[:, 0, :].T, block_counts[:, 0])

    blk = jnp.concatenate([camp_emb, jnp.pad(prices.reshape(1, BLOCK), ((0, PAD - 1), (0, D - BLOCK)))], 0)
    cost = imp_cost.reshape(4, BLOCK).astype(jnp.float32)
    blk4, plus, minus = shift_z(blk, 4), shift_z(blk, 2), shift_z(blk, -2)
    near = other_core(imp_emb)
    bar = lax.optimization_barrier
    blk4, emb, blk = bar((blk4, imp_emb, blk))
    pair = jnp.concatenate([blk, blk4], 0)
    up, down = shift_z(pair, 1), shift_z(pair, -1)
    b = jnp.concatenate([blk, blk4, plus, minus], 0)
    b_up, b_down = shift_y(b, 1), shift_y(b, -1)
    left, right, across = shift_x(emb, 1), shift_x(emb, -1), shift_x(emb, 2)
    a = jnp.concatenate([up, down], 0)
    a_up, a_down = shift_y(a, 1), shift_y(a, -1)
    b_down, left = bar((b_down, left))
    b_two = shift_y(b_down, -1)
    a_up, left, right, groups, cost = bar((a_up, left, right, groups, cost))
    a_two = shift_y(a_up, 1)
    oleft, oright = other_core(left), other_core(right)
    rows_in = [pltpu.with_memory_space_constraint(imp_emb, pltpu.HBM), left, right, across, near, oleft, oright, other_core(across)]
    camps = [a, b, a_up, a_down, b_up, b_down, a_two, b_two]

    stat, expo, tops = pl.pallas_call(
        stats_kernel,
        in_specs=[SM] * 2 + [pl.BlockSpec(memory_space=pl.ANY)] * 8 + [VM] * 9,
        out_specs=[VM] * 3,
        out_shape=[
            OUT((NX * NC, 2 * TILES + 8, BLOCK), jnp.float32),
            OUT((2 * GROUPS, BLOCK, BLOCK), jnp.float32),
            OUT((TRASH + 2, 8, BLOCK), jnp.float32),
        ],
        scratch_shapes=[
            pltpu.VMEM((TILES * BLOCK, D), jnp.bfloat16),
            pltpu.VMEM((OWN + 1, BLOCK, D), jnp.bfloat16),
            pltpu.VMEM((OWN + 1, BLOCK, BLOCK), jnp.float32),
            pltpu.VMEM((TRASH + 2, 8, BLOCK), jnp.float32),
            pltpu.SemaphoreType.DMA((8,)),
        ],
        compiler_params=params,
        name="stats",
    )(groups, where, *rows_in, *(pltpu.with_memory_space_constraint(v, pltpu.VMEM) for v in camps), cost)

    stats = lax.all_to_all(stat, "camp", 0, 0)

    spend, logz = pl.pallas_call(
        spend_kernel,
        in_specs=[SM] + [VM] * 3,
        out_specs=[VM] * 2,
        out_shape=[
            OUT((OWN, BLOCK), jnp.float32),
            jax.ShapeDtypeStruct((TILES, BLOCK), jnp.float32),
        ],
        scratch_shapes=[
            pltpu.VMEM((OWN + 1, BLOCK, BLOCK), jnp.float32),
            pltpu.VMEM((2 * TILES, BLOCK), jnp.float32),
        ],
        compiler_params=params,
        name="spend",
    )(groups, stats, expo, tops)

    mine = jnp.sum(lax.all_to_all(spend, "imp", 0, 0), axis=0)
    new_prices = prices.astype(jnp.float32) + 2.0 * (mine - spend_limits) / (mine + spend_limits)
    return (new_prices, logz.reshape(TILES * BLOCK))


def solution(mesh):
    return jax.shard_map(
        local,
        mesh=mesh,
        in_specs=(
            P(("imp", "camp"), None),
            P(("imp", "camp")),
            P(("camp", "imp"), None),
            P(("camp", "imp")),
            P(("camp", "imp")),
            P("imp", "camp", None),
            P("imp", "camp"),
        ),
        out_specs=(P(("camp", "imp")), P("imp")),
        check_vma=False,
    )
```

time: 89.7 us -> 82.8 us (0.923)
  local copies, waits for them, and re-layouts: 3.48 us -> 0.07 us
  Pallas kernels: 14.2 us -> 11.4 us
  waiting for transfers between devices: 11.5 us -> 13.5 us
  other arithmetic: 4.17 us -> 2.21 us
  blocking collectives: 27.5 us -> 26.6 us
    ppermute x4 -> x5, waiting for transfers between devices: 2.59 us -> 5.97 us  [shift_z(): return lax.ppermute(v, 'imp', perm)]
    ppermute x4 -> x5, starting transfers between devices: 12.2 us -> 14.9 us  [shift_z(): return lax.ppermute(v, 'imp', perm)]
    concatenate x3 -> x0, other arithmetic: 2.68 us -> none  [the longest x1 0.97 us: local(): jnp.concatenate([imp_emb, jnp.pad(imp_cost.reshape(2, D), ((0, PAD - 2),...]
    ppermute x6, starting transfers between devices: 8.89 us -> 6.23 us  [shift_y(): return lax.ppermute(v, 'imp', perm)]
    ppermute x6, waiting for transfers between devices: 6.27 us -> 3.88 us  [shift_y(): return lax.ppermute(v, 'imp', perm)]
    pallas_call x2, Pallas kernels: 5.66 us -> 3.49 us  [the longest x1 1.98 us: local(): pl.pallas_call(spend_kernel, in_specs=[SM] + [VM] * 3, out_specs=[VM] * 2...]
    unnamed x8, local copies, waits for them, and re-layouts: 2.06 us -> 0.05 us
    ppermute x3, waiting for transfers between devices: 1.12 us -> 2.89 us  [shift_x(): return lax.ppermute(v, 'camp', perm)]
  transfers between devices with their start and end apart: 17 -> 18, of which waited for: 9 -> 7; matrix products, arithmetic and copies ran while one was open for 4% -> 1% of each run, Pallas kernels for 3% -> 2%
where the time goes in v4:
time: 82.8 us; the launch traced here: 81.6 us
  starting transfers between devices  27.1 us (33%)
  blocking collectives  26.6 us (32%)
  waiting for transfers between devices  13.5 us (16%)
  Pallas kernels  11.4 us (14%)
  other arithmetic  2.21 us (3%)
    all_to_all x1, blocking collectives, local(): mine = jnp.sum(lax.all_to_all(spend, 'imp', 0, 0), axis=0)  15.2 us
    ppermute x5, starting transfers between devices, shift_z(): return lax.ppermute(v, 'imp', perm)  14.9 us
    all_to_all x1, blocking collectives, local(): stats = lax.all_to_all(stat, 'camp', 0, 0)  11.4 us
    pallas_call x1, Pallas kernels, local(): pl.pallas_call(stats_kernel, in_specs=[SM] * 2 + [pl.BlockSpec(memory_spa...  7.88 us
    ppermute x6, starting transfers between devices, shift_y(): return lax.ppermute(v, 'imp', perm)  6.23 us
    ppermute x5, waiting for transfers between devices, shift_z(): return lax.ppermute(v, 'imp', perm)  5.97 us
    ppermute x3, starting transfers between devices, shift_x(): return lax.ppermute(v, 'camp', perm)  5.14 us
    ppermute x6, waiting for transfers between devices, shift_y(): return lax.ppermute(v, 'imp', perm)  3.88 us
  transfers between devices with their start and end apart: 18, of which 7 were waited for; matrix products, arithmetic and copies ran while one was open for 1% of the time, Pallas kernels for 2%

profile of v4, /device:TPU:8, one launch (start us, length us, event | category | flops | bytes accessed | tf_op | source)
XLA Modules:
  0.0 81.6 jit_solution(16059632015059746999)
XLA Ops:
  0.6 0.0 copy-start
  0.7 0.9 %fusion.1 = bf16[144,256]{1,0:T(8,128)(2,1)S(1)} fusion(bf16[1,128]{1,0:T(2,128)(2,1)} %bitcast.18, bf16[128,256]{1,0:T(8,128)(2,1)} %param.9), kind=kLoop, calls=%fused_computation.2 | loop fusion | flops 221184 | bytes 139520 | tf_op jit(solution)/shard_map/concatenate | solution.py:188
  1.5 7.2 %collective-permute-start = (bf16[144,256]{1,0:T(8,128)(2,1)S(1)}, bf16[144,256]{1,0:T(8,128)(2,1)S(1)}, u32[]{:S(2)}, u32[]{:S(2)}) collective-permute-start(bf16[144,256]{1,0:T(8,128)(2,1)S(1)} %fusion.1), channel_id=1, source_target_pairs={{0,128},{8,136},{16,144},{24,152},{32,160},{40,168},{48,176},{56,1... | collective-permute-start | bytes 221192 | tf_op jit(solution)/shard_map/ppermute | solution.py:34
  8.7 0.0 collective-permute-start.5
  8.7 2.9 %collective-permute-start.4 = (bf16[144,256]{1,0:T(8,128)(2,1)S(1)}, bf16[144,256]{1,0:T(8,128)(2,1)S(1)}, u32[]{:S(2)}, u32[]{:S(2)}) collective-permute-start(bf16[144,256]{1,0:T(8,128)(2,1)S(1)} %fusion.1), channel_id=1, source_target_pairs={{0,64},{8,72},{16,80},{24,88},{32,96},{40,104},{48,112},{56,120},{... | collective-permute-start | bytes 221192 | tf_op jit(solution)/shard_map/ppermute | solution.py:34
  11.6 0.2 collective-permute-done
  11.8 2.8 %collective-permute-start.8 = (bf16[512,256]{1,0:T(8,128)(2,1)}, bf16[512,256]{1,0:T(8,128)(2,1)S(1)}, u32[]{:S(2)}, u32[]{:S(2)}) collective-permute-start(bf16[512,256]{1,0:T(8,128)(2,1)} %refs_0_.1), channel_id=1, source_target_pairs={{0,6},{1,7},{2,0},{3,1},{4,2},{5,3},{6,4},{7,5},{8,14},{9,15},{10,... | collective-permute-start | bytes 786440 | tf_op jit(solution)/shard_map/ppermute | solution.py:44
  14.6 0.0 collective-permute-start.7
  14.6 4.8 %collective-permute-start.2 = (bf16[288,256]{1,0:T(8,128)(2,1)S(1)}, bf16[288,256]{1,0:T(8,128)(2,1)S(1)}, u32[]{:S(2)}, u32[]{:S(2)}) collective-permute-start(bf16[288,256]{1,0:T(8,128)(2,1)S(1)} %get-tuple-element.33), channel_id=1, source_target_pairs={{0,224},{8,232},{16,240},{24,248},{32,0},{40,8},{48,16},{56,24},{6... | collective-permute-start | bytes 442376 | tf_op jit(solution)/shard_map/ppermute | solution.py:34
  19.4 0.0 collective-permute-done.4
  19.4 0.0 collective-permute-start.1
  19.4 0.0 collective-permute-done.5
  19.5 0.5 collective-permute-start.6
  20.0 5.8 %collective-permute-done.1 = bf16[288,256]{1,0:T(8,128)(2,1)S(1)} collective-permute-done((bf16[288,256]{1,0:T(8,128)(2,1)S(1)}, bf16[288,256]{1,0:T(8,128)(2,1)S(1)}, u32[]{:S(2)}, u32[]{:S(2)}) %collective-permute-start.1) | collective-permute-done | bytes 147488 | tf_op jit(solution)/shard_map/ppermute | solution.py:34
  25.8 0.0 collective-permute-done.2
  25.8 1.7 %collective-permute-start.3 = (bf16[576,256]{1,0:T(8,128)(2,1)S(1)}, bf16[576,256]{1,0:T(8,128)(2,1)S(1)}, u32[]{:S(2)}, u32[]{:S(2)}) collective-permute-start(bf16[576,256]{1,0:T(8,128)(2,1)S(1)} %constant_dynamic-update-slice_fusion.2.refs_8_), channel_id=1, source_target_pairs={{0,8},{8,16},{16,24},{24,0},{32,40},{40,48},{48,56},{56,32},{64,72... | collective-permute-start | bytes 884744 | tf_op jit(solution)/shard_map/ppermute | solution.py:39
  27.5 1.3 %collective-permute-start.15 = (bf16[576,256]{1,0:T(8,128)(2,1)S(1)}, bf16[576,256]{1,0:T(8,128)(2,1)S(1)}, u32[]{:S(2)}, u32[]{:S(2)}) collective-permute-start(bf16[576,256]{1,0:T(8,128)(2,1)S(1)} %constant_dynamic-update-slice_fusion.4.refs_9_), channel_id=1, source_target_pairs={{0,8},{8,16},{16,24},{24,0},{32,40},{40,48},{48,56},{56,32},{64,72... | collective-permute-start | bytes 884744 | tf_op jit(solution)/shard_map/ppermute | solution.py:39
  28.8 0.0 collective-permute-done.8.refs_2_
  28.8 0.7 collective-permute-start.14
  29.5 0.0 collective-permute-done.7.refs_1_
  29.5 0.0 collective-permute-start.10
  29.5 0.0 collective-permute-done.6.refs_13_
  29.5 2.4 %collective-permute-start.9 = (bf16[512,256]{1,0:T(8,128)(2,1)}, bf16[512,256]{1,0:T(8,128)(2,1)S(1)}, u32[]{:S(2)}, u32[]{:S(2)}) collective-permute-start(bf16[512,256]{1,0:T(8,128)(2,1)} %refs_0_.1), channel_id=1, source_target_pairs={{0,4},{1,5},{2,6},{3,7},{4,0},{5,1},{6,2},{7,3},{8,12},{9,13},{10,... | collective-permute-start | bytes 786440 | tf_op jit(solution)/shard_map/ppermute | solution.py:44
  31.9 1.5 %prep.1.groups = s32[133]{0:T(256)S(4)} custom-call(s32[8,32]{1,0:T(8,128)} %bitcast.17, s32[32]{0:T(128)} %bitcast.19), custom_call_target="tpu_custom_call" | custom-call | tf_op jit(solution)/shard_map/prep/pallas_call | solution.py:180
  33.4 0.7 bitcast_convert_fusion.refs_16_
  34.1 1.0 %collective-permute-done.3.refs_10_ = bf16[576,256]{1,0:T(8,128)(2,1)S(1)} collective-permute-done((bf16[576,256]{1,0:T(8,128)(2,1)S(1)}, bf16[576,256]{1,0:T(8,128)(2,1)S(1)}, u32[]{:S(2)}, u32[]{:S(2)}) %collective-permute-start.3) | collective-permute-done | bytes 294944 | tf_op jit(solution)/shard_map/ppermute | solution.py:39
  35.1 1.7 %collective-permute-start.17 = (bf16[576,256]{1,0:T(8,128)(2,1)S(1)}, bf16[576,256]{1,0:T(8,128)(2,1)S(1)}, u32[]{:S(2)}, u32[]{:S(2)}) collective-permute-start(bf16[576,256]{1,0:T(8,128)(2,1)S(1)} %collective-permute-done.6.refs_13_), channel_id=1, source_target_pairs={{0,24},{8,0},{16,8},{24,16},{32,56},{40,32},{48,40},{56,48},{64,88... | collective-permute-start | bytes 884744 | tf_op jit(solution)/shard_map/ppermute | solution.py:39
  36.8 0.0 collective-permute-done.10.refs_4_
  36.8 0.3 collective-permute-start.16
  37.1 2.9 %collective-permute-done.9.refs_3_ = bf16[512,256]{1,0:T(8,128)(2,1)S(1)} collective-permute-done((bf16[512,256]{1,0:T(8,128)(2,1)}, bf16[512,256]{1,0:T(8,128)(2,1)S(1)}, u32[]{:S(2)}, u32[]{:S(2)}) %collective-permute-start.9) | collective-permute-done | bytes 262176 | tf_op jit(solution)/shard_map/ppermute | solution.py:44
  40.0 0.0 collective-permute-start.13
  40.0 0.0 collective-permute-done.15.refs_12_
  40.0 0.5 collective-permute-start.11
  40.5 0.0 collective-permute-done.14.refs_11_
  40.5 0.3 collective-permute-start.12
  40.8 0.1 pad_add_fusion.where
  40.8 0.8 collective-permute-done.13.refs_7_
  41.6 1.5 %collective-permute-done.17.refs_15_ = bf16[576,256]{1,0:T(8,128)(2,1)S(1)} collective-permute-done((bf16[576,256]{1,0:T(8,128)(2,1)S(1)}, bf16[576,256]{1,0:T(8,128)(2,1)S(1)}, u32[]{:S(2)}, u32[]{:S(2)}) %collective-permute-start.17) | collective-permute-done | bytes 294944 | tf_op jit(solution)/shard_map/ppermute | solution.py:39
  43.2 0.0 collective-permute-done.11.refs_5_
  43.2 0.0 collective-permute-done.12.refs_6_
  43.2 1.4 %collective-permute-done.16.refs_14_ = bf16[576,256]{1,0:T(8,128)(2,1)S(1)} collective-permute-done((bf16[576,256]{1,0:T(8,128)(2,1)S(1)}, bf16[576,256]{1,0:T(8,128)(2,1)S(1)}, u32[]{:S(2)}, u32[]{:S(2)}) %collective-permute-start.16) | collective-permute-done | bytes 294944 | tf_op jit(solution)/shard_map/ppermute | solution.py:39
  44.6 7.9 %stats.1 = (f32[8,72,128]{2,1,0:T(8,128)S(1)}, f32[264,128,128]{2,1,0:T(8,128)S(1)}, f32[258,8,128]{2,1,0:T(8,128)S(1)}) custom-call(s32[133]{0:T(256)S(4)} %prep.1.groups, s32[4]{0:T(128)S(1)} %pad_add_fusion.where, bf16[512,256]{1,0:T(8,128)(2,1)} %refs_0_.1, bf16[512,256]{1,0:T(8,128)(2,1)S(1)} %collective-permute-done.7.refs_1_, ...), custom_call_target="tpu_custom_call" | custom-call | tf_op jit(solution)/shard_map/stats/pallas_call | solution.py:209
  52.4 11.4 %all_to_all.14.stats = f32[8,72,128]{2,1,0:T(8,128)S(1)} all-to-all(f32[8,72,128]{2,1,0:T(8,128)S(1)} %get-tuple-element.27), channel_id=1, replica_groups=mesh['imp'=32,'camp'=8] {'camp'}, dimensions={0} | all-to-all | bytes 589824 | tf_op jit(solution)/shard_map/all_to_all | solution.py:229
  63.8 2.0 %spend.1 = (f32[32,128]{1,0:T(8,128)S(1)}, f32[32,128]{1,0:T(8,128)}) custom-call(s32[133]{0:T(256)S(4)} %prep.1.groups, f32[8,72,128]{2,1,0:T(8,128)S(1)} %all_to_all.14.stats, f32[264,128,128]{2,1,0:T(8,128)S(1)} %get-tuple-element.28.expo, f32[258,8,128]{2,1,0:T(8,128)S(1)} %get-tuple-element.29.tops), custom_call_target="tpu_custom_call" | custom-call | tf_op jit(solution)/shard_map/spend/pallas_call | solution.py:231
  65.8 15.2 %all_to_all.15 = f32[32,1,128]{2,1,0:T(1,128)S(1)} all-to-all(f32[32,1,128]{2,1,0:T(1,128)S(1)} %bitcast.16), channel_id=1, replica_groups=mesh['imp'=32,'camp'=8] {'imp'}, dimensions={0} | all-to-all | bytes 32768 | tf_op jit(solution)/shard_map/all_to_all | solution.py:247
  81.0 0.1 reduce_sum.9
  81.1 0.0 copy-done.1
  81.1 0.5 divide_add_fusion
  (8 shorter events, 0.1 us)
Async XLA Ops:
  0.6 80.4 %copy-start = (bf16[128]{0:T(256)(128)(2,1)S(1)}, bf16[128]{0:T(256)(128)(2,1)}, u32[]{:S(2)}) copy-start(bf16[128]{0:T(256)(128)(2,1)} %param.10) | copy-start | bytes 772
  0.6 80.4 %copy-start.1 = (f32[128]{0:T(128)S(1)}, f32[128]{0:T(128)}, u32[]{:S(2)}) copy-start(f32[128]{0:T(128)} %param.11) | copy-start | bytes 1540
  1.5 10.3 %collective-permute-start = (bf16[144,256]{1,0:T(8,128)(2,1)S(1)}, bf16[144,256]{1,0:T(8,128)(2,1)S(1)}, u32[]{:S(2)}, u32[]{:S(2)}) collective-permute-start(bf16[144,256]{1,0:T(8,128)(2,1)S(1)} %fusion.1), channel_id=1, source_target_pairs={{0,128},{8,136},{16,144},{24,152},{32,160},{40,168},{48,176},{56,1... | collective-permute-start | bytes 221192 | tf_op jit(solution)/shard_map/ppermute | solution.py:34
  8.7 10.7 %collective-permute-start.5 = (bf16[144,256]{1,0:T(8,128)(2,1)S(1)}, bf16[144,256]{1,0:T(8,128)(2,1)S(1)}, u32[]{:S(2)}, u32[]{:S(2)}) collective-permute-start(bf16[144,256]{1,0:T(8,128)(2,1)S(1)} %fusion.1), channel_id=1, source_target_pairs={{0,192},{8,200},{16,208},{24,216},{32,224},{40,232},{48,240},{56,2... | collective-permute-start | bytes 221192 | tf_op jit(solution)/shard_map/ppermute | solution.py:34
  8.7 10.7 %collective-permute-start.4 = (bf16[144,256]{1,0:T(8,128)(2,1)S(1)}, bf16[144,256]{1,0:T(8,128)(2,1)S(1)}, u32[]{:S(2)}, u32[]{:S(2)}) collective-permute-start(bf16[144,256]{1,0:T(8,128)(2,1)S(1)} %fusion.1), channel_id=1, source_target_pairs={{0,64},{8,72},{16,80},{24,88},{32,96},{40,104},{48,112},{56,120},{... | collective-permute-start | bytes 221192 | tf_op jit(solution)/shard_map/ppermute | solution.py:34
  11.8 17.0 %collective-permute-start.8 = (bf16[512,256]{1,0:T(8,128)(2,1)}, bf16[512,256]{1,0:T(8,128)(2,1)S(1)}, u32[]{:S(2)}, u32[]{:S(2)}) collective-permute-start(bf16[512,256]{1,0:T(8,128)(2,1)} %refs_0_.1), channel_id=1, source_target_pairs={{0,6},{1,7},{2,0},{3,1},{4,2},{5,3},{6,4},{7,5},{8,14},{9,15},{10,... | collective-permute-start | bytes 786440 | tf_op jit(solution)/shard_map/ppermute | solution.py:44
  14.6 14.9 %collective-permute-start.7 = (bf16[512,256]{1,0:T(8,128)(2,1)}, bf16[512,256]{1,0:T(8,128)(2,1)S(1)}, u32[]{:S(2)}, u32[]{:S(2)}) collective-permute-start(bf16[512,256]{1,0:T(8,128)(2,1)} %refs_0_.1), channel_id=1, source_target_pairs={{0,2},{1,3},{2,4},{3,5},{4,6},{5,7},{6,0},{7,1},{8,10},{9,11},{10,... | collective-permute-start | bytes 786440 | tf_op jit(solution)/shard_map/ppermute | solution.py:44
  14.6 11.2 %collective-permute-start.2 = (bf16[288,256]{1,0:T(8,128)(2,1)S(1)}, bf16[288,256]{1,0:T(8,128)(2,1)S(1)}, u32[]{:S(2)}, u32[]{:S(2)}) collective-permute-start(bf16[288,256]{1,0:T(8,128)(2,1)S(1)} %get-tuple-element.33), channel_id=1, source_target_pairs={{0,224},{8,232},{16,240},{24,248},{32,0},{40,8},{48,16},{56,24},{6... | collective-permute-start | bytes 442376 | tf_op jit(solution)/shard_map/ppermute | solution.py:34
  19.4 6.4 %collective-permute-start.1 = (bf16[288,256]{1,0:T(8,128)(2,1)S(1)}, bf16[288,256]{1,0:T(8,128)(2,1)S(1)}, u32[]{:S(2)}, u32[]{:S(2)}) collective-permute-start(bf16[288,256]{1,0:T(8,128)(2,1)S(1)} %get-tuple-element.33), channel_id=1, source_target_pairs={{0,32},{8,40},{16,48},{24,56},{32,64},{40,72},{48,80},{56,88},{64,... | collective-permute-start | bytes 442376 | tf_op jit(solution)/shard_map/ppermute | solution.py:34
  19.5 10.1 %collective-permute-start.6 = (bf16[576,256]{1,0:T(8,128)(2,1)S(1)}, bf16[576,256]{1,0:T(8,128)(2,1)S(1)}, u32[]{:S(2)}, u32[]{:S(2)}) collective-permute-start(bf16[576,256]{1,0:T(8,128)(2,1)S(1)} %constant_dynamic-update-slice_fusion.4.refs_9_), channel_id=1, source_target_pairs={{0,24},{8,0},{16,8},{24,16},{32,56},{40,32},{48,40},{56,48},{64,88... | collective-permute-start | bytes 884744 | tf_op jit(solution)/shard_map/ppermute | solution.py:39
  25.8 9.2 %collective-permute-start.3 = (bf16[576,256]{1,0:T(8,128)(2,1)S(1)}, bf16[576,256]{1,0:T(8,128)(2,1)S(1)}, u32[]{:S(2)}, u32[]{:S(2)}) collective-permute-start(bf16[576,256]{1,0:T(8,128)(2,1)S(1)} %constant_dynamic-update-slice_fusion.2.refs_8_), channel_id=1, source_target_pairs={{0,8},{8,16},{16,24},{24,0},{32,40},{40,48},{48,56},{56,32},{64,72... | collective-permute-start | bytes 884744 | tf_op jit(solution)/shard_map/ppermute | solution.py:39
  27.5 12.5 %collective-permute-start.15 = (bf16[576,256]{1,0:T(8,128)(2,1)S(1)}, bf16[576,256]{1,0:T(8,128)(2,1)S(1)}, u32[]{:S(2)}, u32[]{:S(2)}) collective-permute-start(bf16[576,256]{1,0:T(8,128)(2,1)S(1)} %constant_dynamic-update-slice_fusion.4.refs_9_), channel_id=1, source_target_pairs={{0,8},{8,16},{16,24},{24,0},{32,40},{40,48},{48,56},{56,32},{64,72... | collective-permute-start | bytes 884744 | tf_op jit(solution)/shard_map/ppermute | solution.py:39
  28.8 11.7 %collective-permute-start.14 = (bf16[576,256]{1,0:T(8,128)(2,1)S(1)}, bf16[576,256]{1,0:T(8,128)(2,1)S(1)}, u32[]{:S(2)}, u32[]{:S(2)}) collective-permute-start(bf16[576,256]{1,0:T(8,128)(2,1)S(1)} %constant_dynamic-update-slice_fusion.2.refs_8_), channel_id=1, source_target_pairs={{0,24},{8,0},{16,8},{24,16},{32,56},{40,32},{48,40},{56,48},{64,88... | collective-permute-start | bytes 884744 | tf_op jit(solution)/shard_map/ppermute | solution.py:39
  29.5 7.3 %collective-permute-start.10 = (bf16[512,256]{1,0:T(8,128)(2,1)}, bf16[512,256]{1,0:T(8,128)(2,1)S(1)}, u32[]{:S(2)}, u32[]{:S(2)}) collective-permute-start(bf16[512,256]{1,0:T(8,128)(2,1)} %refs_0_.1), channel_id=1, source_target_pairs={{0,1},{1,0},{2,3},{3,2},{4,5},{5,4},{6,7},{7,6},{8,9},{9,8},{10,11... | collective-permute-start | bytes 786440 | tf_op jit(solution)/shard_map/ppermute | solution.py:49
  29.5 10.4 %collective-permute-start.9 = (bf16[512,256]{1,0:T(8,128)(2,1)}, bf16[512,256]{1,0:T(8,128)(2,1)S(1)}, u32[]{:S(2)}, u32[]{:S(2)}) collective-permute-start(bf16[512,256]{1,0:T(8,128)(2,1)} %refs_0_.1), channel_id=1, source_target_pairs={{0,4},{1,5},{2,6},{3,7},{4,0},{5,1},{6,2},{7,3},{8,12},{9,13},{10,... | collective-permute-start | bytes 786440 | tf_op jit(solution)/shard_map/ppermute | solution.py:44
  35.1 8.1 %collective-permute-start.17 = (bf16[576,256]{1,0:T(8,128)(2,1)S(1)}, bf16[576,256]{1,0:T(8,128)(2,1)S(1)}, u32[]{:S(2)}, u32[]{:S(2)}) collective-permute-start(bf16[576,256]{1,0:T(8,128)(2,1)S(1)} %collective-permute-done.6.refs_13_), channel_id=1, source_target_pairs={{0,24},{8,0},{16,8},{24,16},{32,56},{40,32},{48,40},{56,48},{64,88... | collective-permute-start | bytes 884744 | tf_op jit(solution)/shard_map/ppermute | solution.py:39
  36.8 7.8 %collective-permute-start.16 = (bf16[576,256]{1,0:T(8,128)(2,1)S(1)}, bf16[576,256]{1,0:T(8,128)(2,1)S(1)}, u32[]{:S(2)}, u32[]{:S(2)}) collective-permute-start(bf16[576,256]{1,0:T(8,128)(2,1)S(1)} %collective-permute-done.3.refs_10_), channel_id=1, source_target_pairs={{0,8},{8,16},{16,24},{24,0},{32,40},{40,48},{48,56},{56,32},{64,72... | collective-permute-start | bytes 884744 | tf_op jit(solution)/shard_map/ppermute | solution.py:39
  40.0 1.7 %collective-permute-start.13 = (bf16[512,256]{1,0:T(8,128)(2,1)S(1)}, bf16[512,256]{1,0:T(8,128)(2,1)}, u32[]{:S(2)}, u32[]{:S(2)}) collective-permute-start(bf16[512,256]{1,0:T(8,128)(2,1)S(1)} %collective-permute-done.9.refs_3_), channel_id=1, source_target_pairs={{0,1},{1,0},{2,3},{3,2},{4,5},{5,4},{6,7},{7,6},{8,9},{9,8},{10,11... | collective-permute-start | bytes 786440 | tf_op jit(solution)/shard_map/ppermute | solution.py:49
  40.0 3.2 %collective-permute-start.11 = (bf16[512,256]{1,0:T(8,128)(2,1)S(1)}, bf16[512,256]{1,0:T(8,128)(2,1)}, u32[]{:S(2)}, u32[]{:S(2)}) collective-permute-start(bf16[512,256]{1,0:T(8,128)(2,1)S(1)} %collective-permute-done.7.refs_1_), channel_id=1, source_target_pairs={{0,1},{1,0},{2,3},{3,2},{4,5},{5,4},{6,7},{7,6},{8,9},{9,8},{10,11... | collective-permute-start | bytes 786440 | tf_op jit(solution)/shard_map/ppermute | solution.py:49
  40.5 2.7 %collective-permute-start.12 = (bf16[512,256]{1,0:T(8,128)(2,1)S(1)}, bf16[512,256]{1,0:T(8,128)(2,1)}, u32[]{:S(2)}, u32[]{:S(2)}) collective-permute-start(bf16[512,256]{1,0:T(8,128)(2,1)S(1)} %collective-permute-done.8.refs_2_), channel_id=1, source_target_pairs={{0,1},{1,0},{2,3},{3,2},{4,5},{5,4},{6,7},{7,6},{8,9},{9,8},{10,11... | collective-permute-start | bytes 786440 | tf_op jit(solution)/shard_map/ppermute | solution.py:49

commit v5 on v4

--- a/solution.py
+++ b/solution.py
@@ -21,7 +21,7 @@
 LN2 = math.log(2.0)
 SCALE2 = 3.0 / math.sqrt(D) * LOG2E
 VMEM_LIMIT = 16 * 1024 * 1024
-UNROLL = 4
+UNROLL = 16
 GROUPS = TILES * SLOTS // 2 + UNROLL
 LAST = GROUPS
 FIRST, SECOND = 1024, 1024 * 64

time: 82.8 us -> 80.4 us (0.971)
  Pallas kernels: 11.4 us -> 8.93 us
    pallas_call x1, Pallas kernels: 7.88 us -> 5.48 us  [local(): pl.pallas_call(stats_kernel, in_specs=[SM] * 2 + [pl.BlockSpec(memory_spa...]
where the time goes in v5:
time: 80.4 us; the launch traced here: 79.8 us
  blocking collectives  27.2 us (34%)
  starting transfers between devices  27.1 us (34%)
  waiting for transfers between devices  13.5 us (17%)
  Pallas kernels  8.93 us (11%)
  other arithmetic  2.21 us (3%)
    all_to_all x1, blocking collectives, local(): mine = jnp.sum(lax.all_to_all(spend, 'imp', 0, 0), axis=0)  15.5 us
    ppermute x5, starting transfers between devices, shift_z(): return lax.ppermute(v, 'imp', perm)  14.9 us
    all_to_all x1, blocking collectives, local(): stats = lax.all_to_all(stat, 'camp', 0, 0)  11.7 us
    ppermute x6, starting transfers between devices, shift_y(): return lax.ppermute(v, 'imp', perm)  6.23 us
    ppermute x5, waiting for transfers between devices, shift_z(): return lax.ppermute(v, 'imp', perm)  5.97 us
    pallas_call x1, Pallas kernels, local(): pl.pallas_call(stats_kernel, in_specs=[SM] * 2 + [pl.BlockSpec(memory_spa...  5.48 us
    ppermute x3, starting transfers between devices, shift_x(): return lax.ppermute(v, 'camp', perm)  5.14 us
    ppermute x6, waiting for transfers between devices, shift_y(): return lax.ppermute(v, 'imp', perm)  3.88 us
  transfers between devices with their start and end apart: 18, of which 7 were waited for; matrix products, arithmetic and copies ran while one was open for 1% of the time, Pallas kernels for 2%

profile of v5, /device:TPU:8, one launch (start us, length us, event | category | flops | bytes accessed | tf_op | source)
XLA Modules:
  0.0 79.8 jit_solution(13632770692296329629)
XLA Ops:
  0.6 0.0 copy-start
  0.6 0.0 copy-start.1
  0.7 0.9 %fusion.1 = bf16[144,256]{1,0:T(8,128)(2,1)S(1)} fusion(bf16[1,128]{1,0:T(2,128)(2,1)} %bitcast.18, bf16[128,256]{1,0:T(8,128)(2,1)} %param.9), kind=kLoop, calls=%fused_computation.2 | loop fusion | flops 221184 | bytes 139520 | tf_op jit(solution)/shard_map/concatenate | solution.py:188
  1.5 7.2 %collective-permute-start = (bf16[144,256]{1,0:T(8,128)(2,1)S(1)}, bf16[144,256]{1,0:T(8,128)(2,1)S(1)}, u32[]{:S(2)}, u32[]{:S(2)}) collective-permute-start(bf16[144,256]{1,0:T(8,128)(2,1)S(1)} %fusion.1), channel_id=1, source_target_pairs={{0,128},{8,136},{16,144},{24,152},{32,160},{40,168},{48,176},{56,1... | collective-permute-start | bytes 221192 | tf_op jit(solution)/shard_map/ppermute | solution.py:34
  8.7 0.0 collective-permute-start.5
  8.7 2.9 %collective-permute-start.4 = (bf16[144,256]{1,0:T(8,128)(2,1)S(1)}, bf16[144,256]{1,0:T(8,128)(2,1)S(1)}, u32[]{:S(2)}, u32[]{:S(2)}) collective-permute-start(bf16[144,256]{1,0:T(8,128)(2,1)S(1)} %fusion.1), channel_id=1, source_target_pairs={{0,64},{8,72},{16,80},{24,88},{32,96},{40,104},{48,112},{56,120},{... | collective-permute-start | bytes 221192 | tf_op jit(solution)/shard_map/ppermute | solution.py:34
  11.6 0.2 collective-permute-done
  11.8 2.8 %collective-permute-start.8 = (bf16[512,256]{1,0:T(8,128)(2,1)}, bf16[512,256]{1,0:T(8,128)(2,1)S(1)}, u32[]{:S(2)}, u32[]{:S(2)}) collective-permute-start(bf16[512,256]{1,0:T(8,128)(2,1)} %refs_0_.1), channel_id=1, source_target_pairs={{0,6},{1,7},{2,0},{3,1},{4,2},{5,3},{6,4},{7,5},{8,14},{9,15},{10,... | collective-permute-start | bytes 786440 | tf_op jit(solution)/shard_map/ppermute | solution.py:44
  14.6 0.0 collective-permute-start.7
  14.6 4.8 %collective-permute-start.2 = (bf16[288,256]{1,0:T(8,128)(2,1)S(1)}, bf16[288,256]{1,0:T(8,128)(2,1)S(1)}, u32[]{:S(2)}, u32[]{:S(2)}) collective-permute-start(bf16[288,256]{1,0:T(8,128)(2,1)S(1)} %get-tuple-element.33), channel_id=1, source_target_pairs={{0,224},{8,232},{16,240},{24,248},{32,0},{40,8},{48,16},{56,24},{6... | collective-permute-start | bytes 442376 | tf_op jit(solution)/shard_map/ppermute | solution.py:34
  19.4 0.0 collective-permute-done.4
  19.4 0.0 collective-permute-start.1
  19.4 0.0 collective-permute-done.5
  19.5 0.5 collective-permute-start.6
  20.0 5.8 %collective-permute-done.1 = bf16[288,256]{1,0:T(8,128)(2,1)S(1)} collective-permute-done((bf16[288,256]{1,0:T(8,128)(2,1)S(1)}, bf16[288,256]{1,0:T(8,128)(2,1)S(1)}, u32[]{:S(2)}, u32[]{:S(2)}) %collective-permute-start.1) | collective-permute-done | bytes 147488 | tf_op jit(solution)/shard_map/ppermute | solution.py:34
  25.8 0.0 collective-permute-done.2
  25.8 1.7 %collective-permute-start.3 = (bf16[576,256]{1,0:T(8,128)(2,1)S(1)}, bf16[576,256]{1,0:T(8,128)(2,1)S(1)}, u32[]{:S(2)}, u32[]{:S(2)}) collective-permute-start(bf16[576,256]{1,0:T(8,128)(2,1)S(1)} %constant_dynamic-update-slice_fusion.2.refs_8_), channel_id=1, source_target_pairs={{0,8},{8,16},{16,24},{24,0},{32,40},{40,48},{48,56},{56,32},{64,72... | collective-permute-start | bytes 884744 | tf_op jit(solution)/shard_map/ppermute | solution.py:39
  27.5 1.3 %collective-permute-start.15 = (bf16[576,256]{1,0:T(8,128)(2,1)S(1)}, bf16[576,256]{1,0:T(8,128)(2,1)S(1)}, u32[]{:S(2)}, u32[]{:S(2)}) collective-permute-start(bf16[576,256]{1,0:T(8,128)(2,1)S(1)} %constant_dynamic-update-slice_fusion.4.refs_9_), channel_id=1, source_target_pairs={{0,8},{8,16},{16,24},{24,0},{32,40},{40,48},{48,56},{56,32},{64,72... | collective-permute-start | bytes 884744 | tf_op jit(solution)/shard_map/ppermute | solution.py:39
  28.8 0.0 collective-permute-done.8.refs_2_
  28.8 0.7 collective-permute-start.14
  29.5 0.0 collective-permute-done.7.refs_1_
  29.5 0.0 collective-permute-start.10
  29.5 0.0 collective-permute-done.6.refs_13_
  29.5 2.4 %collective-permute-start.9 = (bf16[512,256]{1,0:T(8,128)(2,1)}, bf16[512,256]{1,0:T(8,128)(2,1)S(1)}, u32[]{:S(2)}, u32[]{:S(2)}) collective-permute-start(bf16[512,256]{1,0:T(8,128)(2,1)} %refs_0_.1), channel_id=1, source_target_pairs={{0,4},{1,5},{2,6},{3,7},{4,0},{5,1},{6,2},{7,3},{8,12},{9,13},{10,... | collective-permute-start | bytes 786440 | tf_op jit(solution)/shard_map/ppermute | solution.py:44
  31.9 1.5 %prep.1.groups = s32[145]{0:T(256)S(4)} custom-call(s32[8,32]{1,0:T(8,128)} %bitcast.17, s32[32]{0:T(128)} %bitcast.19), custom_call_target="tpu_custom_call" | custom-call | tf_op jit(solution)/shard_map/prep/pallas_call | solution.py:180
  33.4 0.7 bitcast_convert_fusion.refs_16_
  34.1 0.9 %collective-permute-done.3.refs_10_ = bf16[576,256]{1,0:T(8,128)(2,1)S(1)} collective-permute-done((bf16[576,256]{1,0:T(8,128)(2,1)S(1)}, bf16[576,256]{1,0:T(8,128)(2,1)S(1)}, u32[]{:S(2)}, u32[]{:S(2)}) %collective-permute-start.3) | collective-permute-done | bytes 294944 | tf_op jit(solution)/shard_map/ppermute | solution.py:39
  35.1 1.7 %collective-permute-start.17 = (bf16[576,256]{1,0:T(8,128)(2,1)S(1)}, bf16[576,256]{1,0:T(8,128)(2,1)S(1)}, u32[]{:S(2)}, u32[]{:S(2)}) collective-permute-start(bf16[576,256]{1,0:T(8,128)(2,1)S(1)} %collective-permute-done.6.refs_13_), channel_id=1, source_target_pairs={{0,24},{8,0},{16,8},{24,16},{32,56},{40,32},{48,40},{56,48},{64,88... | collective-permute-start | bytes 884744 | tf_op jit(solution)/shard_map/ppermute | solution.py:39
  36.8 0.0 collective-permute-done.10.refs_4_
  36.8 0.3 collective-permute-start.16
  37.1 2.9 %collective-permute-done.9.refs_3_ = bf16[512,256]{1,0:T(8,128)(2,1)S(1)} collective-permute-done((bf16[512,256]{1,0:T(8,128)(2,1)}, bf16[512,256]{1,0:T(8,128)(2,1)S(1)}, u32[]{:S(2)}, u32[]{:S(2)}) %collective-permute-start.9) | collective-permute-done | bytes 262176 | tf_op jit(solution)/shard_map/ppermute | solution.py:44
  40.0 0.0 collective-permute-start.13
  40.0 0.0 collective-permute-done.15.refs_12_
  40.0 0.5 collective-permute-start.11
  40.5 0.0 collective-permute-done.14.refs_11_
  40.5 0.3 collective-permute-start.12
  40.8 0.1 pad_add_fusion.where
  40.8 0.8 %collective-permute-done.13.refs_7_ = bf16[512,256]{1,0:T(8,128)(2,1)} collective-permute-done((bf16[512,256]{1,0:T(8,128)(2,1)S(1)}, bf16[512,256]{1,0:T(8,128)(2,1)}, u32[]{:S(2)}, u32[]{:S(2)}) %collective-permute-start.13) | collective-permute-done | bytes 262176 | tf_op jit(solution)/shard_map/ppermute | solution.py:49
  41.6 1.5 %collective-permute-done.17.refs_15_ = bf16[576,256]{1,0:T(8,128)(2,1)S(1)} collective-permute-done((bf16[576,256]{1,0:T(8,128)(2,1)S(1)}, bf16[576,256]{1,0:T(8,128)(2,1)S(1)}, u32[]{:S(2)}, u32[]{:S(2)}) %collective-permute-start.17) | collective-permute-done | bytes 294944 | tf_op jit(solution)/shard_map/ppermute | solution.py:39
  43.2 0.0 collective-permute-done.11.refs_5_
  43.2 0.0 collective-permute-done.12.refs_6_
  43.2 1.4 %collective-permute-done.16.refs_14_ = bf16[576,256]{1,0:T(8,128)(2,1)S(1)} collective-permute-done((bf16[576,256]{1,0:T(8,128)(2,1)S(1)}, bf16[576,256]{1,0:T(8,128)(2,1)S(1)}, u32[]{:S(2)}, u32[]{:S(2)}) %collective-permute-start.16) | collective-permute-done | bytes 294944 | tf_op jit(solution)/shard_map/ppermute | solution.py:39
  44.6 5.5 %stats.1 = (f32[8,72,128]{2,1,0:T(8,128)S(1)}, f32[288,128,128]{2,1,0:T(8,128)S(1)}, f32[258,8,128]{2,1,0:T(8,128)S(1)}) custom-call(s32[145]{0:T(256)S(4)} %prep.1.groups, s32[4]{0:T(128)S(1)} %pad_add_fusion.where, bf16[512,256]{1,0:T(8,128)(2,1)} %refs_0_.1, bf16[512,256]{1,0:T(8,128)(2,1)S(1)} %collective-permute-done.7.refs_1_, ...), custom_call_target="tpu_custom_call" | custom-call | tf_op jit(solution)/shard_map/stats/pallas_call | solution.py:209
  50.1 11.7 %all_to_all.14.stats = f32[8,72,128]{2,1,0:T(8,128)S(1)} all-to-all(f32[8,72,128]{2,1,0:T(8,128)S(1)} %get-tuple-element.27), channel_id=1, replica_groups=mesh['imp'=32,'camp'=8] {'camp'}, dimensions={0} | all-to-all | bytes 589824 | tf_op jit(solution)/shard_map/all_to_all | solution.py:229
  61.8 1.9 %spend.1 = (f32[32,128]{1,0:T(8,128)S(1)}, f32[32,128]{1,0:T(8,128)}) custom-call(s32[145]{0:T(256)S(4)} %prep.1.groups, f32[8,72,128]{2,1,0:T(8,128)S(1)} %all_to_all.14.stats, f32[288,128,128]{2,1,0:T(8,128)S(1)} %get-tuple-element.28.expo, f32[258,8,128]{2,1,0:T(8,128)S(1)} %get-tuple-element.29.tops), custom_call_target="tpu_custom_call" | custom-call | tf_op jit(solution)/shard_map/spend/pallas_call | solution.py:231
  63.7 15.5 %all_to_all.15 = f32[32,1,128]{2,1,0:T(1,128)S(1)} all-to-all(f32[32,1,128]{2,1,0:T(1,128)S(1)} %bitcast.16), channel_id=1, replica_groups=mesh['imp'=32,'camp'=8] {'imp'}, dimensions={0} | all-to-all | bytes 32768 | tf_op jit(solution)/shard_map/all_to_all | solution.py:247
  79.2 0.1 reduce_sum.9
  79.3 0.5 divide_add_fusion
  (8 shorter events, 0.1 us)
Async XLA Ops:
  0.6 78.6 %copy-start = (bf16[128]{0:T(256)(128)(2,1)S(1)}, bf16[128]{0:T(256)(128)(2,1)}, u32[]{:S(2)}) copy-start(bf16[128]{0:T(256)(128)(2,1)} %param.10) | copy-start | bytes 772
  0.6 78.6 %copy-start.1 = (f32[128]{0:T(128)S(1)}, f32[128]{0:T(128)}, u32[]{:S(2)}) copy-start(f32[128]{0:T(128)} %param.11) | copy-start | bytes 1540
  1.5 10.3 %collective-permute-start = (bf16[144,256]{1,0:T(8,128)(2,1)S(1)}, bf16[144,256]{1,0:T(8,128)(2,1)S(1)}, u32[]{:S(2)}, u32[]{:S(2)}) collective-permute-start(bf16[144,256]{1,0:T(8,128)(2,1)S(1)} %fusion.1), channel_id=1, source_target_pairs={{0,128},{8,136},{16,144},{24,152},{32,160},{40,168},{48,176},{56,1... | collective-permute-start | bytes 221192 | tf_op jit(solution)/shard_map/ppermute | solution.py:34
  8.7 10.7 %collective-permute-start.5 = (bf16[144,256]{1,0:T(8,128)(2,1)S(1)}, bf16[144,256]{1,0:T(8,128)(2,1)S(1)}, u32[]{:S(2)}, u32[]{:S(2)}) collective-permute-start(bf16[144,256]{1,0:T(8,128)(2,1)S(1)} %fusion.1), channel_id=1, source_target_pairs={{0,192},{8,200},{16,208},{24,216},{32,224},{40,232},{48,240},{56,2... | collective-permute-start | bytes 221192 | tf_op jit(solution)/shard_map/ppermute | solution.py:34
  8.7 10.7 %collective-permute-start.4 = (bf16[144,256]{1,0:T(8,128)(2,1)S(1)}, bf16[144,256]{1,0:T(8,128)(2,1)S(1)}, u32[]{:S(2)}, u32[]{:S(2)}) collective-permute-start(bf16[144,256]{1,0:T(8,128)(2,1)S(1)} %fusion.1), channel_id=1, source_target_pairs={{0,64},{8,72},{16,80},{24,88},{32,96},{40,104},{48,112},{56,120},{... | collective-permute-start | bytes 221192 | tf_op jit(solution)/shard_map/ppermute | solution.py:34
  11.8 17.0 %collective-permute-start.8 = (bf16[512,256]{1,0:T(8,128)(2,1)}, bf16[512,256]{1,0:T(8,128)(2,1)S(1)}, u32[]{:S(2)}, u32[]{:S(2)}) collective-permute-start(bf16[512,256]{1,0:T(8,128)(2,1)} %refs_0_.1), channel_id=1, source_target_pairs={{0,6},{1,7},{2,0},{3,1},{4,2},{5,3},{6,4},{7,5},{8,14},{9,15},{10,... | collective-permute-start | bytes 786440 | tf_op jit(solution)/shard_map/ppermute | solution.py:44
  14.6 14.9 %collective-permute-start.7 = (bf16[512,256]{1,0:T(8,128)(2,1)}, bf16[512,256]{1,0:T(8,128)(2,1)S(1)}, u32[]{:S(2)}, u32[]{:S(2)}) collective-permute-start(bf16[512,256]{1,0:T(8,128)(2,1)} %refs_0_.1), channel_id=1, source_target_pairs={{0,2},{1,3},{2,4},{3,5},{4,6},{5,7},{6,0},{7,1},{8,10},{9,11},{10,... | collective-permute-start | bytes 786440 | tf_op jit(solution)/shard_map/ppermute | solution.py:44
  14.6 11.2 %collective-permute-start.2 = (bf16[288,256]{1,0:T(8,128)(2,1)S(1)}, bf16[288,256]{1,0:T(8,128)(2,1)S(1)}, u32[]{:S(2)}, u32[]{:S(2)}) collective-permute-start(bf16[288,256]{1,0:T(8,128)(2,1)S(1)} %get-tuple-element.33), channel_id=1, source_target_pairs={{0,224},{8,232},{16,240},{24,248},{32,0},{40,8},{48,16},{56,24},{6... | collective-permute-start | bytes 442376 | tf_op jit(solution)/shard_map/ppermute | solution.py:34
  19.4 6.4 %collective-permute-start.1 = (bf16[288,256]{1,0:T(8,128)(2,1)S(1)}, bf16[288,256]{1,0:T(8,128)(2,1)S(1)}, u32[]{:S(2)}, u32[]{:S(2)}) collective-permute-start(bf16[288,256]{1,0:T(8,128)(2,1)S(1)} %get-tuple-element.33), channel_id=1, source_target_pairs={{0,32},{8,40},{16,48},{24,56},{32,64},{40,72},{48,80},{56,88},{64,... | collective-permute-start | bytes 442376 | tf_op jit(solution)/shard_map/ppermute | solution.py:34
  19.5 10.1 %collective-permute-start.6 = (bf16[576,256]{1,0:T(8,128)(2,1)S(1)}, bf16[576,256]{1,0:T(8,128)(2,1)S(1)}, u32[]{:S(2)}, u32[]{:S(2)}) collective-permute-start(bf16[576,256]{1,0:T(8,128)(2,1)S(1)} %constant_dynamic-update-slice_fusion.4.refs_9_), channel_id=1, source_target_pairs={{0,24},{8,0},{16,8},{24,16},{32,56},{40,32},{48,40},{56,48},{64,88... | collective-permute-start | bytes 884744 | tf_op jit(solution)/shard_map/ppermute | solution.py:39
  25.8 9.2 %collective-permute-start.3 = (bf16[576,256]{1,0:T(8,128)(2,1)S(1)}, bf16[576,256]{1,0:T(8,128)(2,1)S(1)}, u32[]{:S(2)}, u32[]{:S(2)}) collective-permute-start(bf16[576,256]{1,0:T(8,128)(2,1)S(1)} %constant_dynamic-update-slice_fusion.2.refs_8_), channel_id=1, source_target_pairs={{0,8},{8,16},{16,24},{24,0},{32,40},{40,48},{48,56},{56,32},{64,72... | collective-permute-start | bytes 884744 | tf_op jit(solution)/shard_map/ppermute | solution.py:39
  27.5 12.5 %collective-permute-start.15 = (bf16[576,256]{1,0:T(8,128)(2,1)S(1)}, bf16[576,256]{1,0:T(8,128)(2,1)S(1)}, u32[]{:S(2)}, u32[]{:S(2)}) collective-permute-start(bf16[576,256]{1,0:T(8,128)(2,1)S(1)} %constant_dynamic-update-slice_fusion.4.refs_9_), channel_id=1, source_target_pairs={{0,8},{8,16},{16,24},{24,0},{32,40},{40,48},{48,56},{56,32},{64,72... | collective-permute-start | bytes 884744 | tf_op jit(solution)/shard_map/ppermute | solution.py:39
  28.8 11.7 %collective-permute-start.14 = (bf16[576,256]{1,0:T(8,128)(2,1)S(1)}, bf16[576,256]{1,0:T(8,128)(2,1)S(1)}, u32[]{:S(2)}, u32[]{:S(2)}) collective-permute-start(bf16[576,256]{1,0:T(8,128)(2,1)S(1)} %constant_dynamic-update-slice_fusion.2.refs_8_), channel_id=1, source_target_pairs={{0,24},{8,0},{16,8},{24,16},{32,56},{40,32},{48,40},{56,48},{64,88... | collective-permute-start | bytes 884744 | tf_op jit(solution)/shard_map/ppermute | solution.py:39
  29.5 7.3 %collective-permute-start.10 = (bf16[512,256]{1,0:T(8,128)(2,1)}, bf16[512,256]{1,0:T(8,128)(2,1)S(1)}, u32[]{:S(2)}, u32[]{:S(2)}) collective-permute-start(bf16[512,256]{1,0:T(8,128)(2,1)} %refs_0_.1), channel_id=1, source_target_pairs={{0,1},{1,0},{2,3},{3,2},{4,5},{5,4},{6,7},{7,6},{8,9},{9,8},{10,11... | collective-permute-start | bytes 786440 | tf_op jit(solution)/shard_map/ppermute | solution.py:49
  29.5 10.4 %collective-permute-start.9 = (bf16[512,256]{1,0:T(8,128)(2,1)}, bf16[512,256]{1,0:T(8,128)(2,1)S(1)}, u32[]{:S(2)}, u32[]{:S(2)}) collective-permute-start(bf16[512,256]{1,0:T(8,128)(2,1)} %refs_0_.1), channel_id=1, source_target_pairs={{0,4},{1,5},{2,6},{3,7},{4,0},{5,1},{6,2},{7,3},{8,12},{9,13},{10,... | collective-permute-start | bytes 786440 | tf_op jit(solution)/shard_map/ppermute | solution.py:44
  35.1 8.1 %collective-permute-start.17 = (bf16[576,256]{1,0:T(8,128)(2,1)S(1)}, bf16[576,256]{1,0:T(8,128)(2,1)S(1)}, u32[]{:S(2)}, u32[]{:S(2)}) collective-permute-start(bf16[576,256]{1,0:T(8,128)(2,1)S(1)} %collective-permute-done.6.refs_13_), channel_id=1, source_target_pairs={{0,24},{8,0},{16,8},{24,16},{32,56},{40,32},{48,40},{56,48},{64,88... | collective-permute-start | bytes 884744 | tf_op jit(solution)/shard_map/ppermute | solution.py:39
  36.8 7.8 %collective-permute-start.16 = (bf16[576,256]{1,0:T(8,128)(2,1)S(1)}, bf16[576,256]{1,0:T(8,128)(2,1)S(1)}, u32[]{:S(2)}, u32[]{:S(2)}) collective-permute-start(bf16[576,256]{1,0:T(8,128)(2,1)S(1)} %collective-permute-done.3.refs_10_), channel_id=1, source_target_pairs={{0,8},{8,16},{16,24},{24,0},{32,40},{40,48},{48,56},{56,32},{64,72... | collective-permute-start | bytes 884744 | tf_op jit(solution)/shard_map/ppermute | solution.py:39
  40.0 1.7 %collective-permute-start.13 = (bf16[512,256]{1,0:T(8,128)(2,1)S(1)}, bf16[512,256]{1,0:T(8,128)(2,1)}, u32[]{:S(2)}, u32[]{:S(2)}) collective-permute-start(bf16[512,256]{1,0:T(8,128)(2,1)S(1)} %collective-permute-done.9.refs_3_), channel_id=1, source_target_pairs={{0,1},{1,0},{2,3},{3,2},{4,5},{5,4},{6,7},{7,6},{8,9},{9,8},{10,11... | collective-permute-start | bytes 786440 | tf_op jit(solution)/shard_map/ppermute | solution.py:49
  40.0 3.2 %collective-permute-start.11 = (bf16[512,256]{1,0:T(8,128)(2,1)S(1)}, bf16[512,256]{1,0:T(8,128)(2,1)}, u32[]{:S(2)}, u32[]{:S(2)}) collective-permute-start(bf16[512,256]{1,0:T(8,128)(2,1)S(1)} %collective-permute-done.7.refs_1_), channel_id=1, source_target_pairs={{0,1},{1,0},{2,3},{3,2},{4,5},{5,4},{6,7},{7,6},{8,9},{9,8},{10,11... | collective-permute-start | bytes 786440 | tf_op jit(solution)/shard_map/ppermute | solution.py:49
  40.5 2.7 %collective-permute-start.12 = (bf16[512,256]{1,0:T(8,128)(2,1)S(1)}, bf16[512,256]{1,0:T(8,128)(2,1)}, u32[]{:S(2)}, u32[]{:S(2)}) collective-permute-start(bf16[512,256]{1,0:T(8,128)(2,1)S(1)} %collective-permute-done.8.refs_2_), channel_id=1, source_target_pairs={{0,1},{1,0},{2,3},{3,2},{4,5},{5,4},{6,7},{7,6},{8,9},{9,8},{10,11... | collective-permute-start | bytes 786440 | tf_op jit(solution)/shard_map/ppermute | solution.py:49

commit v6 on v5

--- a/solution.py
+++ b/solution.py
@@ -190,12 +190,12 @@
     blk4, plus, minus = shift_z(blk, 4), shift_z(blk, 2), shift_z(blk, -2)
     near = other_core(imp_emb)
     bar = lax.optimization_barrier
-    blk4, emb, blk = bar((blk4, imp_emb, blk))
+    blk4, blk = bar((blk4, blk))
     pair = jnp.concatenate([blk, blk4], 0)
     up, down = shift_z(pair, 1), shift_z(pair, -1)
     b = jnp.concatenate([blk, blk4, plus, minus], 0)
     b_up, b_down = shift_y(b, 1), shift_y(b, -1)
-    left, right, across = shift_x(emb, 1), shift_x(emb, -1), shift_x(emb, 2)
+    left, right, across = shift_x(imp_emb, 1), shift_x(imp_emb, -1), shift_x(imp_emb, 2)
     a = jnp.concatenate([up, down], 0)
     a_up, a_down = shift_y(a, 1), shift_y(a, -1)
     b_down, left = bar((b_down, left))

time: 80.4 us -> 79.9 us (level)
  waiting for transfers between devices: 13.5 us -> 12.3 us
  Pallas kernels: 8.93 us -> 9.98 us
    ppermute x6, waiting for transfers between devices: 3.88 us -> 6.74 us  [shift_y(): return lax.ppermute(v, 'imp', perm)]
    ppermute x3, waiting for transfers between devices: 2.89 us -> 0.1 us  [shift_x(): return lax.ppermute(v, 'camp', perm)]
    ppermute x5, starting transfers between devices: 14.9 us -> 13.1 us  [shift_z(): return lax.ppermute(v, 'imp', perm)]
    ppermute x5, waiting for transfers between devices: 5.97 us -> 5.04 us  [shift_z(): return lax.ppermute(v, 'imp', perm)]
    ppermute x6, starting transfers between devices: 6.23 us -> 7.15 us  [shift_y(): return lax.ppermute(v, 'imp', perm)]
where the time goes in v6:
time: 79.9 us; the launch traced here: 78.8 us
  blocking collectives  26.9 us (34%)
  starting transfers between devices  26.6 us (33%)
  waiting for transfers between devices  12.3 us (15%)
  Pallas kernels  9.98 us (12%)
  other arithmetic  2.21 us (3%)
    all_to_all x1, blocking collectives, local(): mine = jnp.sum(lax.all_to_all(spend, 'imp', 0, 0), axis=0)  16 us
    ppermute x5, starting transfers between devices, shift_z(): return lax.ppermute(v, 'imp', perm)  13.1 us
    all_to_all x1, blocking collectives, local(): stats = lax.all_to_all(stat, 'camp', 0, 0)  10.9 us
    ppermute x6, starting transfers between devices, shift_y(): return lax.ppermute(v, 'imp', perm)  7.15 us
    ppermute x6, waiting for transfers between devices, shift_y(): return lax.ppermute(v, 'imp', perm)  6.74 us
    pallas_call x1, Pallas kernels, local(): pl.pallas_call(stats_kernel, in_specs=[SM] * 2 + [pl.BlockSpec(memory_spa...  6.23 us
    ppermute x3, starting transfers between devices, shift_x(): return lax.ppermute(v, 'camp', perm)  5.79 us
    ppermute x5, waiting for transfers between devices, shift_z(): return lax.ppermute(v, 'imp', perm)  5.04 us
  transfers between devices with their start and end apart: 18, of which 7 were waited for; matrix products, arithmetic and copies ran while one was open for 1% of the time, Pallas kernels for 2%

profile of v6, /device:TPU:8, one launch (start us, length us, event | category | flops | bytes accessed | tf_op | source)
XLA Modules:
  0.0 78.8 jit_solution(13807541228020510949)
XLA Ops:
  0.6 0.0 copy-start
  0.7 0.9 %fusion.1 = bf16[144,256]{1,0:T(8,128)(2,1)S(1)} fusion(bf16[1,128]{1,0:T(2,128)(2,1)} %bitcast.18, bf16[128,256]{1,0:T(8,128)(2,1)} %param.9), kind=kLoop, calls=%fused_computation.2 | loop fusion | flops 221184 | bytes 139520 | tf_op jit(solution)/shard_map/concatenate | solution.py:188
  1.5 7.2 %collective-permute-start = (bf16[144,256]{1,0:T(8,128)(2,1)S(1)}, bf16[144,256]{1,0:T(8,128)(2,1)S(1)}, u32[]{:S(2)}, u32[]{:S(2)}) collective-permute-start(bf16[144,256]{1,0:T(8,128)(2,1)S(1)} %fusion.1), channel_id=1, source_target_pairs={{0,128},{8,136},{16,144},{24,152},{32,160},{40,168},{48,176},{56,1... | collective-permute-start | bytes 221192 | tf_op jit(solution)/shard_map/ppermute | solution.py:34
  8.7 0.0 collective-permute-start.5
  8.7 2.9 %collective-permute-start.4 = (bf16[144,256]{1,0:T(8,128)(2,1)S(1)}, bf16[144,256]{1,0:T(8,128)(2,1)S(1)}, u32[]{:S(2)}, u32[]{:S(2)}) collective-permute-start(bf16[144,256]{1,0:T(8,128)(2,1)S(1)} %fusion.1), channel_id=1, source_target_pairs={{0,64},{8,72},{16,80},{24,88},{32,96},{40,104},{48,112},{56,120},{... | collective-permute-start | bytes 221192 | tf_op jit(solution)/shard_map/ppermute | solution.py:34
  11.6 2.8 %collective-permute-start.8 = (bf16[512,256]{1,0:T(8,128)(2,1)}, bf16[512,256]{1,0:T(8,128)(2,1)S(1)}, u32[]{:S(2)}, u32[]{:S(2)}) collective-permute-start(bf16[512,256]{1,0:T(8,128)(2,1)} %refs_0_.1), channel_id=1, source_target_pairs={{0,6},{1,7},{2,0},{3,1},{4,2},{5,3},{6,4},{7,5},{8,14},{9,15},{10,... | collective-permute-start | bytes 786440 | tf_op jit(solution)/shard_map/ppermute | solution.py:44
  14.4 0.0 collective-permute-start.7
  14.4 0.0 collective-permute-done
  14.4 2.2 %collective-permute-start.2 = (bf16[288,256]{1,0:T(8,128)(2,1)S(1)}, bf16[288,256]{1,0:T(8,128)(2,1)S(1)}, u32[]{:S(2)}, u32[]{:S(2)}) collective-permute-start(bf16[288,256]{1,0:T(8,128)(2,1)S(1)} %get-tuple-element.31), channel_id=1, source_target_pairs={{0,224},{8,232},{16,240},{24,248},{32,0},{40,8},{48,16},{56,24},{6... | collective-permute-start | bytes 442376 | tf_op jit(solution)/shard_map/ppermute | solution.py:34
  16.7 0.0 collective-permute-done.4
  16.7 0.8 collective-permute-start.1
  17.4 0.0 collective-permute-done.5
  17.5 0.5 collective-permute-start.6
  18.0 5.0 %collective-permute-done.1 = bf16[288,256]{1,0:T(8,128)(2,1)S(1)} collective-permute-done((bf16[288,256]{1,0:T(8,128)(2,1)S(1)}, bf16[288,256]{1,0:T(8,128)(2,1)S(1)}, u32[]{:S(2)}, u32[]{:S(2)}) %collective-permute-start.1) | collective-permute-done | bytes 147488 | tf_op jit(solution)/shard_map/ppermute | solution.py:34
  23.0 0.0 collective-permute-done.2
  23.1 1.7 %collective-permute-start.3 = (bf16[576,256]{1,0:T(8,128)(2,1)S(1)}, bf16[576,256]{1,0:T(8,128)(2,1)S(1)}, u32[]{:S(2)}, u32[]{:S(2)}) collective-permute-start(bf16[576,256]{1,0:T(8,128)(2,1)S(1)} %constant_dynamic-update-slice_fusion.2.refs_8_), channel_id=1, source_target_pairs={{0,8},{8,16},{16,24},{24,0},{32,40},{40,48},{48,56},{56,32},{64,72... | collective-permute-start | bytes 884744 | tf_op jit(solution)/shard_map/ppermute | solution.py:39
  24.7 1.3 %collective-permute-start.15 = (bf16[576,256]{1,0:T(8,128)(2,1)S(1)}, bf16[576,256]{1,0:T(8,128)(2,1)S(1)}, u32[]{:S(2)}, u32[]{:S(2)}) collective-permute-start(bf16[576,256]{1,0:T(8,128)(2,1)S(1)} %constant_dynamic-update-slice_fusion.4.refs_9_), channel_id=1, source_target_pairs={{0,8},{8,16},{16,24},{24,0},{32,40},{40,48},{48,56},{56,32},{64,72... | collective-permute-start | bytes 884744 | tf_op jit(solution)/shard_map/ppermute | solution.py:39
  26.0 0.0 collective-permute-done.8.refs_2_
  26.0 0.7 collective-permute-start.14
  26.8 0.0 collective-permute-done.7.refs_1_
  26.8 3.0 %collective-permute-start.9 = (bf16[512,256]{1,0:T(8,128)(2,1)}, bf16[512,256]{1,0:T(8,128)(2,1)S(1)}, u32[]{:S(2)}, u32[]{:S(2)}) collective-permute-start(bf16[512,256]{1,0:T(8,128)(2,1)} %refs_0_.1), channel_id=1, source_target_pairs={{0,4},{1,5},{2,6},{3,7},{4,0},{5,1},{6,2},{7,3},{8,12},{9,13},{10,... | collective-permute-start | bytes 786440 | tf_op jit(solution)/shard_map/ppermute | solution.py:44
  29.8 0.0 collective-permute-done.6.refs_13_
  29.8 0.0 collective-permute-start.10
  29.8 1.5 %prep.1.groups = s32[145]{0:T(256)S(4)} custom-call(s32[8,32]{1,0:T(8,128)} %bitcast.17, s32[32]{0:T(128)} %bitcast.19), custom_call_target="tpu_custom_call" | custom-call | tf_op jit(solution)/shard_map/prep/pallas_call | solution.py:180
  31.3 0.7 bitcast_convert_fusion.refs_16_
  32.0 1.1 %collective-permute-done.3.refs_10_ = bf16[576,256]{1,0:T(8,128)(2,1)S(1)} collective-permute-done((bf16[576,256]{1,0:T(8,128)(2,1)S(1)}, bf16[576,256]{1,0:T(8,128)(2,1)S(1)}, u32[]{:S(2)}, u32[]{:S(2)}) %collective-permute-start.3) | collective-permute-done | bytes 294944 | tf_op jit(solution)/shard_map/ppermute | solution.py:39
  33.1 1.7 %collective-permute-start.17 = (bf16[576,256]{1,0:T(8,128)(2,1)S(1)}, bf16[576,256]{1,0:T(8,128)(2,1)S(1)}, u32[]{:S(2)}, u32[]{:S(2)}) collective-permute-start(bf16[576,256]{1,0:T(8,128)(2,1)S(1)} %collective-permute-done.6.refs_13_), channel_id=1, source_target_pairs={{0,24},{8,0},{16,8},{24,16},{32,56},{40,32},{48,40},{56,48},{64,88... | collective-permute-start | bytes 884744 | tf_op jit(solution)/shard_map/ppermute | solution.py:39
  34.7 0.1 collective-permute-done.9.refs_3_
  34.8 1.3 %collective-permute-start.16 = (bf16[576,256]{1,0:T(8,128)(2,1)S(1)}, bf16[576,256]{1,0:T(8,128)(2,1)S(1)}, u32[]{:S(2)}, u32[]{:S(2)}) collective-permute-start(bf16[576,256]{1,0:T(8,128)(2,1)S(1)} %collective-permute-done.3.refs_10_), channel_id=1, source_target_pairs={{0,8},{8,16},{16,24},{24,0},{32,40},{40,48},{48,56},{56,32},{64,72... | collective-permute-start | bytes 884744 | tf_op jit(solution)/shard_map/ppermute | solution.py:39
  36.1 0.0 collective-permute-done.10.refs_4_
  36.1 0.0 collective-permute-start.13
  36.1 0.6 collective-permute-done.15.refs_12_
  36.8 0.0 collective-permute-start.11
  36.8 0.0 collective-permute-done.14.refs_11_
  36.8 0.5 collective-permute-start.12
  37.3 0.1 pad_add_fusion.where
  37.3 0.4 collective-permute-done.13.refs_7_
  37.8 3.6 %collective-permute-done.17.refs_15_ = bf16[576,256]{1,0:T(8,128)(2,1)S(1)} collective-permute-done((bf16[576,256]{1,0:T(8,128)(2,1)S(1)}, bf16[576,256]{1,0:T(8,128)(2,1)S(1)}, u32[]{:S(2)}, u32[]{:S(2)}) %collective-permute-start.17) | collective-permute-done | bytes 294944 | tf_op jit(solution)/shard_map/ppermute | solution.py:39
  41.4 0.0 collective-permute-done.11.refs_5_
  41.4 0.0 collective-permute-done.12.refs_6_
  41.4 1.4 %collective-permute-done.16.refs_14_ = bf16[576,256]{1,0:T(8,128)(2,1)S(1)} collective-permute-done((bf16[576,256]{1,0:T(8,128)(2,1)S(1)}, bf16[576,256]{1,0:T(8,128)(2,1)S(1)}, u32[]{:S(2)}, u32[]{:S(2)}) %collective-permute-start.16) | collective-permute-done | bytes 294944 | tf_op jit(solution)/shard_map/ppermute | solution.py:39
  42.8 6.2 %stats.1 = (f32[8,72,128]{2,1,0:T(8,128)S(1)}, f32[288,128,128]{2,1,0:T(8,128)S(1)}, f32[258,8,128]{2,1,0:T(8,128)S(1)}) custom-call(s32[145]{0:T(256)S(4)} %prep.1.groups, s32[4]{0:T(128)S(1)} %pad_add_fusion.where, bf16[512,256]{1,0:T(8,128)(2,1)} %refs_0_.1, bf16[512,256]{1,0:T(8,128)(2,1)S(1)} %collective-permute-done.7.refs_1_, ...), custom_call_target="tpu_custom_call" | custom-call | tf_op jit(solution)/shard_map/stats/pallas_call | solution.py:209
  49.1 10.9 %all_to_all.14.stats = f32[8,72,128]{2,1,0:T(8,128)S(1)} all-to-all(f32[8,72,128]{2,1,0:T(8,128)S(1)} %get-tuple-element.25), channel_id=1, replica_groups=mesh['imp'=32,'camp'=8] {'camp'}, dimensions={0} | all-to-all | bytes 589824 | tf_op jit(solution)/shard_map/all_to_all | solution.py:229
  60.0 2.2 %spend.1 = (f32[32,128]{1,0:T(8,128)S(1)}, f32[32,128]{1,0:T(8,128)}) custom-call(s32[145]{0:T(256)S(4)} %prep.1.groups, f32[8,72,128]{2,1,0:T(8,128)S(1)} %all_to_all.14.stats, f32[288,128,128]{2,1,0:T(8,128)S(1)} %get-tuple-element.26.expo, f32[258,8,128]{2,1,0:T(8,128)S(1)} %get-tuple-element.27.tops), custom_call_target="tpu_custom_call" | custom-call | tf_op jit(solution)/shard_map/spend/pallas_call | solution.py:231
  62.2 16.0 %all_to_all.15 = f32[32,1,128]{2,1,0:T(1,128)S(1)} all-to-all(f32[32,1,128]{2,1,0:T(1,128)S(1)} %bitcast.16), channel_id=1, replica_groups=mesh['imp'=32,'camp'=8] {'imp'}, dimensions={0} | all-to-all | bytes 32768 | tf_op jit(solution)/shard_map/all_to_all | solution.py:247
  78.2 0.1 reduce_sum.9
  78.3 0.0 copy-done
  78.3 0.5 divide_add_fusion
  (8 shorter events, 0.1 us)
Async XLA Ops:
  0.6 77.7 %copy-start = (bf16[128]{0:T(256)(128)(2,1)S(1)}, bf16[128]{0:T(256)(128)(2,1)}, u32[]{:S(2)}) copy-start(bf16[128]{0:T(256)(128)(2,1)} %param.10) | copy-start | bytes 772
  0.6 77.7 %copy-start.1 = (f32[128]{0:T(128)S(1)}, f32[128]{0:T(128)}, u32[]{:S(2)}) copy-start(f32[128]{0:T(128)} %param.11) | copy-start | bytes 1540
  1.5 12.9 %collective-permute-start = (bf16[144,256]{1,0:T(8,128)(2,1)S(1)}, bf16[144,256]{1,0:T(8,128)(2,1)S(1)}, u32[]{:S(2)}, u32[]{:S(2)}) collective-permute-start(bf16[144,256]{1,0:T(8,128)(2,1)S(1)} %fusion.1), channel_id=1, source_target_pairs={{0,128},{8,136},{16,144},{24,152},{32,160},{40,168},{48,176},{56,1... | collective-permute-start | bytes 221192 | tf_op jit(solution)/shard_map/ppermute | solution.py:34
  8.7 8.7 %collective-permute-start.5 = (bf16[144,256]{1,0:T(8,128)(2,1)S(1)}, bf16[144,256]{1,0:T(8,128)(2,1)S(1)}, u32[]{:S(2)}, u32[]{:S(2)}) collective-permute-start(bf16[144,256]{1,0:T(8,128)(2,1)S(1)} %fusion.1), channel_id=1, source_target_pairs={{0,192},{8,200},{16,208},{24,216},{32,224},{40,232},{48,240},{56,2... | collective-permute-start | bytes 221192 | tf_op jit(solution)/shard_map/ppermute | solution.py:34
  8.7 7.9 %collective-permute-start.4 = (bf16[144,256]{1,0:T(8,128)(2,1)S(1)}, bf16[144,256]{1,0:T(8,128)(2,1)S(1)}, u32[]{:S(2)}, u32[]{:S(2)}) collective-permute-start(bf16[144,256]{1,0:T(8,128)(2,1)S(1)} %fusion.1), channel_id=1, source_target_pairs={{0,64},{8,72},{16,80},{24,88},{32,96},{40,104},{48,112},{56,120},{... | collective-permute-start | bytes 221192 | tf_op jit(solution)/shard_map/ppermute | solution.py:34
  11.6 14.4 %collective-permute-start.8 = (bf16[512,256]{1,0:T(8,128)(2,1)}, bf16[512,256]{1,0:T(8,128)(2,1)S(1)}, u32[]{:S(2)}, u32[]{:S(2)}) collective-permute-start(bf16[512,256]{1,0:T(8,128)(2,1)} %refs_0_.1), channel_id=1, source_target_pairs={{0,6},{1,7},{2,0},{3,1},{4,2},{5,3},{6,4},{7,5},{8,14},{9,15},{10,... | collective-permute-start | bytes 786440 | tf_op jit(solution)/shard_map/ppermute | solution.py:44
  14.4 12.4 %collective-permute-start.7 = (bf16[512,256]{1,0:T(8,128)(2,1)}, bf16[512,256]{1,0:T(8,128)(2,1)S(1)}, u32[]{:S(2)}, u32[]{:S(2)}) collective-permute-start(bf16[512,256]{1,0:T(8,128)(2,1)} %refs_0_.1), channel_id=1, source_target_pairs={{0,2},{1,3},{2,4},{3,5},{4,6},{5,7},{6,0},{7,1},{8,10},{9,11},{10,... | collective-permute-start | bytes 786440 | tf_op jit(solution)/shard_map/ppermute | solution.py:44
  14.4 8.6 %collective-permute-start.2 = (bf16[288,256]{1,0:T(8,128)(2,1)S(1)}, bf16[288,256]{1,0:T(8,128)(2,1)S(1)}, u32[]{:S(2)}, u32[]{:S(2)}) collective-permute-start(bf16[288,256]{1,0:T(8,128)(2,1)S(1)} %get-tuple-element.31), channel_id=1, source_target_pairs={{0,224},{8,232},{16,240},{24,248},{32,0},{40,8},{48,16},{56,24},{6... | collective-permute-start | bytes 442376 | tf_op jit(solution)/shard_map/ppermute | solution.py:34
  16.7 6.4 %collective-permute-start.1 = (bf16[288,256]{1,0:T(8,128)(2,1)S(1)}, bf16[288,256]{1,0:T(8,128)(2,1)S(1)}, u32[]{:S(2)}, u32[]{:S(2)}) collective-permute-start(bf16[288,256]{1,0:T(8,128)(2,1)S(1)} %get-tuple-element.31), channel_id=1, source_target_pairs={{0,32},{8,40},{16,48},{24,56},{32,64},{40,72},{48,80},{56,88},{64,... | collective-permute-start | bytes 442376 | tf_op jit(solution)/shard_map/ppermute | solution.py:34
  17.5 12.3 %collective-permute-start.6 = (bf16[576,256]{1,0:T(8,128)(2,1)S(1)}, bf16[576,256]{1,0:T(8,128)(2,1)S(1)}, u32[]{:S(2)}, u32[]{:S(2)}) collective-permute-start(bf16[576,256]{1,0:T(8,128)(2,1)S(1)} %constant_dynamic-update-slice_fusion.4.refs_9_), channel_id=1, source_target_pairs={{0,24},{8,0},{16,8},{24,16},{32,56},{40,32},{48,40},{56,48},{64,88... | collective-permute-start | bytes 884744 | tf_op jit(solution)/shard_map/ppermute | solution.py:39
  23.1 10.0 %collective-permute-start.3 = (bf16[576,256]{1,0:T(8,128)(2,1)S(1)}, bf16[576,256]{1,0:T(8,128)(2,1)S(1)}, u32[]{:S(2)}, u32[]{:S(2)}) collective-permute-start(bf16[576,256]{1,0:T(8,128)(2,1)S(1)} %constant_dynamic-update-slice_fusion.2.refs_8_), channel_id=1, source_target_pairs={{0,8},{8,16},{16,24},{24,0},{32,40},{40,48},{48,56},{56,32},{64,72... | collective-permute-start | bytes 884744 | tf_op jit(solution)/shard_map/ppermute | solution.py:39
  24.7 12.0 %collective-permute-start.15 = (bf16[576,256]{1,0:T(8,128)(2,1)S(1)}, bf16[576,256]{1,0:T(8,128)(2,1)S(1)}, u32[]{:S(2)}, u32[]{:S(2)}) collective-permute-start(bf16[576,256]{1,0:T(8,128)(2,1)S(1)} %constant_dynamic-update-slice_fusion.4.refs_9_), channel_id=1, source_target_pairs={{0,8},{8,16},{16,24},{24,0},{32,40},{40,48},{48,56},{56,32},{64,72... | collective-permute-start | bytes 884744 | tf_op jit(solution)/shard_map/ppermute | solution.py:39
  26.0 10.8 %collective-permute-start.14 = (bf16[576,256]{1,0:T(8,128)(2,1)S(1)}, bf16[576,256]{1,0:T(8,128)(2,1)S(1)}, u32[]{:S(2)}, u32[]{:S(2)}) collective-permute-start(bf16[576,256]{1,0:T(8,128)(2,1)S(1)} %constant_dynamic-update-slice_fusion.2.refs_8_), channel_id=1, source_target_pairs={{0,24},{8,0},{16,8},{24,16},{32,56},{40,32},{48,40},{56,48},{64,88... | collective-permute-start | bytes 884744 | tf_op jit(solution)/shard_map/ppermute | solution.py:39
  26.8 8.1 %collective-permute-start.9 = (bf16[512,256]{1,0:T(8,128)(2,1)}, bf16[512,256]{1,0:T(8,128)(2,1)S(1)}, u32[]{:S(2)}, u32[]{:S(2)}) collective-permute-start(bf16[512,256]{1,0:T(8,128)(2,1)} %refs_0_.1), channel_id=1, source_target_pairs={{0,4},{1,5},{2,6},{3,7},{4,0},{5,1},{6,2},{7,3},{8,12},{9,13},{10,... | collective-permute-start | bytes 786440 | tf_op jit(solution)/shard_map/ppermute | solution.py:44
  29.8 6.3 %collective-permute-start.10 = (bf16[512,256]{1,0:T(8,128)(2,1)}, bf16[512,256]{1,0:T(8,128)(2,1)S(1)}, u32[]{:S(2)}, u32[]{:S(2)}) collective-permute-start(bf16[512,256]{1,0:T(8,128)(2,1)} %refs_0_.1), channel_id=1, source_target_pairs={{0,1},{1,0},{2,3},{3,2},{4,5},{5,4},{6,7},{7,6},{8,9},{9,8},{10,11... | collective-permute-start | bytes 786440 | tf_op jit(solution)/shard_map/ppermute | solution.py:49
  33.1 8.3 %collective-permute-start.17 = (bf16[576,256]{1,0:T(8,128)(2,1)S(1)}, bf16[576,256]{1,0:T(8,128)(2,1)S(1)}, u32[]{:S(2)}, u32[]{:S(2)}) collective-permute-start(bf16[576,256]{1,0:T(8,128)(2,1)S(1)} %collective-permute-done.6.refs_13_), channel_id=1, source_target_pairs={{0,24},{8,0},{16,8},{24,16},{32,56},{40,32},{48,40},{56,48},{64,88... | collective-permute-start | bytes 884744 | tf_op jit(solution)/shard_map/ppermute | solution.py:39
  34.8 8.0 %collective-permute-start.16 = (bf16[576,256]{1,0:T(8,128)(2,1)S(1)}, bf16[576,256]{1,0:T(8,128)(2,1)S(1)}, u32[]{:S(2)}, u32[]{:S(2)}) collective-permute-start(bf16[576,256]{1,0:T(8,128)(2,1)S(1)} %collective-permute-done.3.refs_10_), channel_id=1, source_target_pairs={{0,8},{8,16},{16,24},{24,0},{32,40},{40,48},{48,56},{56,32},{64,72... | collective-permute-start | bytes 884744 | tf_op jit(solution)/shard_map/ppermute | solution.py:39
  36.1 1.7 %collective-permute-start.13 = (bf16[512,256]{1,0:T(8,128)(2,1)S(1)}, bf16[512,256]{1,0:T(8,128)(2,1)}, u32[]{:S(2)}, u32[]{:S(2)}) collective-permute-start(bf16[512,256]{1,0:T(8,128)(2,1)S(1)} %collective-permute-done.9.refs_3_), channel_id=1, source_target_pairs={{0,1},{1,0},{2,3},{3,2},{4,5},{5,4},{6,7},{7,6},{8,9},{9,8},{10,11... | collective-permute-start | bytes 786440 | tf_op jit(solution)/shard_map/ppermute | solution.py:49
  36.8 4.7 %collective-permute-start.11 = (bf16[512,256]{1,0:T(8,128)(2,1)S(1)}, bf16[512,256]{1,0:T(8,128)(2,1)}, u32[]{:S(2)}, u32[]{:S(2)}) collective-permute-start(bf16[512,256]{1,0:T(8,128)(2,1)S(1)} %collective-permute-done.7.refs_1_), channel_id=1, source_target_pairs={{0,1},{1,0},{2,3},{3,2},{4,5},{5,4},{6,7},{7,6},{8,9},{9,8},{10,11... | collective-permute-start | bytes 786440 | tf_op jit(solution)/shard_map/ppermute | solution.py:49
  36.8 4.7 %collective-permute-start.12 = (bf16[512,256]{1,0:T(8,128)(2,1)S(1)}, bf16[512,256]{1,0:T(8,128)(2,1)}, u32[]{:S(2)}, u32[]{:S(2)}) collective-permute-start(bf16[512,256]{1,0:T(8,128)(2,1)S(1)} %collective-permute-done.8.refs_2_), channel_id=1, source_target_pairs={{0,1},{1,0},{2,3},{3,2},{4,5},{5,4},{6,7},{7,6},{8,9},{9,8},{10,11... | collective-permute-start | bytes 786440 | tf_op jit(solution)/shard_map/ppermute | solution.py:49

commit v7 on v6

--- a/solution.py
+++ b/solution.py
@@ -132,9 +132,11 @@
         top = jnp.max(top8, axis=0, keepdims=True)
         total8 = sum(totals[t * SLOTS + s] * jnp.exp2(top_s[s] - top) for s in range(SLOTS))
         total = jnp.sum(total8, axis=0, keepdims=True)
-        for c in range(NX * NC):
-            stat[c, t : t + 1, :] = top
-            stat[c, TILES + t : TILES + t + 1, :] = total
+        stat[0, t : t + 1, :] = top
+        stat[0, TILES + t : TILES + t + 1, :] = total
+    block = stat[0, 0 : 2 * TILES, :]
+    for c in range(1, NX * NC):
+        stat[c, 0 : 2 * TILES, :] = block
 
 
 def spend_kernel(groups, stats, expo, tops, spend, logz, acc, topw):

time: 79.9 us -> 80.4 us (level)
  no operation moved by 1% of the time
where the time goes in v7:
time: 80.4 us; the launch traced here: 79.4 us
  blocking collectives  27.5 us (34%)
  starting transfers between devices  26.6 us (33%)
  waiting for transfers between devices  12.3 us (15%)
  Pallas kernels  9.98 us (12%)
  other arithmetic  2.21 us (3%)
    all_to_all x1, blocking collectives, local(): mine = jnp.sum(lax.all_to_all(spend, 'imp', 0, 0), axis=0)  16.1 us
    ppermute x5, starting transfers between devices, shift_z(): return lax.ppermute(v, 'imp', perm)  13.1 us
    all_to_all x1, blocking collectives, local(): stats = lax.all_to_all(stat, 'camp', 0, 0)  11.4 us
    ppermute x6, starting transfers between devices, shift_y(): return lax.ppermute(v, 'imp', perm)  7.15 us
    ppermute x6, waiting for transfers between devices, shift_y(): return lax.ppermute(v, 'imp', perm)  6.74 us
    pallas_call x1, Pallas kernels, local(): pl.pallas_call(stats_kernel, in_specs=[SM] * 2 + [pl.BlockSpec(memory_spa...  6.24 us
    ppermute x3, starting transfers between devices, shift_x(): return lax.ppermute(v, 'camp', perm)  5.79 us
    ppermute x5, waiting for transfers between devices, shift_z(): return lax.ppermute(v, 'imp', perm)  5.04 us
  transfers between devices with their start and end apart: 18, of which 7 were waited for; matrix products, arithmetic and copies ran while one was open for 1% of the time, Pallas kernels for 2%

profile of v7, /device:TPU:8, one launch (start us, length us, event | category | flops | bytes accessed | tf_op | source)
XLA Modules:
  0.0 79.4 jit_solution(10234001229026677697)
XLA Ops:
  0.6 0.0 copy-start
  0.6 0.0 copy-start.1
  0.7 0.9 %fusion.1 = bf16[144,256]{1,0:T(8,128)(2,1)S(1)} fusion(bf16[1,128]{1,0:T(2,128)(2,1)} %bitcast.18, bf16[128,256]{1,0:T(8,128)(2,1)} %param.9), kind=kLoop, calls=%fused_computation.2 | loop fusion | flops 221184 | bytes 139520 | tf_op jit(solution)/shard_map/concatenate | solution.py:190
  1.5 7.2 %collective-permute-start = (bf16[144,256]{1,0:T(8,128)(2,1)S(1)}, bf16[144,256]{1,0:T(8,128)(2,1)S(1)}, u32[]{:S(2)}, u32[]{:S(2)}) collective-permute-start(bf16[144,256]{1,0:T(8,128)(2,1)S(1)} %fusion.1), channel_id=1, source_target_pairs={{0,128},{8,136},{16,144},{24,152},{32,160},{40,168},{48,176},{56,1... | collective-permute-start | bytes 221192 | tf_op jit(solution)/shard_map/ppermute | solution.py:34
  8.7 0.0 collective-permute-start.5
  8.7 2.9 %collective-permute-start.4 = (bf16[144,256]{1,0:T(8,128)(2,1)S(1)}, bf16[144,256]{1,0:T(8,128)(2,1)S(1)}, u32[]{:S(2)}, u32[]{:S(2)}) collective-permute-start(bf16[144,256]{1,0:T(8,128)(2,1)S(1)} %fusion.1), channel_id=1, source_target_pairs={{0,64},{8,72},{16,80},{24,88},{32,96},{40,104},{48,112},{56,120},{... | collective-permute-start | bytes 221192 | tf_op jit(solution)/shard_map/ppermute | solution.py:34
  11.6 2.8 %collective-permute-start.8 = (bf16[512,256]{1,0:T(8,128)(2,1)}, bf16[512,256]{1,0:T(8,128)(2,1)S(1)}, u32[]{:S(2)}, u32[]{:S(2)}) collective-permute-start(bf16[512,256]{1,0:T(8,128)(2,1)} %refs_0_.1), channel_id=1, source_target_pairs={{0,6},{1,7},{2,0},{3,1},{4,2},{5,3},{6,4},{7,5},{8,14},{9,15},{10,... | collective-permute-start | bytes 786440 | tf_op jit(solution)/shard_map/ppermute | solution.py:44
  14.4 0.0 collective-permute-start.7
  14.4 0.0 collective-permute-done
  14.4 2.2 %collective-permute-start.2 = (bf16[288,256]{1,0:T(8,128)(2,1)S(1)}, bf16[288,256]{1,0:T(8,128)(2,1)S(1)}, u32[]{:S(2)}, u32[]{:S(2)}) collective-permute-start(bf16[288,256]{1,0:T(8,128)(2,1)S(1)} %get-tuple-element.31), channel_id=1, source_target_pairs={{0,224},{8,232},{16,240},{24,248},{32,0},{40,8},{48,16},{56,24},{6... | collective-permute-start | bytes 442376 | tf_op jit(solution)/shard_map/ppermute | solution.py:34
  16.7 0.0 collective-permute-done.4
  16.7 0.8 collective-permute-start.1
  17.4 0.0 collective-permute-done.5
  17.5 0.5 collective-permute-start.6
  18.0 5.0 %collective-permute-done.1 = bf16[288,256]{1,0:T(8,128)(2,1)S(1)} collective-permute-done((bf16[288,256]{1,0:T(8,128)(2,1)S(1)}, bf16[288,256]{1,0:T(8,128)(2,1)S(1)}, u32[]{:S(2)}, u32[]{:S(2)}) %collective-permute-start.1) | collective-permute-done | bytes 147488 | tf_op jit(solution)/shard_map/ppermute | solution.py:34
  23.0 0.0 collective-permute-done.2
  23.1 1.7 %collective-permute-start.3 = (bf16[576,256]{1,0:T(8,128)(2,1)S(1)}, bf16[576,256]{1,0:T(8,128)(2,1)S(1)}, u32[]{:S(2)}, u32[]{:S(2)}) collective-permute-start(bf16[576,256]{1,0:T(8,128)(2,1)S(1)} %constant_dynamic-update-slice_fusion.2.refs_8_), channel_id=1, source_target_pairs={{0,8},{8,16},{16,24},{24,0},{32,40},{40,48},{48,56},{56,32},{64,72... | collective-permute-start | bytes 884744 | tf_op jit(solution)/shard_map/ppermute | solution.py:39
  24.7 1.3 %collective-permute-start.15 = (bf16[576,256]{1,0:T(8,128)(2,1)S(1)}, bf16[576,256]{1,0:T(8,128)(2,1)S(1)}, u32[]{:S(2)}, u32[]{:S(2)}) collective-permute-start(bf16[576,256]{1,0:T(8,128)(2,1)S(1)} %constant_dynamic-update-slice_fusion.4.refs_9_), channel_id=1, source_target_pairs={{0,8},{8,16},{16,24},{24,0},{32,40},{40,48},{48,56},{56,32},{64,72... | collective-permute-start | bytes 884744 | tf_op jit(solution)/shard_map/ppermute | solution.py:39
  26.0 0.0 collective-permute-done.8.refs_2_
  26.0 0.7 collective-permute-start.14
  26.8 0.0 collective-permute-done.7.refs_1_
  26.8 3.0 %collective-permute-start.9 = (bf16[512,256]{1,0:T(8,128)(2,1)}, bf16[512,256]{1,0:T(8,128)(2,1)S(1)}, u32[]{:S(2)}, u32[]{:S(2)}) collective-permute-start(bf16[512,256]{1,0:T(8,128)(2,1)} %refs_0_.1), channel_id=1, source_target_pairs={{0,4},{1,5},{2,6},{3,7},{4,0},{5,1},{6,2},{7,3},{8,12},{9,13},{10,... | collective-permute-start | bytes 786440 | tf_op jit(solution)/shard_map/ppermute | solution.py:44
  29.8 0.0 collective-permute-done.6.refs_13_
  29.8 0.0 collective-permute-start.10
  29.8 1.5 %prep.1.groups = s32[145]{0:T(256)S(4)} custom-call(s32[8,32]{1,0:T(8,128)} %bitcast.17, s32[32]{0:T(128)} %bitcast.19), custom_call_target="tpu_custom_call" | custom-call | tf_op jit(solution)/shard_map/prep/pallas_call | solution.py:182
  31.3 0.7 bitcast_convert_fusion.refs_16_
  32.0 1.1 %collective-permute-done.3.refs_10_ = bf16[576,256]{1,0:T(8,128)(2,1)S(1)} collective-permute-done((bf16[576,256]{1,0:T(8,128)(2,1)S(1)}, bf16[576,256]{1,0:T(8,128)(2,1)S(1)}, u32[]{:S(2)}, u32[]{:S(2)}) %collective-permute-start.3) | collective-permute-done | bytes 294944 | tf_op jit(solution)/shard_map/ppermute | solution.py:39
  33.1 1.7 %collective-permute-start.17 = (bf16[576,256]{1,0:T(8,128)(2,1)S(1)}, bf16[576,256]{1,0:T(8,128)(2,1)S(1)}, u32[]{:S(2)}, u32[]{:S(2)}) collective-permute-start(bf16[576,256]{1,0:T(8,128)(2,1)S(1)} %collective-permute-done.6.refs_13_), channel_id=1, source_target_pairs={{0,24},{8,0},{16,8},{24,16},{32,56},{40,32},{48,40},{56,48},{64,88... | collective-permute-start | bytes 884744 | tf_op jit(solution)/shard_map/ppermute | solution.py:39
  34.7 0.1 collective-permute-done.9.refs_3_
  34.8 1.3 %collective-permute-start.16 = (bf16[576,256]{1,0:T(8,128)(2,1)S(1)}, bf16[576,256]{1,0:T(8,128)(2,1)S(1)}, u32[]{:S(2)}, u32[]{:S(2)}) collective-permute-start(bf16[576,256]{1,0:T(8,128)(2,1)S(1)} %collective-permute-done.3.refs_10_), channel_id=1, source_target_pairs={{0,8},{8,16},{16,24},{24,0},{32,40},{40,48},{48,56},{56,32},{64,72... | collective-permute-start | bytes 884744 | tf_op jit(solution)/shard_map/ppermute | solution.py:39
  36.1 0.0 collective-permute-done.10.refs_4_
  36.1 0.0 collective-permute-start.13
  36.1 0.6 collective-permute-done.15.refs_12_
  36.8 0.0 collective-permute-start.11
  36.8 0.0 collective-permute-done.14.refs_11_
  36.8 0.5 collective-permute-start.12
  37.3 0.1 pad_add_fusion.where
  37.3 0.4 collective-permute-done.13.refs_7_
  37.8 3.6 %collective-permute-done.17.refs_15_ = bf16[576,256]{1,0:T(8,128)(2,1)S(1)} collective-permute-done((bf16[576,256]{1,0:T(8,128)(2,1)S(1)}, bf16[576,256]{1,0:T(8,128)(2,1)S(1)}, u32[]{:S(2)}, u32[]{:S(2)}) %collective-permute-start.17) | collective-permute-done | bytes 294944 | tf_op jit(solution)/shard_map/ppermute | solution.py:39
  41.4 0.0 collective-permute-done.11.refs_5_
  41.4 0.0 collective-permute-done.12.refs_6_
  41.4 1.4 %collective-permute-done.16.refs_14_ = bf16[576,256]{1,0:T(8,128)(2,1)S(1)} collective-permute-done((bf16[576,256]{1,0:T(8,128)(2,1)S(1)}, bf16[576,256]{1,0:T(8,128)(2,1)S(1)}, u32[]{:S(2)}, u32[]{:S(2)}) %collective-permute-start.16) | collective-permute-done | bytes 294944 | tf_op jit(solution)/shard_map/ppermute | solution.py:39
  42.8 6.2 %stats.1 = (f32[8,72,128]{2,1,0:T(8,128)S(1)}, f32[288,128,128]{2,1,0:T(8,128)S(1)}, f32[258,8,128]{2,1,0:T(8,128)S(1)}) custom-call(s32[145]{0:T(256)S(4)} %prep.1.groups, s32[4]{0:T(128)S(1)} %pad_add_fusion.where, bf16[512,256]{1,0:T(8,128)(2,1)} %refs_0_.1, bf16[512,256]{1,0:T(8,128)(2,1)S(1)} %collective-permute-done.7.refs_1_, ...), custom_call_target="tpu_custom_call" | custom-call | tf_op jit(solution)/shard_map/stats/pallas_call | solution.py:211
  49.1 11.4 %all_to_all.14.stats = f32[8,72,128]{2,1,0:T(8,128)S(1)} all-to-all(f32[8,72,128]{2,1,0:T(8,128)S(1)} %get-tuple-element.25), channel_id=1, replica_groups=mesh['imp'=32,'camp'=8] {'camp'}, dimensions={0} | all-to-all | bytes 589824 | tf_op jit(solution)/shard_map/all_to_all | solution.py:231
  60.5 2.2 %spend.1 = (f32[32,128]{1,0:T(8,128)S(1)}, f32[32,128]{1,0:T(8,128)}) custom-call(s32[145]{0:T(256)S(4)} %prep.1.groups, f32[8,72,128]{2,1,0:T(8,128)S(1)} %all_to_all.14.stats, f32[288,128,128]{2,1,0:T(8,128)S(1)} %get-tuple-element.26.expo, f32[258,8,128]{2,1,0:T(8,128)S(1)} %get-tuple-element.27.tops), custom_call_target="tpu_custom_call" | custom-call | tf_op jit(solution)/shard_map/spend/pallas_call | solution.py:233
  62.7 16.1 %all_to_all.15 = f32[32,1,128]{2,1,0:T(1,128)S(1)} all-to-all(f32[32,1,128]{2,1,0:T(1,128)S(1)} %bitcast.16), channel_id=1, replica_groups=mesh['imp'=32,'camp'=8] {'imp'}, dimensions={0} | all-to-all | bytes 32768 | tf_op jit(solution)/shard_map/all_to_all | solution.py:249
  78.8 0.1 reduce_sum.9
  78.9 0.5 divide_add_fusion
  (8 shorter events, 0.1 us)
Async XLA Ops:
  0.6 78.2 %copy-start = (bf16[128]{0:T(256)(128)(2,1)S(1)}, bf16[128]{0:T(256)(128)(2,1)}, u32[]{:S(2)}) copy-start(bf16[128]{0:T(256)(128)(2,1)} %param.10) | copy-start | bytes 772
  0.6 78.2 %copy-start.1 = (f32[128]{0:T(128)S(1)}, f32[128]{0:T(128)}, u32[]{:S(2)}) copy-start(f32[128]{0:T(128)} %param.11) | copy-start | bytes 1540
  1.5 12.9 %collective-permute-start = (bf16[144,256]{1,0:T(8,128)(2,1)S(1)}, bf16[144,256]{1,0:T(8,128)(2,1)S(1)}, u32[]{:S(2)}, u32[]{:S(2)}) collective-permute-start(bf16[144,256]{1,0:T(8,128)(2,1)S(1)} %fusion.1), channel_id=1, source_target_pairs={{0,128},{8,136},{16,144},{24,152},{32,160},{40,168},{48,176},{56,1... | collective-permute-start | bytes 221192 | tf_op jit(solution)/shard_map/ppermute | solution.py:34
  8.7 8.7 %collective-permute-start.5 = (bf16[144,256]{1,0:T(8,128)(2,1)S(1)}, bf16[144,256]{1,0:T(8,128)(2,1)S(1)}, u32[]{:S(2)}, u32[]{:S(2)}) collective-permute-start(bf16[144,256]{1,0:T(8,128)(2,1)S(1)} %fusion.1), channel_id=1, source_target_pairs={{0,192},{8,200},{16,208},{24,216},{32,224},{40,232},{48,240},{56,2... | collective-permute-start | bytes 221192 | tf_op jit(solution)/shard_map/ppermute | solution.py:34
  8.7 7.9 %collective-permute-start.4 = (bf16[144,256]{1,0:T(8,128)(2,1)S(1)}, bf16[144,256]{1,0:T(8,128)(2,1)S(1)}, u32[]{:S(2)}, u32[]{:S(2)}) collective-permute-start(bf16[144,256]{1,0:T(8,128)(2,1)S(1)} %fusion.1), channel_id=1, source_target_pairs={{0,64},{8,72},{16,80},{24,88},{32,96},{40,104},{48,112},{56,120},{... | collective-permute-start | bytes 221192 | tf_op jit(solution)/shard_map/ppermute | solution.py:34
  11.6 14.4 %collective-permute-start.8 = (bf16[512,256]{1,0:T(8,128)(2,1)}, bf16[512,256]{1,0:T(8,128)(2,1)S(1)}, u32[]{:S(2)}, u32[]{:S(2)}) collective-permute-start(bf16[512,256]{1,0:T(8,128)(2,1)} %refs_0_.1), channel_id=1, source_target_pairs={{0,6},{1,7},{2,0},{3,1},{4,2},{5,3},{6,4},{7,5},{8,14},{9,15},{10,... | collective-permute-start | bytes 786440 | tf_op jit(solution)/shard_map/ppermute | solution.py:44
  14.4 12.4 %collective-permute-start.7 = (bf16[512,256]{1,0:T(8,128)(2,1)}, bf16[512,256]{1,0:T(8,128)(2,1)S(1)}, u32[]{:S(2)}, u32[]{:S(2)}) collective-permute-start(bf16[512,256]{1,0:T(8,128)(2,1)} %refs_0_.1), channel_id=1, source_target_pairs={{0,2},{1,3},{2,4},{3,5},{4,6},{5,7},{6,0},{7,1},{8,10},{9,11},{10,... | collective-permute-start | bytes 786440 | tf_op jit(solution)/shard_map/ppermute | solution.py:44
  14.4 8.6 %collective-permute-start.2 = (bf16[288,256]{1,0:T(8,128)(2,1)S(1)}, bf16[288,256]{1,0:T(8,128)(2,1)S(1)}, u32[]{:S(2)}, u32[]{:S(2)}) collective-permute-start(bf16[288,256]{1,0:T(8,128)(2,1)S(1)} %get-tuple-element.31), channel_id=1, source_target_pairs={{0,224},{8,232},{16,240},{24,248},{32,0},{40,8},{48,16},{56,24},{6... | collective-permute-start | bytes 442376 | tf_op jit(solution)/shard_map/ppermute | solution.py:34
  16.7 6.4 %collective-permute-start.1 = (bf16[288,256]{1,0:T(8,128)(2,1)S(1)}, bf16[288,256]{1,0:T(8,128)(2,1)S(1)}, u32[]{:S(2)}, u32[]{:S(2)}) collective-permute-start(bf16[288,256]{1,0:T(8,128)(2,1)S(1)} %get-tuple-element.31), channel_id=1, source_target_pairs={{0,32},{8,40},{16,48},{24,56},{32,64},{40,72},{48,80},{56,88},{64,... | collective-permute-start | bytes 442376 | tf_op jit(solution)/shard_map/ppermute | solution.py:34
  17.5 12.3 %collective-permute-start.6 = (bf16[576,256]{1,0:T(8,128)(2,1)S(1)}, bf16[576,256]{1,0:T(8,128)(2,1)S(1)}, u32[]{:S(2)}, u32[]{:S(2)}) collective-permute-start(bf16[576,256]{1,0:T(8,128)(2,1)S(1)} %constant_dynamic-update-slice_fusion.4.refs_9_), channel_id=1, source_target_pairs={{0,24},{8,0},{16,8},{24,16},{32,56},{40,32},{48,40},{56,48},{64,88... | collective-permute-start | bytes 884744 | tf_op jit(solution)/shard_map/ppermute | solution.py:39
  23.1 10.0 %collective-permute-start.3 = (bf16[576,256]{1,0:T(8,128)(2,1)S(1)}, bf16[576,256]{1,0:T(8,128)(2,1)S(1)}, u32[]{:S(2)}, u32[]{:S(2)}) collective-permute-start(bf16[576,256]{1,0:T(8,128)(2,1)S(1)} %constant_dynamic-update-slice_fusion.2.refs_8_), channel_id=1, source_target_pairs={{0,8},{8,16},{16,24},{24,0},{32,40},{40,48},{48,56},{56,32},{64,72... | collective-permute-start | bytes 884744 | tf_op jit(solution)/shard_map/ppermute | solution.py:39
  24.7 12.0 %collective-permute-start.15 = (bf16[576,256]{1,0:T(8,128)(2,1)S(1)}, bf16[576,256]{1,0:T(8,128)(2,1)S(1)}, u32[]{:S(2)}, u32[]{:S(2)}) collective-permute-start(bf16[576,256]{1,0:T(8,128)(2,1)S(1)} %constant_dynamic-update-slice_fusion.4.refs_9_), channel_id=1, source_target_pairs={{0,8},{8,16},{16,24},{24,0},{32,40},{40,48},{48,56},{56,32},{64,72... | collective-permute-start | bytes 884744 | tf_op jit(solution)/shard_map/ppermute | solution.py:39
  26.0 10.8 %collective-permute-start.14 = (bf16[576,256]{1,0:T(8,128)(2,1)S(1)}, bf16[576,256]{1,0:T(8,128)(2,1)S(1)}, u32[]{:S(2)}, u32[]{:S(2)}) collective-permute-start(bf16[576,256]{1,0:T(8,128)(2,1)S(1)} %constant_dynamic-update-slice_fusion.2.refs_8_), channel_id=1, source_target_pairs={{0,24},{8,0},{16,8},{24,16},{32,56},{40,32},{48,40},{56,48},{64,88... | collective-permute-start | bytes 884744 | tf_op jit(solution)/shard_map/ppermute | solution.py:39
  26.8 8.1 %collective-permute-start.9 = (bf16[512,256]{1,0:T(8,128)(2,1)}, bf16[512,256]{1,0:T(8,128)(2,1)S(1)}, u32[]{:S(2)}, u32[]{:S(2)}) collective-permute-start(bf16[512,256]{1,0:T(8,128)(2,1)} %refs_0_.1), channel_id=1, source_target_pairs={{0,4},{1,5},{2,6},{3,7},{4,0},{5,1},{6,2},{7,3},{8,12},{9,13},{10,... | collective-permute-start | bytes 786440 | tf_op jit(solution)/shard_map/ppermute | solution.py:44
  29.8 6.3 %collective-permute-start.10 = (bf16[512,256]{1,0:T(8,128)(2,1)}, bf16[512,256]{1,0:T(8,128)(2,1)S(1)}, u32[]{:S(2)}, u32[]{:S(2)}) collective-permute-start(bf16[512,256]{1,0:T(8,128)(2,1)} %refs_0_.1), channel_id=1, source_target_pairs={{0,1},{1,0},{2,3},{3,2},{4,5},{5,4},{6,7},{7,6},{8,9},{9,8},{10,11... | collective-permute-start | bytes 786440 | tf_op jit(solution)/shard_map/ppermute | solution.py:49
  33.1 8.3 %collective-permute-start.17 = (bf16[576,256]{1,0:T(8,128)(2,1)S(1)}, bf16[576,256]{1,0:T(8,128)(2,1)S(1)}, u32[]{:S(2)}, u32[]{:S(2)}) collective-permute-start(bf16[576,256]{1,0:T(8,128)(2,1)S(1)} %collective-permute-done.6.refs_13_), channel_id=1, source_target_pairs={{0,24},{8,0},{16,8},{24,16},{32,56},{40,32},{48,40},{56,48},{64,88... | collective-permute-start | bytes 884744 | tf_op jit(solution)/shard_map/ppermute | solution.py:39
  34.8 8.0 %collective-permute-start.16 = (bf16[576,256]{1,0:T(8,128)(2,1)S(1)}, bf16[576,256]{1,0:T(8,128)(2,1)S(1)}, u32[]{:S(2)}, u32[]{:S(2)}) collective-permute-start(bf16[576,256]{1,0:T(8,128)(2,1)S(1)} %collective-permute-done.3.refs_10_), channel_id=1, source_target_pairs={{0,8},{8,16},{16,24},{24,0},{32,40},{40,48},{48,56},{56,32},{64,72... | collective-permute-start | bytes 884744 | tf_op jit(solution)/shard_map/ppermute | solution.py:39
  36.1 1.7 %collective-permute-start.13 = (bf16[512,256]{1,0:T(8,128)(2,1)S(1)}, bf16[512,256]{1,0:T(8,128)(2,1)}, u32[]{:S(2)}, u32[]{:S(2)}) collective-permute-start(bf16[512,256]{1,0:T(8,128)(2,1)S(1)} %collective-permute-done.9.refs_3_), channel_id=1, source_target_pairs={{0,1},{1,0},{2,3},{3,2},{4,5},{5,4},{6,7},{7,6},{8,9},{9,8},{10,11... | collective-permute-start | bytes 786440 | tf_op jit(solution)/shard_map/ppermute | solution.py:49
  36.8 4.7 %collective-permute-start.11 = (bf16[512,256]{1,0:T(8,128)(2,1)S(1)}, bf16[512,256]{1,0:T(8,128)(2,1)}, u32[]{:S(2)}, u32[]{:S(2)}) collective-permute-start(bf16[512,256]{1,0:T(8,128)(2,1)S(1)} %collective-permute-done.7.refs_1_), channel_id=1, source_target_pairs={{0,1},{1,0},{2,3},{3,2},{4,5},{5,4},{6,7},{7,6},{8,9},{9,8},{10,11... | collective-permute-start | bytes 786440 | tf_op jit(solution)/shard_map/ppermute | solution.py:49
  36.8 4.7 %collective-permute-start.12 = (bf16[512,256]{1,0:T(8,128)(2,1)S(1)}, bf16[512,256]{1,0:T(8,128)(2,1)}, u32[]{:S(2)}, u32[]{:S(2)}) collective-permute-start(bf16[512,256]{1,0:T(8,128)(2,1)S(1)} %collective-permute-done.8.refs_2_), channel_id=1, source_target_pairs={{0,1},{1,0},{2,3},{3,2},{4,5},{5,4},{6,7},{7,6},{8,9},{9,8},{10,11... | collective-permute-start | bytes 786440 | tf_op jit(solution)/shard_map/ppermute | solution.py:49

commit v8 on v5

--- a/solution.py
+++ b/solution.py
@@ -21,7 +21,7 @@
 LN2 = math.log(2.0)
 SCALE2 = 3.0 / math.sqrt(D) * LOG2E
 VMEM_LIMIT = 16 * 1024 * 1024
-UNROLL = 16
+UNROLL = 20
 GROUPS = TILES * SLOTS // 2 + UNROLL
 LAST = GROUPS
 FIRST, SECOND = 1024, 1024 * 64

time: 80.4 us -> 80.5 us (level)
  Pallas kernels: 8.93 us -> 9.82 us
    all_to_all x1, blocking collectives: 11.7 us -> 10.8 us  [local(): stats = lax.all_to_all(stat, 'camp', 0, 0)]
where the time goes in v8:
time: 80.5 us; the launch traced here: 80.2 us
  starting transfers between devices  27.1 us (34%)
  blocking collectives  26.7 us (33%)
  waiting for transfers between devices  13.5 us (17%)
  Pallas kernels  9.82 us (12%)
  other arithmetic  2.21 us (3%)
    all_to_all x1, blocking collectives, local(): mine = jnp.sum(lax.all_to_all(spend, 'imp', 0, 0), axis=0)  15.9 us
    ppermute x5, starting transfers between devices, shift_z(): return lax.ppermute(v, 'imp', perm)  14.9 us
    all_to_all x1, blocking collectives, local(): stats = lax.all_to_all(stat, 'camp', 0, 0)  10.8 us
    ppermute x6, starting transfers between devices, shift_y(): return lax.ppermute(v, 'imp', perm)  6.23 us
    pallas_call x1, Pallas kernels, local(): pl.pallas_call(stats_kernel, in_specs=[SM] * 2 + [pl.BlockSpec(memory_spa...  6.03 us
    ppermute x5, waiting for transfers between devices, shift_z(): return lax.ppermute(v, 'imp', perm)  5.97 us
    ppermute x3, starting transfers between devices, shift_x(): return lax.ppermute(v, 'camp', perm)  5.14 us
    ppermute x6, waiting for transfers between devices, shift_y(): return lax.ppermute(v, 'imp', perm)  3.88 us
  transfers between devices with their start and end apart: 18, of which 7 were waited for; matrix products, arithmetic and copies ran while one was open for 1% of the time, Pallas kernels for 2%

profile of v8, /device:TPU:8, one launch (start us, length us, event | category | flops | bytes accessed | tf_op | source)
XLA Modules:
  0.0 80.2 jit_solution(14714750485371523119)
XLA Ops:
  0.6 0.0 copy-start
  0.6 0.0 copy-start.1
  0.7 0.9 %fusion.1 = bf16[144,256]{1,0:T(8,128)(2,1)S(1)} fusion(bf16[1,128]{1,0:T(2,128)(2,1)} %bitcast.18, bf16[128,256]{1,0:T(8,128)(2,1)} %param.9), kind=kLoop, calls=%fused_computation.2 | loop fusion | flops 221184 | bytes 139520 | tf_op jit(solution)/shard_map/concatenate | solution.py:188
  1.5 7.2 %collective-permute-start = (bf16[144,256]{1,0:T(8,128)(2,1)S(1)}, bf16[144,256]{1,0:T(8,128)(2,1)S(1)}, u32[]{:S(2)}, u32[]{:S(2)}) collective-permute-start(bf16[144,256]{1,0:T(8,128)(2,1)S(1)} %fusion.1), channel_id=1, source_target_pairs={{0,128},{8,136},{16,144},{24,152},{32,160},{40,168},{48,176},{56,1... | collective-permute-start | bytes 221192 | tf_op jit(solution)/shard_map/ppermute | solution.py:34
  8.7 0.0 collective-permute-start.5
  8.7 2.9 %collective-permute-start.4 = (bf16[144,256]{1,0:T(8,128)(2,1)S(1)}, bf16[144,256]{1,0:T(8,128)(2,1)S(1)}, u32[]{:S(2)}, u32[]{:S(2)}) collective-permute-start(bf16[144,256]{1,0:T(8,128)(2,1)S(1)} %fusion.1), channel_id=1, source_target_pairs={{0,64},{8,72},{16,80},{24,88},{32,96},{40,104},{48,112},{56,120},{... | collective-permute-start | bytes 221192 | tf_op jit(solution)/shard_map/ppermute | solution.py:34
  11.6 0.2 collective-permute-done
  11.8 2.8 %collective-permute-start.8 = (bf16[512,256]{1,0:T(8,128)(2,1)}, bf16[512,256]{1,0:T(8,128)(2,1)S(1)}, u32[]{:S(2)}, u32[]{:S(2)}) collective-permute-start(bf16[512,256]{1,0:T(8,128)(2,1)} %refs_0_.1), channel_id=1, source_target_pairs={{0,6},{1,7},{2,0},{3,1},{4,2},{5,3},{6,4},{7,5},{8,14},{9,15},{10,... | collective-permute-start | bytes 786440 | tf_op jit(solution)/shard_map/ppermute | solution.py:44
  14.6 0.0 collective-permute-start.7
  14.6 4.8 %collective-permute-start.2 = (bf16[288,256]{1,0:T(8,128)(2,1)S(1)}, bf16[288,256]{1,0:T(8,128)(2,1)S(1)}, u32[]{:S(2)}, u32[]{:S(2)}) collective-permute-start(bf16[288,256]{1,0:T(8,128)(2,1)S(1)} %get-tuple-element.33), channel_id=1, source_target_pairs={{0,224},{8,232},{16,240},{24,248},{32,0},{40,8},{48,16},{56,24},{6... | collective-permute-start | bytes 442376 | tf_op jit(solution)/shard_map/ppermute | solution.py:34
  19.4 0.0 collective-permute-done.4
  19.4 0.0 collective-permute-start.1
  19.4 0.0 collective-permute-done.5
  19.5 0.5 collective-permute-start.6
  20.0 5.8 %collective-permute-done.1 = bf16[288,256]{1,0:T(8,128)(2,1)S(1)} collective-permute-done((bf16[288,256]{1,0:T(8,128)(2,1)S(1)}, bf16[288,256]{1,0:T(8,128)(2,1)S(1)}, u32[]{:S(2)}, u32[]{:S(2)}) %collective-permute-start.1) | collective-permute-done | bytes 147488 | tf_op jit(solution)/shard_map/ppermute | solution.py:34
  25.8 0.0 collective-permute-done.2
  25.8 1.7 %collective-permute-start.3 = (bf16[576,256]{1,0:T(8,128)(2,1)S(1)}, bf16[576,256]{1,0:T(8,128)(2,1)S(1)}, u32[]{:S(2)}, u32[]{:S(2)}) collective-permute-start(bf16[576,256]{1,0:T(8,128)(2,1)S(1)} %constant_dynamic-update-slice_fusion.2.refs_8_), channel_id=1, source_target_pairs={{0,8},{8,16},{16,24},{24,0},{32,40},{40,48},{48,56},{56,32},{64,72... | collective-permute-start | bytes 884744 | tf_op jit(solution)/shard_map/ppermute | solution.py:39
  27.5 1.3 %collective-permute-start.15 = (bf16[576,256]{1,0:T(8,128)(2,1)S(1)}, bf16[576,256]{1,0:T(8,128)(2,1)S(1)}, u32[]{:S(2)}, u32[]{:S(2)}) collective-permute-start(bf16[576,256]{1,0:T(8,128)(2,1)S(1)} %constant_dynamic-update-slice_fusion.4.refs_9_), channel_id=1, source_target_pairs={{0,8},{8,16},{16,24},{24,0},{32,40},{40,48},{48,56},{56,32},{64,72... | collective-permute-start | bytes 884744 | tf_op jit(solution)/shard_map/ppermute | solution.py:39
  28.8 0.0 collective-permute-done.8.refs_2_
  28.8 0.7 collective-permute-start.14
  29.5 0.0 collective-permute-done.7.refs_1_
  29.5 0.0 collective-permute-start.10
  29.5 0.0 collective-permute-done.6.refs_13_
  29.5 2.4 %collective-permute-start.9 = (bf16[512,256]{1,0:T(8,128)(2,1)}, bf16[512,256]{1,0:T(8,128)(2,1)S(1)}, u32[]{:S(2)}, u32[]{:S(2)}) collective-permute-start(bf16[512,256]{1,0:T(8,128)(2,1)} %refs_0_.1), channel_id=1, source_target_pairs={{0,4},{1,5},{2,6},{3,7},{4,0},{5,1},{6,2},{7,3},{8,12},{9,13},{10,... | collective-permute-start | bytes 786440 | tf_op jit(solution)/shard_map/ppermute | solution.py:44
  31.9 1.5 %prep.1.groups = s32[149]{0:T(256)S(4)} custom-call(s32[8,32]{1,0:T(8,128)} %bitcast.17, s32[32]{0:T(128)} %bitcast.19), custom_call_target="tpu_custom_call" | custom-call | tf_op jit(solution)/shard_map/prep/pallas_call | solution.py:180
  33.4 0.7 bitcast_convert_fusion.refs_16_
  34.1 0.9 %collective-permute-done.3.refs_10_ = bf16[576,256]{1,0:T(8,128)(2,1)S(1)} collective-permute-done((bf16[576,256]{1,0:T(8,128)(2,1)S(1)}, bf16[576,256]{1,0:T(8,128)(2,1)S(1)}, u32[]{:S(2)}, u32[]{:S(2)}) %collective-permute-start.3) | collective-permute-done | bytes 294944 | tf_op jit(solution)/shard_map/ppermute | solution.py:39
  35.1 1.7 %collective-permute-start.17 = (bf16[576,256]{1,0:T(8,128)(2,1)S(1)}, bf16[576,256]{1,0:T(8,128)(2,1)S(1)}, u32[]{:S(2)}, u32[]{:S(2)}) collective-permute-start(bf16[576,256]{1,0:T(8,128)(2,1)S(1)} %collective-permute-done.6.refs_13_), channel_id=1, source_target_pairs={{0,24},{8,0},{16,8},{24,16},{32,56},{40,32},{48,40},{56,48},{64,88... | collective-permute-start | bytes 884744 | tf_op jit(solution)/shard_map/ppermute | solution.py:39
  36.8 0.0 collective-permute-done.10.refs_4_
  36.8 0.3 collective-permute-start.16
  37.1 2.9 %collective-permute-done.9.refs_3_ = bf16[512,256]{1,0:T(8,128)(2,1)S(1)} collective-permute-done((bf16[512,256]{1,0:T(8,128)(2,1)}, bf16[512,256]{1,0:T(8,128)(2,1)S(1)}, u32[]{:S(2)}, u32[]{:S(2)}) %collective-permute-start.9) | collective-permute-done | bytes 262176 | tf_op jit(solution)/shard_map/ppermute | solution.py:44
  40.0 0.0 collective-permute-start.13
  40.0 0.0 collective-permute-done.15.refs_12_
  40.0 0.5 collective-permute-start.11
  40.5 0.0 collective-permute-done.14.refs_11_
  40.5 0.3 collective-permute-start.12
  40.8 0.1 pad_add_fusion.where
  40.8 0.8 collective-permute-done.13.refs_7_
  41.6 1.5 %collective-permute-done.17.refs_15_ = bf16[576,256]{1,0:T(8,128)(2,1)S(1)} collective-permute-done((bf16[576,256]{1,0:T(8,128)(2,1)S(1)}, bf16[576,256]{1,0:T(8,128)(2,1)S(1)}, u32[]{:S(2)}, u32[]{:S(2)}) %collective-permute-start.17) | collective-permute-done | bytes 294944 | tf_op jit(solution)/shard_map/ppermute | solution.py:39
  43.2 0.0 collective-permute-done.11.refs_5_
  43.2 0.0 collective-permute-done.12.refs_6_
  43.2 1.4 %collective-permute-done.16.refs_14_ = bf16[576,256]{1,0:T(8,128)(2,1)S(1)} collective-permute-done((bf16[576,256]{1,0:T(8,128)(2,1)S(1)}, bf16[576,256]{1,0:T(8,128)(2,1)S(1)}, u32[]{:S(2)}, u32[]{:S(2)}) %collective-permute-start.16) | collective-permute-done | bytes 294944 | tf_op jit(solution)/shard_map/ppermute | solution.py:39
  44.6 6.0 %stats.1 = (f32[8,72,128]{2,1,0:T(8,128)S(1)}, f32[296,128,128]{2,1,0:T(8,128)S(1)}, f32[258,8,128]{2,1,0:T(8,128)S(1)}) custom-call(s32[149]{0:T(256)S(4)} %prep.1.groups, s32[4]{0:T(128)S(1)} %pad_add_fusion.where, bf16[512,256]{1,0:T(8,128)(2,1)} %refs_0_.1, bf16[512,256]{1,0:T(8,128)(2,1)S(1)} %collective-permute-done.7.refs_1_, ...), custom_call_target="tpu_custom_call" | custom-call | tf_op jit(solution)/shard_map/stats/pallas_call | solution.py:209
  50.6 10.8 %all_to_all.14.stats = f32[8,72,128]{2,1,0:T(8,128)S(1)} all-to-all(f32[8,72,128]{2,1,0:T(8,128)S(1)} %get-tuple-element.27), channel_id=1, replica_groups=mesh['imp'=32,'camp'=8] {'camp'}, dimensions={0} | all-to-all | bytes 589824 | tf_op jit(solution)/shard_map/all_to_all | solution.py:229
  61.4 2.3 %spend.1 = (f32[32,128]{1,0:T(8,128)S(1)}, f32[32,128]{1,0:T(8,128)}) custom-call(s32[149]{0:T(256)S(4)} %prep.1.groups, f32[8,72,128]{2,1,0:T(8,128)S(1)} %all_to_all.14.stats, f32[296,128,128]{2,1,0:T(8,128)S(1)} %get-tuple-element.28.expo, f32[258,8,128]{2,1,0:T(8,128)S(1)} %get-tuple-element.29.tops), custom_call_target="tpu_custom_call" | custom-call | tf_op jit(solution)/shard_map/spend/pallas_call | solution.py:231
  63.7 15.9 %all_to_all.15 = f32[32,1,128]{2,1,0:T(1,128)S(1)} all-to-all(f32[32,1,128]{2,1,0:T(1,128)S(1)} %bitcast.16), channel_id=1, replica_groups=mesh['imp'=32,'camp'=8] {'imp'}, dimensions={0} | all-to-all | bytes 32768 | tf_op jit(solution)/shard_map/all_to_all | solution.py:247
  79.6 0.1 reduce_sum.9
  79.7 0.5 divide_add_fusion
  (8 shorter events, 0.1 us)
Async XLA Ops:
  0.6 79.0 %copy-start = (bf16[128]{0:T(256)(128)(2,1)S(1)}, bf16[128]{0:T(256)(128)(2,1)}, u32[]{:S(2)}) copy-start(bf16[128]{0:T(256)(128)(2,1)} %param.10) | copy-start | bytes 772
  0.6 79.0 %copy-start.1 = (f32[128]{0:T(128)S(1)}, f32[128]{0:T(128)}, u32[]{:S(2)}) copy-start(f32[128]{0:T(128)} %param.11) | copy-start | bytes 1540
  1.5 10.3 %collective-permute-start = (bf16[144,256]{1,0:T(8,128)(2,1)S(1)}, bf16[144,256]{1,0:T(8,128)(2,1)S(1)}, u32[]{:S(2)}, u32[]{:S(2)}) collective-permute-start(bf16[144,256]{1,0:T(8,128)(2,1)S(1)} %fusion.1), channel_id=1, source_target_pairs={{0,128},{8,136},{16,144},{24,152},{32,160},{40,168},{48,176},{56,1... | collective-permute-start | bytes 221192 | tf_op jit(solution)/shard_map/ppermute | solution.py:34
  8.7 10.7 %collective-permute-start.5 = (bf16[144,256]{1,0:T(8,128)(2,1)S(1)}, bf16[144,256]{1,0:T(8,128)(2,1)S(1)}, u32[]{:S(2)}, u32[]{:S(2)}) collective-permute-start(bf16[144,256]{1,0:T(8,128)(2,1)S(1)} %fusion.1), channel_id=1, source_target_pairs={{0,192},{8,200},{16,208},{24,216},{32,224},{40,232},{48,240},{56,2... | collective-permute-start | bytes 221192 | tf_op jit(solution)/shard_map/ppermute | solution.py:34
  8.7 10.7 %collective-permute-start.4 = (bf16[144,256]{1,0:T(8,128)(2,1)S(1)}, bf16[144,256]{1,0:T(8,128)(2,1)S(1)}, u32[]{:S(2)}, u32[]{:S(2)}) collective-permute-start(bf16[144,256]{1,0:T(8,128)(2,1)S(1)} %fusion.1), channel_id=1, source_target_pairs={{0,64},{8,72},{16,80},{24,88},{32,96},{40,104},{48,112},{56,120},{... | collective-permute-start | bytes 221192 | tf_op jit(solution)/shard_map/ppermute | solution.py:34
  11.8 17.0 %collective-permute-start.8 = (bf16[512,256]{1,0:T(8,128)(2,1)}, bf16[512,256]{1,0:T(8,128)(2,1)S(1)}, u32[]{:S(2)}, u32[]{:S(2)}) collective-permute-start(bf16[512,256]{1,0:T(8,128)(2,1)} %refs_0_.1), channel_id=1, source_target_pairs={{0,6},{1,7},{2,0},{3,1},{4,2},{5,3},{6,4},{7,5},{8,14},{9,15},{10,... | collective-permute-start | bytes 786440 | tf_op jit(solution)/shard_map/ppermute | solution.py:44
  14.6 14.9 %collective-permute-start.7 = (bf16[512,256]{1,0:T(8,128)(2,1)}, bf16[512,256]{1,0:T(8,128)(2,1)S(1)}, u32[]{:S(2)}, u32[]{:S(2)}) collective-permute-start(bf16[512,256]{1,0:T(8,128)(2,1)} %refs_0_.1), channel_id=1, source_target_pairs={{0,2},{1,3},{2,4},{3,5},{4,6},{5,7},{6,0},{7,1},{8,10},{9,11},{10,... | collective-permute-start | bytes 786440 | tf_op jit(solution)/shard_map/ppermute | solution.py:44
  14.6 11.2 %collective-permute-start.2 = (bf16[288,256]{1,0:T(8,128)(2,1)S(1)}, bf16[288,256]{1,0:T(8,128)(2,1)S(1)}, u32[]{:S(2)}, u32[]{:S(2)}) collective-permute-start(bf16[288,256]{1,0:T(8,128)(2,1)S(1)} %get-tuple-element.33), channel_id=1, source_target_pairs={{0,224},{8,232},{16,240},{24,248},{32,0},{40,8},{48,16},{56,24},{6... | collective-permute-start | bytes 442376 | tf_op jit(solution)/shard_map/ppermute | solution.py:34
  19.4 6.4 %collective-permute-start.1 = (bf16[288,256]{1,0:T(8,128)(2,1)S(1)}, bf16[288,256]{1,0:T(8,128)(2,1)S(1)}, u32[]{:S(2)}, u32[]{:S(2)}) collective-permute-start(bf16[288,256]{1,0:T(8,128)(2,1)S(1)} %get-tuple-element.33), channel_id=1, source_target_pairs={{0,32},{8,40},{16,48},{24,56},{32,64},{40,72},{48,80},{56,88},{64,... | collective-permute-start | bytes 442376 | tf_op jit(solution)/shard_map/ppermute | solution.py:34
  19.5 10.1 %collective-permute-start.6 = (bf16[576,256]{1,0:T(8,128)(2,1)S(1)}, bf16[576,256]{1,0:T(8,128)(2,1)S(1)}, u32[]{:S(2)}, u32[]{:S(2)}) collective-permute-start(bf16[576,256]{1,0:T(8,128)(2,1)S(1)} %constant_dynamic-update-slice_fusion.4.refs_9_), channel_id=1, source_target_pairs={{0,24},{8,0},{16,8},{24,16},{32,56},{40,32},{48,40},{56,48},{64,88... | collective-permute-start | bytes 884744 | tf_op jit(solution)/shard_map/ppermute | solution.py:39
  25.8 9.2 %collective-permute-start.3 = (bf16[576,256]{1,0:T(8,128)(2,1)S(1)}, bf16[576,256]{1,0:T(8,128)(2,1)S(1)}, u32[]{:S(2)}, u32[]{:S(2)}) collective-permute-start(bf16[576,256]{1,0:T(8,128)(2,1)S(1)} %constant_dynamic-update-slice_fusion.2.refs_8_), channel_id=1, source_target_pairs={{0,8},{8,16},{16,24},{24,0},{32,40},{40,48},{48,56},{56,32},{64,72... | collective-permute-start | bytes 884744 | tf_op jit(solution)/shard_map/ppermute | solution.py:39
  27.5 12.5 %collective-permute-start.15 = (bf16[576,256]{1,0:T(8,128)(2,1)S(1)}, bf16[576,256]{1,0:T(8,128)(2,1)S(1)}, u32[]{:S(2)}, u32[]{:S(2)}) collective-permute-start(bf16[576,256]{1,0:T(8,128)(2,1)S(1)} %constant_dynamic-update-slice_fusion.4.refs_9_), channel_id=1, source_target_pairs={{0,8},{8,16},{16,24},{24,0},{32,40},{40,48},{48,56},{56,32},{64,72... | collective-permute-start | bytes 884744 | tf_op jit(solution)/shard_map/ppermute | solution.py:39
  28.8 11.7 %collective-permute-start.14 = (bf16[576,256]{1,0:T(8,128)(2,1)S(1)}, bf16[576,256]{1,0:T(8,128)(2,1)S(1)}, u32[]{:S(2)}, u32[]{:S(2)}) collective-permute-start(bf16[576,256]{1,0:T(8,128)(2,1)S(1)} %constant_dynamic-update-slice_fusion.2.refs_8_), channel_id=1, source_target_pairs={{0,24},{8,0},{16,8},{24,16},{32,56},{40,32},{48,40},{56,48},{64,88... | collective-permute-start | bytes 884744 | tf_op jit(solution)/shard_map/ppermute | solution.py:39
  29.5 7.3 %collective-permute-start.10 = (bf16[512,256]{1,0:T(8,128)(2,1)}, bf16[512,256]{1,0:T(8,128)(2,1)S(1)}, u32[]{:S(2)}, u32[]{:S(2)}) collective-permute-start(bf16[512,256]{1,0:T(8,128)(2,1)} %refs_0_.1), channel_id=1, source_target_pairs={{0,1},{1,0},{2,3},{3,2},{4,5},{5,4},{6,7},{7,6},{8,9},{9,8},{10,11... | collective-permute-start | bytes 786440 | tf_op jit(solution)/shard_map/ppermute | solution.py:49
  29.5 10.4 %collective-permute-start.9 = (bf16[512,256]{1,0:T(8,128)(2,1)}, bf16[512,256]{1,0:T(8,128)(2,1)S(1)}, u32[]{:S(2)}, u32[]{:S(2)}) collective-permute-start(bf16[512,256]{1,0:T(8,128)(2,1)} %refs_0_.1), channel_id=1, source_target_pairs={{0,4},{1,5},{2,6},{3,7},{4,0},{5,1},{6,2},{7,3},{8,12},{9,13},{10,... | collective-permute-start | bytes 786440 | tf_op jit(solution)/shard_map/ppermute | solution.py:44
  35.1 8.1 %collective-permute-start.17 = (bf16[576,256]{1,0:T(8,128)(2,1)S(1)}, bf16[576,256]{1,0:T(8,128)(2,1)S(1)}, u32[]{:S(2)}, u32[]{:S(2)}) collective-permute-start(bf16[576,256]{1,0:T(8,128)(2,1)S(1)} %collective-permute-done.6.refs_13_), channel_id=1, source_target_pairs={{0,24},{8,0},{16,8},{24,16},{32,56},{40,32},{48,40},{56,48},{64,88... | collective-permute-start | bytes 884744 | tf_op jit(solution)/shard_map/ppermute | solution.py:39
  36.8 7.8 %collective-permute-start.16 = (bf16[576,256]{1,0:T(8,128)(2,1)S(1)}, bf16[576,256]{1,0:T(8,128)(2,1)S(1)}, u32[]{:S(2)}, u32[]{:S(2)}) collective-permute-start(bf16[576,256]{1,0:T(8,128)(2,1)S(1)} %collective-permute-done.3.refs_10_), channel_id=1, source_target_pairs={{0,8},{8,16},{16,24},{24,0},{32,40},{40,48},{48,56},{56,32},{64,72... | collective-permute-start | bytes 884744 | tf_op jit(solution)/shard_map/ppermute | solution.py:39
  40.0 1.7 %collective-permute-start.13 = (bf16[512,256]{1,0:T(8,128)(2,1)S(1)}, bf16[512,256]{1,0:T(8,128)(2,1)}, u32[]{:S(2)}, u32[]{:S(2)}) collective-permute-start(bf16[512,256]{1,0:T(8,128)(2,1)S(1)} %collective-permute-done.9.refs_3_), channel_id=1, source_target_pairs={{0,1},{1,0},{2,3},{3,2},{4,5},{5,4},{6,7},{7,6},{8,9},{9,8},{10,11... | collective-permute-start | bytes 786440 | tf_op jit(solution)/shard_map/ppermute | solution.py:49
  40.0 3.2 %collective-permute-start.11 = (bf16[512,256]{1,0:T(8,128)(2,1)S(1)}, bf16[512,256]{1,0:T(8,128)(2,1)}, u32[]{:S(2)}, u32[]{:S(2)}) collective-permute-start(bf16[512,256]{1,0:T(8,128)(2,1)S(1)} %collective-permute-done.7.refs_1_), channel_id=1, source_target_pairs={{0,1},{1,0},{2,3},{3,2},{4,5},{5,4},{6,7},{7,6},{8,9},{9,8},{10,11... | collective-permute-start | bytes 786440 | tf_op jit(solution)/shard_map/ppermute | solution.py:49
  40.5 2.7 %collective-permute-start.12 = (bf16[512,256]{1,0:T(8,128)(2,1)S(1)}, bf16[512,256]{1,0:T(8,128)(2,1)}, u32[]{:S(2)}, u32[]{:S(2)}) collective-permute-start(bf16[512,256]{1,0:T(8,128)(2,1)S(1)} %collective-permute-done.8.refs_2_), channel_id=1, source_target_pairs={{0,1},{1,0},{2,3},{3,2},{4,5},{5,4},{6,7},{7,6},{8,9},{9,8},{10,11... | collective-permute-start | bytes 786440 | tf_op jit(solution)/shard_map/ppermute | solution.py:49
